TPU v7x, 512 devices: a whole 4x8x8 slice. The times are simulated.
512 devices in a mesh: gx: 32 (over y, x), gy: 16 (over z, core).
Axes of the slice: x: 4, y: 8, z: 8, core: 2. Of those that a mesh axis runs over, the one named last changes fastest.
Arguments:
- slip_field: float32 [4096, 3, 128], P(('gy', 'gx')), may hold values from -6 to 6
- positions: float32 [4096, 3, 128], P(('gy', 'gx')), may hold values from -6 to 6
- neighbours: int32 [4096, 8], P(('gy', 'gx')), may hold values from 0 to 255, as said below
- near_counts: int32 [4096], P(('gy', 'gx')), may hold values from 1 to 8, as said below
- cluster_basis: float32 [4096, 16, 3, 128], P(('gy', 'gx')), may hold values from -0.4375 to 0.4375
- transfer: float32 [1022, 16, 16], replicated, may hold values from -1 to 1
- coupling: float32 [1022, 16, 16], replicated, may hold values from -1.5 to 1.5
- prestress: float32 [4096, 3, 128], P(('gy', 'gx')), may hold values from -6 to 6
- normal_stress: float32 [4096, 128], P(('gy', 'gx')), may hold values from 1 to 3
- friction: float32 [4096, 128], P(('gy', 'gx')), may hold values from 0.3 to 0.9
- compliance: float32 [4096, 128], P(('gy', 'gx')), may hold values from 0.1 to 1
- slip_state: int32 [4096, 128], P(('gy', 'gx')), may hold values 0 or 1
- cell_index: int32 [4096, 4, 128], P(('gy', 'gx')), may hold values from 0 to 32767, as said below
- cell_weight: float32 [4096, 4, 128], P(('gy', 'gx')), may hold values from 0.1 to 0.5
- dilation: float32 [4096, 128], P(('gy', 'gx')), may hold values from 1 to 10
- pressure: float32 [256, 2048], P('gx', 'gy'), may hold values from -4 to 4
- mobility: float32 [256, 2048], P('gx', 'gy'), may hold values from 0.05 to 0.24
Outputs:
- final_slip: float32 [4096, 3, 128], P(('gy', 'gx'))
- final_pressure: float32 [256, 2048], P('gx', 'gy')
Inputs may be any that keep to these rules, and one draw needn't show every extreme that they name: `neighbours`: entry 0 of a row is the cluster's own number within its subtree; the entries of a row are distinct and lie within 8 clusters of the cluster's own number, counted cyclically within its subtree of 256 clusters. Only the first near_counts[c] entries of a row of neighbours are used; some cluster has exactly 8. `slip_state`: 1 marks an element that slips. `cell_index`: the four cells of an element are band rows r and r + 1 (counted cyclically over the 256 rows) at columns b and b + 1 of the band, in that order: (r, b), (r + 1, b), (r, b + 1), (r + 1, b + 1). For an element of cluster c with j = (c % 256) // 8, both rows lie in (j - 1) * 8 to (j + 2) * 8 - 1, cyclically; both ends are reached in every draw.
All inputs are finite; a program needn't handle non-finite values. No bound on the sum of `slip_state` on one device may be relied on, other than what follows from the above.
Results may differ from a plain program's by a relative error of at most 0.00027.
Values sent between devices are 32-bit elements; how exact they have to be, the bound alone decides.
No kernel may reach another device: no remote copies, remote signals or barrier semaphores. Data moves between devices by JAX's collectives and lax.ppermute only.
A program may use at most 64 MiB of HBM per device.

v0:
```python
import jax
import jax.numpy as jnp
from jax import lax
from jax.sharding import PartitionSpec as P

ITERS = 2
FLOW_STEPS = 2


HIGHEST = lax.Precision.HIGHEST
KERNEL_SCALE = 0.04
SOFTENING = 0.25
PAIR_GROUP = 4


def in_order(blocks, dim):
    dims = list(blocks.shape[1:])
    dims[dim] *= blocks.shape[0]
    return jnp.moveaxis(blocks, 0, dim).reshape(dims)


def copy_for_each(x, axis):
    peers = lax.axis_size(axis)
    return lax.all_to_all(jnp.broadcast_to(x[None], (peers, *x.shape)), axis, 0, 0, tiled=True)


def gathered_copies(x, axis, dim):
    return in_order(copy_for_each(x, axis), dim)


def partner_2(x, axis, apart):
    return lax.ppermute(x, axis, [(i, i ^ 1 << apart) for i in range(lax.axis_size(axis))])


def in_one_piece(arrays, axis, dim, along):
    columns = [a.reshape(*a.shape[:along], -1) for a in arrays]
    both = jnp.concatenate(columns, axis=along)
    filled, at, gathered = (lax.all_gather(both, axis, axis=dim, tiled=True), 0, [])
    for a, column in zip(arrays, columns):
        slab = filled[..., at : at + column.shape[along]]
        gathered.append(slab.reshape(*slab.shape[:along], *a.shape[along:]))
        at += column.shape[along]
    return tuple(gathered)


def with_halo(block, sides, width):
    for axis, dim in sides:
        count = lax.axis_size(axis)
        forward = [(i, i + 1) for i in range(count - 1)]
        forward.append((count - 1, 0))
        backward = [(target, source) for source, target in forward]
        low = lax.ppermute(
            lax.slice_in_dim(block, block.shape[dim] - width, None, axis=dim), axis, forward
        )
        high = lax.ppermute(lax.slice_in_dim(block, 0, width, axis=dim), axis, backward)
        block = jnp.concatenate([low, block, high], axis=dim)
    return block


def cut_along(x, dim, peers):
    before, after = (x.shape[:dim], x.shape[dim + 1 :])
    return jnp.moveaxis(x.reshape(*before, peers, -1, *after), dim, 0)


def summed_on_arrival(x, axis, dim):
    peers = lax.axis_size(axis)
    blocks = lax.all_to_all(cut_along(x, dim, peers), axis, 0, 0, tiled=True)
    return jnp.sum(blocks, axis=0)


def from_behind(value, axis, steps):
    count = lax.axis_size(axis)
    pairs = [(source, (source + steps) % count) for source in range(count)]
    return lax.ppermute(value, axis, pairs)


def with_halo_2(x, sides, width):
    edges = {}
    for axis, dim in sides:
        peers, length = (lax.axis_size(axis), x.shape[dim])
        up = [(i, (i + 1) % peers) for i in range(peers - 1)]
        last = lax.slice_in_dim(x, length - width, length, axis=dim)
        first = lax.slice_in_dim(x, 0, width, axis=dim)
        edges[dim] = (
            lax.ppermute(last, axis, up),
            lax.ppermute(first, axis, [(b, a) for a, b in up]),
        )
    done = []
    for _, dim in sides:
        low, high = edges[dim]
        around = [(width, width) if d in done else (0, 0) for d in range(x.ndim)]
        x = jnp.concatenate([jnp.pad(low, around), x, jnp.pad(high, around)], axis=dim)
        done.append(dim)
    return x


def pair_blocks(targets, sources, slipped):
    offsets = targets[:, :, :, None] - sources[:, :, None, :]
    radius = jnp.sum(offsets * offsets, axis=1) + SOFTENING
    inverse = lax.rsqrt(radius)
    inverse_cube = inverse * inverse * inverse
    projected = jnp.sum(offsets * slipped[:, :, None, :], axis=1)
    direct = jnp.sum(inverse[:, None] * slipped[:, :, None, :], axis=3)
    dyadic = jnp.sum(offsets * (projected * inverse_cube)[:, None], axis=3)
    return KERNEL_SCALE * (direct + dyadic)


def near_sweep(pair_total, first_rank, locate, target_table, source_table, slip_table, out_rows):
    group_turns = (pair_total + PAIR_GROUP - 1) // PAIR_GROUP
    group_offsets = jnp.arange(PAIR_GROUP, dtype=jnp.int32)

    def one_group(turn_index, result):
        ranking = first_rank + turn_index * PAIR_GROUP + group_offsets
        active = ranking < first_rank + pair_total
        target_idx, source_idx = locate(jnp.where(active, ranking, first_rank))
        blocks = pair_blocks(
            target_table[target_idx], source_table[source_idx], slip_table[source_idx]
        )
        blocks = jnp.where(active[:, None, None], blocks, 0.0)
        return result.at[target_idx].add(blocks)

    result = jnp.zeros((out_rows,) + slip_table.shape[1:], jnp.float32)
    return lax.fori_loop(0, group_turns, one_group, result)


def node_matrix(table, node_index):
    return lax.dynamic_index_in_dim(table, node_index, keepdims=False)


def climb_tree(moments, tier_start, first_node, my_node, transfer, devices, siblings):
    for tier_level in range(tier_start, tier_start + moments.shape[0].bit_length() - 1):
        node_count = moments.shape[0]
        node_base = 2 * devices - 2 * (devices >> tier_level)
        matrices = lax.dynamic_slice_in_dim(transfer, node_base + first_node, node_count)
        lifted = jnp.einsum("nmk,nm->nk", matrices, moments, precision=HIGHEST)
        siblings.append(
            lax.dynamic_index_in_dim(
                moments, jnp.bitwise_xor(my_node, 1) - first_node, keepdims=False
            )
        )
        moments = lifted[0::2] + lifted[1::2]
        first_node = first_node // 2
        my_node = my_node // 2
    return moments[0]


def far_field(slip_field, cluster_basis, transfer, coupling, flat_index, bits_x, bits_y, lanes_x):
    devices = 1 << bits_x + bits_y
    moment = jnp.einsum("ckia,cia->k", cluster_basis, slip_field, precision=HIGHEST)
    siblings = []
    row_moment = gathered_copies(moment[None, :], "gx", 0)
    upper_moment = climb_tree(
        row_moment, 0, flat_index - flat_index % lanes_x, flat_index, transfer, devices, siblings
    )
    for bit_level in range(bits_y):
        partner = partner_2(upper_moment, "gy", bit_level)
        siblings.append(partner)
        lift_tier_level = bits_x + bit_level
        node_base = 2 * devices - 2 * (devices >> lift_tier_level)
        node_now = flat_index >> lift_tier_level
        own_lift = jnp.dot(
            upper_moment, node_matrix(transfer, node_base + node_now), precision=HIGHEST
        )
        partner_lift = jnp.dot(
            partner,
            node_matrix(transfer, node_base + jnp.bitwise_xor(node_now, 1)),
            precision=HIGHEST,
        )
        upper_moment = own_lift + partner_lift
    incoming = jnp.zeros((transfer.shape[1],), jnp.float32)
    for tier_level in reversed(range(bits_x + bits_y)):
        node_index = 2 * devices - 2 * (devices >> tier_level) + (flat_index >> tier_level)
        downward = jnp.dot(node_matrix(transfer, node_index), incoming, precision=HIGHEST)
        across = jnp.dot(node_matrix(coupling, node_index), siblings[tier_level], precision=HIGHEST)
        incoming = downward + across
    return jnp.einsum("ckia,k->cia", cluster_basis, incoming, precision=HIGHEST)


def shards(
    slip_field,
    positions,
    neighbours,
    near_counts,
    cluster_basis,
    transfer,
    coupling,
    prestress,
    normal_stress,
    friction,
    compliance,
    slip_state,
    cell_index,
    cell_weight,
    dilation,
    pressure,
    mobility,
):
    lanes_x = lax.axis_size("gx")
    lanes_y = lax.axis_size("gy")
    bits_x = lanes_x.bit_length() - 1
    bits_y = lanes_y.bit_length() - 1
    column_x = lax.axis_index("gx")
    flat_index = lax.axis_index("gy") * lanes_x + column_x
    own_rows = slip_field.shape[0]
    subtree_size = own_rows * lanes_x
    slot_count = neighbours.shape[1]
    state_mask = slip_state.astype(jnp.float32)
    flow_rows = pressure.shape[0]
    flow_cols = pressure.shape[1]
    band_rows = flow_rows * lanes_x
    cell_rows = cell_index // flow_cols
    cell_cols = cell_index % flow_cols
    rim_rows = (cell_rows - column_x * flow_rows + flow_rows) % band_rows
    rim_cells = rim_rows * flow_cols + cell_cols
    all_positions = gathered_copies(positions, "gx", 0)
    all_lists, all_counts = in_one_piece((neighbours, near_counts), "gx", 0, 1)
    list_ends = jnp.cumsum(all_counts)
    list_begins = list_ends - all_counts
    whole_total = list_ends[-1]
    pair_share = (whole_total + lanes_x - 1) // lanes_x
    share_number = (column_x + lanes_x // 2) % lanes_x
    first_rank = share_number * pair_share
    pair_count = jnp.clip(whole_total - first_rank, 0, pair_share)

    def locate_pairs(ranking):
        target_idx = jnp.minimum(
            jnp.searchsorted(list_ends, ranking, side="right"), subtree_size - 1
        )
        column = jnp.clip(ranking - list_begins[target_idx], 0, slot_count - 1)
        return (target_idx, all_lists[target_idx, column])

    for outer_step in range(ITERS):
        read_table = with_halo(pressure, (("gx", 0),), flow_rows)
        all_slip = gathered_copies(slip_field, "gx", 0)
        partial_near = near_sweep(
            pair_count,
            first_rank,
            locate_pairs,
            all_positions,
            all_positions,
            all_slip,
            subtree_size,
        )
        near_part = summed_on_arrival(partial_near, "gx", 0)
        far_part = far_field(
            slip_field, cluster_basis, transfer, coupling, flat_index, bits_x, bits_y, lanes_x
        )
        at_elements = jnp.sum(cell_weight * read_table.reshape(-1)[rim_cells], axis=1)
        stress = prestress - (near_part + far_part)
        effective = normal_stress - at_elements
        magnitude = jnp.sqrt(jnp.sum(stress * stress, axis=1) + 1.0)
        factor = jnp.maximum(1.0 - friction * effective / magnitude, 0.0)
        step_slip = (state_mask * compliance * factor)[:, None, :] * stress
        slip_field = slip_field + step_slip
        dilated = dilation * jnp.sum(step_slip * step_slip, axis=1)
        loaded = jax.ops.segment_sum(
            (cell_weight * dilated[:, None, :]).reshape(-1),
            rim_cells.reshape(-1),
            num_segments=read_table.size,
        ).reshape(read_table.shape)
        from_below = from_behind(loaded[2 * flow_rows :], "gx", 1)
        from_above = from_behind(loaded[:flow_rows], "gx", -1)
        source = loaded[flow_rows : 2 * flow_rows] + from_below + from_above
        pressure = pressure + source
        for flow_step in range(FLOW_STEPS):
            padded = with_halo_2(pressure, (("gx", 0), ("gy", 1)), 1)
            beside_all = padded[2:, 1:-1] + padded[:-2, 1:-1] + padded[1:-1, 2:] + padded[1:-1, :-2]
            pressure = pressure + mobility * (beside_all - 4.0 * pressure)
    return (slip_field, pressure)


def solution(mesh):
    in_specs = (
        P(("gy", "gx"), None, None),
        P(("gy", "gx"), None, None),
        P(("gy", "gx"), None),
        P(("gy", "gx")),
        P(("gy", "gx"), None, None, None),
        P(),
        P(),
        P(("gy", "gx"), None, None),
        P(("gy", "gx"), None),
        P(("gy", "gx"), None),
        P(("gy", "gx"), None),
        P(("gy", "gx"), None),
        P(("gy", "gx"), None, None),
        P(("gy", "gx"), None, None),
        P(("gy", "gx"), None),
        P("gx", "gy"),
        P("gx", "gy"),
    )
    out_specs = (P(("gy", "gx"), None, None), P("gx", "gy"))
    return jax.shard_map(shards, mesh=mesh, in_specs=in_specs, out_specs=out_specs, check_vma=False)
```

profile of v0, /device:TPU:95, one launch (start us, length us, event | category | flops | bytes accessed | tf_op | source)
XLA Modules:
  0.0 549.5 jit_solution(16967458097611822873)
XLA Ops:
  3.2 6.1 %collective-permute-start = (f32[8,128]{1,0:T(8,128)}, f32[8,128]{1,0:T(8,128)}, u32[]{:S(2)}, u32[]{:S(2)}) collective-permute-start(f32[8,128]{1,0:T(8,128)} %param.40), channel_id=1, source_target_pairs={{0,16},{16,32},{32,48},{48,64},{64,80},{80,96},{96,112},{112,128},... | collective-permute-start | bytes 12296 | tf_op jit(solution)/shard_map/ppermute | solution.py:52
  11.1 7.9 %all-to-all-start.3 = ((f32[32,1,16]{2,1,0:T(1,128)}), f32[32,1,16]{2,1,0:T(1,128)}, u32[]{:S(2)}, u32[]{:S(2)}) async-start(f32[32,1,16]{2,1,0:T(1,128)} %broadcast_in_dim.139), calls=%async_computation.3 | async-start | bytes 32768 | tf_op jit(solution)/shard_map/all_to_all | solution.py:24
  20.0 29.7 %all_gather.3 = s32[256,9]{1,0:T(8,128)S(1)} all-gather(s32[8,9]{1,0:T(8,128)S(1)} %pad_add_fusion), channel_id=1, replica_groups=mesh['gx'=32,'gy'=16] {'gx'}, dimensions={0}, use_global_device_ids=true | all-gather | bytes 9504 | tf_op jit(solution)/shard_map/all_gather | solution.py:38
  72.2 7.6 %all-to-all-start = ((f32[32,8,3,128]{3,1,2,0:T(8,128)}), f32[32,8,3,128]{3,1,2,0:T(8,128)S(1)}, u32[]{:S(2)}, u32[]{:S(2)}) async-start(f32[32,8,3,128]{3,1,2,0:T(8,128)} %broadcast_in_dim.137), calls=%async_computation | async-start | bytes 786432 | tf_op jit(solution)/shard_map/all_to_all | solution.py:24
  82.2 12.6 %collective-permute-start.2 = (f32[16]{0:T(128)S(1)}, f32[16]{0:T(128)S(1)}, u32[]{:S(2)}, u32[]{:S(2)}) collective-permute-start(f32[16]{0:T(128)S(1)} %fusion.215), channel_id=1, source_target_pairs={{0,1},{1,0},{2,3},{3,2},{4,5},{5,4},{6,7},{7,6},{8,9},{9,8},{10,11... | collective-permute-start | bytes 200 | tf_op jit(solution)/shard_map/ppermute | solution.py:32
  98.6 23.0 %gather_fusion.12 = f32[4096]{0:T(1024)S(1)} fusion(f32[3072]{0:T(1024)S(1)} %maximum_bitcast_fusion, s32[4096]{0:T(1024)S(1)} %broadcast_clamp_fusion), kind=kCustom, calls=%fused_computation.12 | custom fusion | bytes 49152 | tf_op jit(solution)/shard_map/gather | solution.py:248
  128.5 8.5 %collective-permute-start.5 = (f32[16]{0:T(128)S(1)}, f32[16]{0:T(128)S(1)}, u32[]{:S(2)}, u32[]{:S(2)}) collective-permute-start(f32[16]{0:T(128)S(1)} %fusion.69), channel_id=1, source_target_pairs={{0,8},{1,9},{2,10},{3,11},{4,12},{5,13},{6,14},{7,15},{8,0},{9,1},... | collective-permute-start | bytes 200 | tf_op jit(solution)/shard_map/ppermute | solution.py:32
  139.7 9.2 %all-to-all-start.1 = ((f32[32,8,3,128]{3,1,2,0:T(8,128)}), f32[32,8,3,128]{3,1,2,0:T(8,128)S(1)}, u32[]{:S(2)}, u32[]{:S(2)}) async-start(f32[32,8,3,128]{3,1,2,0:T(8,128)} %broadcast_in_dim.138), calls=%async_computation.1 | async-start | bytes 786432 | tf_op jit(solution)/shard_map/all_to_all | solution.py:24
  150.2 7.6 %all-to-all-done.1 = f32[32,8,3,128]{3,1,2,0:T(8,128)S(1)} async-done(((f32[32,8,3,128]{3,1,2,0:T(8,128)}), f32[32,8,3,128]{3,1,2,0:T(8,128)S(1)}, u32[]{:S(2)}, u32[]{:S(2)}) %all-to-all-start.1) | async-done | bytes 393248 | tf_op jit(solution)/shard_map/all_to_all | solution.py:24
  159.0 75.5 %all-to-all-start.2 = ((f32[32,8,3,128]{3,1,2,0:T(8,128)}), f32[32,8,3,128]{3,1,2,0:T(8,128)S(1)}, u32[]{:S(2)}, u32[]{:S(2)}) async-start(f32[32,8,3,128]{3,1,2,0:T(8,128)} %copy.128), calls=%async_computation.2 | async-start | bytes 786432 | tf_op jit(solution)/shard_map/all_to_all | solution.py:67
  236.1 6.6 %all-to-all-done.2 = f32[32,8,3,128]{3,1,2,0:T(8,128)S(1)} async-done(((f32[32,8,3,128]{3,1,2,0:T(8,128)}), f32[32,8,3,128]{3,1,2,0:T(8,128)S(1)}, u32[]{:S(2)}, u32[]{:S(2)}) %all-to-all-start.2) | async-done | bytes 393248 | tf_op jit(solution)/shard_map/all_to_all | solution.py:67
  243.8 8.0 %all-to-all-start.6 = ((f32[32,1,16]{2,1,0:T(1,128)}), f32[32,1,16]{2,1,0:T(1,128)S(1)}, u32[]{:S(2)}, u32[]{:S(2)}) async-start(f32[32,1,16]{2,1,0:T(1,128)} %broadcast_in_dim.141), calls=%async_computation.6 | async-start | bytes 32768 | tf_op jit(solution)/shard_map/all_to_all | solution.py:24
  251.9 22.0 %scatter_custom_fusion.2 = f32[3072]{0:T(1024)S(1)} fusion(s32[4096]{0:T(1024)} %bitcast.702, f32[4096]{0:T(1024)S(1)} %bitcast.709, f32[]{:T(128)} %constant.512.clone.1), kind=kCustom, calls=%fused_computation.305 | custom fusion | flops 4096 | bytes 12800 | tf_op jit(solution)/shard_map/scatter-add | solution.py:256
  283.4 7.7 %all-to-all-start.4 = ((f32[32,8,3,128]{3,1,2,0:T(8,128)}), f32[32,8,3,128]{3,1,2,0:T(8,128)S(1)}, u32[]{:S(2)}, u32[]{:S(2)}) async-start(f32[32,8,3,128]{3,1,2,0:T(8,128)} %broadcast_in_dim.140), calls=%async_computation.4 | async-start | bytes 786432 | tf_op jit(solution)/shard_map/all_to_all | solution.py:24
  292.7 7.7 %collective-permute-start.18 = (f32[16]{0:T(128)S(1)}, f32[16]{0:T(128)S(1)}, u32[]{:S(2)}, u32[]{:S(2)}) collective-permute-start(f32[16]{0:T(128)S(1)} %fusion.216), channel_id=1, source_target_pairs={{0,1},{1,0},{2,3},{3,2},{4,5},{5,4},{6,7},{7,6},{8,9},{9,8},{10,11... | collective-permute-start | bytes 200 | tf_op jit(solution)/shard_map/ppermute | solution.py:32
  317.1 15.9 %collective-permute-start.20 = (f32[16]{0:T(128)S(1)}, f32[16]{0:T(128)S(1)}, u32[]{:S(2)}, u32[]{:S(2)}) collective-permute-start(f32[16]{0:T(128)S(1)} %fusion.49), channel_id=1, source_target_pairs={{0,4},{1,5},{2,6},{3,7},{4,0},{5,1},{6,2},{7,3},{8,12},{9,13},{10,... | collective-permute-start | bytes 200 | tf_op jit(solution)/shard_map/ppermute | solution.py:32
  348.4 6.7 %collective-permute-start.13 = (f32[1,128]{1,0:T(1,128)S(1)}, f32[1,128]{1,0:T(1,128)S(1)}, u32[]{:S(2)}, u32[]{:S(2)}) collective-permute-start(f32[1,128]{1,0:T(1,128)S(1)} %get-tuple-element.713), channel_id=1, source_target_pairs={{0,16},{16,32},{32,48},{48,64},{64,80},{80,96},{96,112},{112,128},... | collective-permute-start | bytes 1544 | tf_op jit(solution)/shard_map/ppermute | solution.py:85
  356.3 73.6 %all-to-all-start.5 = ((f32[32,8,3,128]{3,1,2,0:T(8,128)}), f32[32,8,3,128]{3,1,2,0:T(8,128)S(1)}, u32[]{:S(2)}, u32[]{:S(2)}) async-start(f32[32,8,3,128]{3,1,2,0:T(8,128)} %copy.159), calls=%async_computation.5 | async-start | bytes 786432 | tf_op jit(solution)/shard_map/all_to_all | solution.py:67
  446.5 23.0 %gather_fusion.13 = f32[4096]{0:T(1024)S(1)} fusion(f32[3072]{0:T(1024)S(1)} %maximum_bitcast_fusion.1, s32[4096]{0:T(1024)S(1)} %broadcast_clamp_fusion), kind=kCustom, calls=%fused_computation.13 | custom fusion | bytes 49152 | tf_op jit(solution)/shard_map/gather | solution.py:248
  469.8 22.0 %scatter_custom_fusion.3 = f32[3072]{0:T(1024)S(1)} fusion(s32[4096]{0:T(1024)} %bitcast.703, f32[4096]{0:T(1024)S(1)} %bitcast.708, f32[]{:T(128)} %constant.512.clone.1), kind=kCustom, calls=%fused_computation.303 | custom fusion | flops 4096 | bytes 12800 | tf_op jit(solution)/shard_map/scatter-add | solution.py:256
  493.7 6.9 %collective-permute-start.22 = (f32[8,128]{1,0:T(8,128)S(1)}, f32[8,128]{1,0:T(8,128)S(1)}, u32[]{:S(2)}, u32[]{:S(2)}) collective-permute-start(f32[8,128]{1,0:T(8,128)S(1)} %get-tuple-element.699), channel_id=1, source_target_pairs={{0,16},{16,32},{32,48},{48,64},{64,80},{80,96},{96,112},{112,128},... | collective-permute-start | bytes 12296 | tf_op jit(solution)/shard_map/ppermute | solution.py:74
  503.3 6.9 %collective-permute-start.25 = (f32[1,128]{1,0:T(1,128)S(1)}, f32[1,128]{1,0:T(1,128)S(1)}, u32[]{:S(2)}, u32[]{:S(2)}) collective-permute-start(f32[1,128]{1,0:T(1,128)S(1)} %get-tuple-element.709), channel_id=1, source_target_pairs={{0,16},{16,32},{32,48},{48,64},{64,80},{80,96},{96,112},{112,128},... | collective-permute-start | bytes 1544 | tf_op jit(solution)/shard_map/ppermute | solution.py:85
  521.8 6.7 %collective-permute-start.29 = (f32[1,128]{1,0:T(1,128)S(1)}, f32[1,128]{1,0:T(1,128)S(1)}, u32[]{:S(2)}, u32[]{:S(2)}) collective-permute-start(f32[1,128]{1,0:T(1,128)S(1)} %get-tuple-element.705), channel_id=1, source_target_pairs={{0,16},{16,32},{32,48},{48,64},{64,80},{80,96},{96,112},{112,128},... | collective-permute-start | bytes 1544 | tf_op jit(solution)/shard_map/ppermute | solution.py:85
  528.6 15.2 %collective-permute-start.31 = (f32[8,1]{1,0:T(8,128)S(1)}, f32[8,1]{1,0:T(8,128)S(1)}, u32[]{:S(2)}, u32[]{:S(2)}) collective-permute-start(f32[8,1]{1,0:T(8,128)S(1)} %get-tuple-element.704), channel_id=1, source_target_pairs={{0,1},{1,2},{2,3},{3,4},{4,5},{5,6},{6,7},{7,8},{8,9},{9,10},{10,1... | collective-permute-start | bytes 104 | tf_op jit(solution)/shard_map/ppermute | solution.py:85
  (297 shorter events, 129.4 us)
Async XLA Ops:
  0.6 97.2 %collective-permute-start.1 = (f32[8,128]{1,0:T(8,128)}, f32[8,128]{1,0:T(8,128)}, u32[]{:S(2)}, u32[]{:S(2)}) collective-permute-start(f32[8,128]{1,0:T(8,128)} %param.40), channel_id=1, source_target_pairs={{16,0},{32,16},{48,32},{64,48},{80,64},{96,80},{112,96},{128,112},... | collective-permute-start | bytes 12296 | tf_op jit(solution)/shard_map/ppermute | solution.py:55
  3.2 94.6 %collective-permute-start = (f32[8,128]{1,0:T(8,128)}, f32[8,128]{1,0:T(8,128)}, u32[]{:S(2)}, u32[]{:S(2)}) collective-permute-start(f32[8,128]{1,0:T(8,128)} %param.40), channel_id=1, source_target_pairs={{0,16},{16,32},{32,48},{48,64},{64,80},{80,96},{96,112},{112,128},... | collective-permute-start | bytes 12296 | tf_op jit(solution)/shard_map/ppermute | solution.py:52
  11.1 59.6 %all-to-all-start.3 = ((f32[32,1,16]{2,1,0:T(1,128)}), f32[32,1,16]{2,1,0:T(1,128)}, u32[]{:S(2)}, u32[]{:S(2)}) async-start(f32[32,1,16]{2,1,0:T(1,128)} %broadcast_in_dim.139), calls=%async_computation.3 | async-start | bytes 32768 | tf_op jit(solution)/shard_map/all_to_all | solution.py:24
  72.2 66.4 %all-to-all-start = ((f32[32,8,3,128]{3,1,2,0:T(8,128)}), f32[32,8,3,128]{3,1,2,0:T(8,128)S(1)}, u32[]{:S(2)}, u32[]{:S(2)}) async-start(f32[32,8,3,128]{3,1,2,0:T(8,128)} %broadcast_in_dim.137), calls=%async_computation | async-start | bytes 786432 | tf_op jit(solution)/shard_map/all_to_all | solution.py:24
  95.7 26.0 %collective-permute-start.3 = (f32[16]{0:T(128)S(1)}, f32[16]{0:T(128)S(1)}, u32[]{:S(2)}, u32[]{:S(2)}) collective-permute-start(f32[16]{0:T(128)S(1)} %fusion.71), channel_id=1, source_target_pairs={{0,2},{1,3},{2,0},{3,1},{4,6},{5,7},{6,4},{7,5},{8,10},{9,11},{10,... | collective-permute-start | bytes 200 | tf_op jit(solution)/shard_map/ppermute | solution.py:32
  139.7 18.1 %all-to-all-start.1 = ((f32[32,8,3,128]{3,1,2,0:T(8,128)}), f32[32,8,3,128]{3,1,2,0:T(8,128)S(1)}, u32[]{:S(2)}, u32[]{:S(2)}) async-start(f32[32,8,3,128]{3,1,2,0:T(8,128)} %broadcast_in_dim.138), calls=%async_computation.1 | async-start | bytes 786432 | tf_op jit(solution)/shard_map/all_to_all | solution.py:24
  159.0 83.7 %all-to-all-start.2 = ((f32[32,8,3,128]{3,1,2,0:T(8,128)}), f32[32,8,3,128]{3,1,2,0:T(8,128)S(1)}, u32[]{:S(2)}, u32[]{:S(2)}) async-start(f32[32,8,3,128]{3,1,2,0:T(8,128)} %copy.128), calls=%async_computation.2 | async-start | bytes 786432 | tf_op jit(solution)/shard_map/all_to_all | solution.py:67
  243.8 38.8 %all-to-all-start.6 = ((f32[32,1,16]{2,1,0:T(1,128)}), f32[32,1,16]{2,1,0:T(1,128)S(1)}, u32[]{:S(2)}, u32[]{:S(2)}) async-start(f32[32,1,16]{2,1,0:T(1,128)} %broadcast_in_dim.141), calls=%async_computation.6 | async-start | bytes 32768 | tf_op jit(solution)/shard_map/all_to_all | solution.py:24
  274.0 30.7 %collective-permute-start.7 = (f32[8,128]{1,0:T(8,128)S(1)}, f32[8,128]{1,0:T(8,128)S(1)}, u32[]{:S(2)}, u32[]{:S(2)}) collective-permute-start(f32[8,128]{1,0:T(8,128)S(1)} %get-tuple-element.702), channel_id=1, source_target_pairs={{0,496},{16,0},{32,16},{48,32},{64,48},{80,64},{96,80},{112,96},{1... | collective-permute-start | bytes 12296 | tf_op jit(solution)/shard_map/ppermute | solution.py:74
  276.4 28.2 %collective-permute-start.6 = (f32[8,128]{1,0:T(8,128)S(1)}, f32[8,128]{1,0:T(8,128)S(1)}, u32[]{:S(2)}, u32[]{:S(2)}) collective-permute-start(f32[8,128]{1,0:T(8,128)S(1)} %get-tuple-element.701), channel_id=1, source_target_pairs={{0,16},{16,32},{32,48},{48,64},{64,80},{80,96},{96,112},{112,128},... | collective-permute-start | bytes 12296 | tf_op jit(solution)/shard_map/ppermute | solution.py:74
  283.4 71.7 %all-to-all-start.4 = ((f32[32,8,3,128]{3,1,2,0:T(8,128)}), f32[32,8,3,128]{3,1,2,0:T(8,128)S(1)}, u32[]{:S(2)}, u32[]{:S(2)}) async-start(f32[32,8,3,128]{3,1,2,0:T(8,128)} %broadcast_in_dim.140), calls=%async_computation.4 | async-start | bytes 786432 | tf_op jit(solution)/shard_map/all_to_all | solution.py:24
  301.5 15.4 %collective-permute-start.19 = (f32[16]{0:T(128)S(1)}, f32[16]{0:T(128)S(1)}, u32[]{:S(2)}, u32[]{:S(2)}) collective-permute-start(f32[16]{0:T(128)S(1)} %fusion.50), channel_id=1, source_target_pairs={{0,2},{1,3},{2,0},{3,1},{4,6},{5,7},{6,4},{7,5},{8,10},{9,11},{10,... | collective-permute-start | bytes 200 | tf_op jit(solution)/shard_map/ppermute | solution.py:32
  304.8 41.1 %collective-permute-start.11 = (f32[8,1]{1,0:T(8,128)S(1)}, f32[8,1]{1,0:T(8,128)S(1)}, u32[]{:S(2)}, u32[]{:S(2)}) collective-permute-start(f32[8,1]{1,0:T(8,128)S(1)} %get-tuple-element.716), channel_id=1, source_target_pairs={{0,1},{1,2},{2,3},{3,4},{4,5},{5,6},{6,7},{7,8},{8,9},{9,10},{10,1... | collective-permute-start | bytes 104 | tf_op jit(solution)/shard_map/ppermute | solution.py:85
  308.3 37.6 %collective-permute-start.8 = (f32[1,128]{1,0:T(1,128)S(1)}, f32[1,128]{1,0:T(1,128)S(1)}, u32[]{:S(2)}, u32[]{:S(2)}) collective-permute-start(f32[1,128]{1,0:T(1,128)S(1)} %get-tuple-element.718), channel_id=1, source_target_pairs={{16,0},{32,16},{48,32},{64,48},{80,64},{96,80},{112,96},{128,112},... | collective-permute-start | bytes 1544 | tf_op jit(solution)/shard_map/ppermute | solution.py:86
  310.8 35.1 %collective-permute-start.9 = (f32[1,128]{1,0:T(1,128)S(1)}, f32[1,128]{1,0:T(1,128)S(1)}, u32[]{:S(2)}, u32[]{:S(2)}) collective-permute-start(f32[1,128]{1,0:T(1,128)S(1)} %get-tuple-element.717), channel_id=1, source_target_pairs={{0,16},{16,32},{32,48},{48,64},{64,80},{80,96},{96,112},{112,128},... | collective-permute-start | bytes 1544 | tf_op jit(solution)/shard_map/ppermute | solution.py:85
  317.1 16.8 %collective-permute-start.20 = (f32[16]{0:T(128)S(1)}, f32[16]{0:T(128)S(1)}, u32[]{:S(2)}, u32[]{:S(2)}) collective-permute-start(f32[16]{0:T(128)S(1)} %fusion.49), channel_id=1, source_target_pairs={{0,4},{1,5},{2,6},{3,7},{4,0},{5,1},{6,2},{7,3},{8,12},{9,13},{10,... | collective-permute-start | bytes 200 | tf_op jit(solution)/shard_map/ppermute | solution.py:32
  346.5 90.6 %collective-permute-start.12 = (f32[1,128]{1,0:T(1,128)S(1)}, f32[1,128]{1,0:T(1,128)S(1)}, u32[]{:S(2)}, u32[]{:S(2)}) collective-permute-start(f32[1,128]{1,0:T(1,128)S(1)} %get-tuple-element.714), channel_id=1, source_target_pairs={{16,0},{32,16},{48,32},{64,48},{80,64},{96,80},{112,96},{128,112},... | collective-permute-start | bytes 1544 | tf_op jit(solution)/shard_map/ppermute | solution.py:86
  348.4 88.7 %collective-permute-start.13 = (f32[1,128]{1,0:T(1,128)S(1)}, f32[1,128]{1,0:T(1,128)S(1)}, u32[]{:S(2)}, u32[]{:S(2)}) collective-permute-start(f32[1,128]{1,0:T(1,128)S(1)} %get-tuple-element.713), channel_id=1, source_target_pairs={{0,16},{16,32},{32,48},{48,64},{64,80},{80,96},{96,112},{112,128},... | collective-permute-start | bytes 1544 | tf_op jit(solution)/shard_map/ppermute | solution.py:85
  356.3 113.3 %all-to-all-start.5 = ((f32[32,8,3,128]{3,1,2,0:T(8,128)}), f32[32,8,3,128]{3,1,2,0:T(8,128)S(1)}, u32[]{:S(2)}, u32[]{:S(2)}) async-start(f32[32,8,3,128]{3,1,2,0:T(8,128)} %copy.159), calls=%async_computation.5 | async-start | bytes 786432 | tf_op jit(solution)/shard_map/all_to_all | solution.py:67
  501.4 18.4 %collective-permute-start.24 = (f32[1,128]{1,0:T(1,128)S(1)}, f32[1,128]{1,0:T(1,128)S(1)}, u32[]{:S(2)}, u32[]{:S(2)}) collective-permute-start(f32[1,128]{1,0:T(1,128)S(1)} %get-tuple-element.710), channel_id=1, source_target_pairs={{16,0},{32,16},{48,32},{64,48},{80,64},{96,80},{112,96},{128,112},... | collective-permute-start | bytes 1544 | tf_op jit(solution)/shard_map/ppermute | solution.py:86
  503.3 16.5 %collective-permute-start.25 = (f32[1,128]{1,0:T(1,128)S(1)}, f32[1,128]{1,0:T(1,128)S(1)}, u32[]{:S(2)}, u32[]{:S(2)}) collective-permute-start(f32[1,128]{1,0:T(1,128)S(1)} %get-tuple-element.709), channel_id=1, source_target_pairs={{0,16},{16,32},{32,48},{48,64},{64,80},{80,96},{96,112},{112,128},... | collective-permute-start | bytes 1544 | tf_op jit(solution)/shard_map/ppermute | solution.py:85
  519.9 28.9 %collective-permute-start.28 = (f32[1,128]{1,0:T(1,128)S(1)}, f32[1,128]{1,0:T(1,128)S(1)}, u32[]{:S(2)}, u32[]{:S(2)}) collective-permute-start(f32[1,128]{1,0:T(1,128)S(1)} %get-tuple-element.706), channel_id=1, source_target_pairs={{16,0},{32,16},{48,32},{64,48},{80,64},{96,80},{112,96},{128,112},... | collective-permute-start | bytes 1544 | tf_op jit(solution)/shard_map/ppermute | solution.py:86
  521.8 27.0 %collective-permute-start.29 = (f32[1,128]{1,0:T(1,128)S(1)}, f32[1,128]{1,0:T(1,128)S(1)}, u32[]{:S(2)}, u32[]{:S(2)}) collective-permute-start(f32[1,128]{1,0:T(1,128)S(1)} %get-tuple-element.705), channel_id=1, source_target_pairs={{0,16},{16,32},{32,48},{48,64},{64,80},{80,96},{96,112},{112,128},... | collective-permute-start | bytes 1544 | tf_op jit(solution)/shard_map/ppermute | solution.py:85
  528.6 17.1 %collective-permute-start.31 = (f32[8,1]{1,0:T(8,128)S(1)}, f32[8,1]{1,0:T(8,128)S(1)}, u32[]{:S(2)}, u32[]{:S(2)}) collective-permute-start(f32[8,1]{1,0:T(8,128)S(1)} %get-tuple-element.704), channel_id=1, source_target_pairs={{0,1},{1,2},{2,3},{3,4},{4,5},{5,6},{6,7},{7,8},{8,9},{9,10},{10,1... | collective-permute-start | bytes 104 | tf_op jit(solution)/shard_map/ppermute | solution.py:85
  (43 other events, 245.9 us)
where the time goes:
time: 553 us; the launch traced here: 549 us
  starting transfers between devices  357 us (65%)
  local copies, waits for them, and re-layouts  74.1 us (13%)
  other arithmetic  47.2 us (9%)
  blocking collectives  29.7 us (5%)
  waiting for transfers between devices  25.8 us (5%)
  matrix products  12.3 us (2%)
    all_to_all x2, starting transfers between devices, summed_on_arrival(): blocks = lax.all_to_all(cut_along(x, dim, peers), axis, 0, 0, tiled=True)  149 us
    ppermute x8, starting transfers between devices, partner_2(): lax.ppermute(x, axis, [(i, i ^ 1 << apart) for i in range(lax.axis_size(a...  60.5 us
    ppermute x8, starting transfers between devices, with_halo_2(): lax.ppermute(last, axis, up)  51.6 us
    gather x2, local copies, waits for them, and re-layouts, shards(): read_table.reshape(-1)[rim_cells]  46 us
    scatter-add x2, other arithmetic, shards(): jax.ops.segment_sum((cell_weight * dilated[:, None, :]).reshape(-1), rim_...  44.1 us
    all_to_all x5, starting transfers between devices, copy_for_each(): lax.all_to_all(jnp.broadcast_to(x[None], (peers, *x.shape)), axis, 0, 0,...  40.5 us
    all_gather x1, blocking collectives, in_one_piece(): lax.all_gather(both, axis, axis=dim, tiled=True)  29.7 us
    ppermute x8, starting transfers between devices, with_halo_2(): lax.ppermute(first, axis, [(b, a) for a, b in up])  20.7 us
  transfers between devices with their start and end apart: 39, of which 12 were waited for; matrix products, arithmetic and copies ran while one was open for 18% of the time, Pallas kernels for 0%

commit v1 on v0

v1 whole, which is shorter than its diff:
```python
import jax
import jax.numpy as jnp
from jax import lax
from jax.experimental import pallas as pl
from jax.experimental.pallas import tpu as pltpu
from jax.sharding import PartitionSpec as P

HI = lax.Precision.HIGHEST
F32 = jnp.float32
BF16 = jnp.bfloat16
SCALE = 0.04
SOFT = 0.25
LV = 9
RK = 16
GX_BITS = 5
WIDE = 18
NARROW = 10
HALO = 10

NN = (((1,), (0,)), ((), ()))
NT = (((1,), (1,)), ((), ()))
TN = (((0,), (0,)), ((), ()))


def dot(a, b, dims=NN, precision=HI):
    return lax.dot_general(a, b, dims, precision=precision, preferred_element_type=F32)


def iota(shape, dim):
    return lax.broadcasted_iota(jnp.int32, shape, dim)


def thirds(x):
    hi = x.astype(BF16)
    rest = x - hi.astype(F32)
    mid = rest.astype(BF16)
    low = (rest - mid.astype(F32)).astype(BF16)
    return jnp.concatenate([hi, mid, low], axis=0)


def call(kernel, outs, args, scratch=(), smem=0, flops=0):
    specs = [pl.BlockSpec(memory_space=pltpu.SMEM)] * smem
    specs += [pl.BlockSpec(memory_space=pltpu.VMEM)] * (len(args) - smem)
    return pl.pallas_call(
        kernel,
        out_shape=[jax.ShapeDtypeStruct(s, d) for s, d in outs],
        in_specs=specs,
        out_specs=[pl.BlockSpec(memory_space=pltpu.VMEM)] * len(outs),
        scratch_shapes=list(scratch),
        compiler_params=pltpu.CompilerParams(vmem_limit_bytes=32 * 1024 * 1024),
        cost_estimate=pl.CostEstimate(flops=flops, bytes_accessed=1 << 20, transcendentals=0),
    )(*args)


def project(basis_ref, slip_rows, g_ref):
    total = jnp.zeros((RK, 128), F32)
    for c in range(8):
        for i in range(3):
            total += basis_ref[c, i] * slip_rows(i, c)
    moment = dot(jnp.ones((8, 128), F32), total, NT)
    return dot(moment, g_ref[0:128, :], NT), dot(moment, g_ref[128:256, :], NT)


def setup_kernel(
    place, slip, basis, transfer, coupling, pressure, mobility, g_out, h_out, tile_out
):
    flat = place[2]
    nodes = transfer.shape[1]
    spot = iota((nodes, 256), 0)
    level = iota((nodes, 256), 1) // RK
    first = 1024 - jnp.right_shift(jnp.full(level.shape, 1024, jnp.int32), level)
    wanted = first + jnp.right_shift(jnp.full(level.shape, 0, jnp.int32) + flat, level)
    pick = jnp.where((spot == wanted) & (level < LV), 1.0, 0.0).astype(F32)
    mine = (iota((256, 256), 1) % RK) == (iota((256, 256), 0) // RK)

    def path_matrices(table):
        spread = jnp.where(mine, dot(table[...], pick), 0.0)
        return jnp.sum(spread.reshape(RK, RK, 256), axis=0)

    lifts = path_matrices(transfer)
    across = path_matrices(coupling)
    eye = jnp.where(iota((RK, RK), 0) == iota((RK, RK), 1), 1.0, 0.0).astype(F32)
    g_out[...] = jnp.zeros(g_out.shape, F32)
    h_out[...] = jnp.zeros(h_out.shape, F32)
    chain = eye
    for l in range(LV):
        g_out[l * RK : (l + 1) * RK, :] = chain
        h_out[l * RK : (l + 1) * RK, :] = dot(across[:, l * RK : (l + 1) * RK], chain)
        if l + 1 < LV:
            chain = dot(lifts[:, l * RK : (l + 1) * RK], chain)
    low, high = project(basis, lambda i, c: slip[i, c : c + 1, :], g_out)
    tile_out[...] = jnp.zeros(tile_out.shape, F32)
    tile_out[0:8, :] = pressure[...]
    tile_out[8:16, :] = mobility[...]
    tile_out[18:19, :] = low[0:1]
    tile_out[19:20, :] = high[0:1]


def cells_kernel(row_in, col_in, weight, pick_out, weight_out):
    for c in range(8):
        lanes = slice(c * 128, (c + 1) * 128)
        row = row_in[c : c + 1, :]
        col = col_in[c : c + 1, :]
        pick_out[:, lanes] = jnp.where(iota((128, 128), 0) == col, 1.0, 0.0).astype(BF16)
        at = iota((24, 128), 0)
        for side in range(2):
            weight_out[side * 24 : side * 24 + 24, lanes] = jnp.where(
                at == row, weight[2 * side, c : c + 1, :], 0.0
            ) + jnp.where(at == row + 1, weight[2 * side + 1, c : c + 1, :], 0.0)


def near_kernel(counts, slots, points, slips, near_out, target, total):
    ones = jnp.ones((128, 128), F32)
    diagonal = iota((128, 128), 0) == iota((128, 128), 1)
    for c in range(8):
        for i in range(3):
            target[i] = jnp.transpose(jnp.broadcast_to(points[1, i, c : c + 1, :], (128, 128)))
        total[...] = jnp.zeros(total.shape, F32)

        def one_source(k, _):
            slot = slots[c, k]
            block = slot // 8
            row = pl.ds(slot % 8, 1)
            y = [points[block, i, row, :] for i in range(3)]
            s = [slips[block, i, row, :] for i in range(3)]
            for part in range(8):
                rows = slice(part * 16, part * 16 + 16)
                r = [target[i, rows, :] - y[i] for i in range(3)]
                inverse = lax.rsqrt(r[0] * r[0] + r[1] * r[1] + r[2] * r[2] + SOFT)
                along = (r[0] * s[0] + r[1] * s[1] + r[2] * s[2]) * (inverse * inverse)
                for i in range(3):
                    total[i, rows, :] += inverse * (s[i] + along * r[i])
            return 0

        lax.fori_loop(0, counts[c], one_source, 0)
        for i in range(3):
            summed = dot(total[i], ones)
            near_out[i, c : c + 1, :] = SCALE * jnp.sum(
                jnp.where(diagonal, summed, 0.0), axis=0, keepdims=True
            )


def pick_edges(window):
    row, lane = iota((8, 128), 0), iota((8, 128), 1)
    wanted = jnp.where(row < 2, row, row + 124)
    pick = jnp.where((lane == wanted) & (row < 4), 1.0, 0.0).astype(F32)
    return dot(pick, window, NT)


def spread_edges(edges, width):
    row, lane = iota((8, 128), 0), iota((8, 128), 1)
    wanted = jnp.where(row < 2, row, row + 124)
    pick = jnp.where((lane == wanted) & (row < 4), 1.0, 0.0).astype(F32)
    return dot(edges[:, 0:32], pick, TN)


def sum_over_row(place, received):
    j = place[0]
    row, lane = iota((8, 128), 0), iota((8, 128), 1)
    level = lane // RK + jnp.where(row == 3, 8, 0)
    own = jnp.right_shift(jnp.zeros((8, 128), jnp.int32) + j, level)
    total = jnp.zeros((8, 128), F32)
    for p in range(received.shape[0]):
        theirs = jnp.right_shift(jnp.full((8, 128), p, jnp.int32), level)
        used = (level >= GX_BITS) | (theirs == jnp.bitwise_xor(own, 1))
        total += jnp.where(used, received[p, 16:24, :], 0.0)
    return total


def first_kernel(place, received, pressure_out, mobility_out, tile_out):
    j = place[0]
    peers = received.shape[0]
    pressure_out[...] = jnp.zeros(pressure_out.shape, F32)
    mobility_out[...] = jnp.zeros(mobility_out.shape, F32)
    for out, at in ((pressure_out, 0), (mobility_out, 8)):
        for off in (-1, 0, 1):
            p = lax.rem(j + off + peers, peers)
            out[HALO + 8 * off : HALO + 8 * off + 8, :] = received[p, at : at + 8, :]
        p = lax.rem(j - 2 + peers, peers)
        out[0:2, :] = received[p, at + 6 : at + 8, :]
        p = lax.rem(j + 2, peers)
        out[26:28, :] = received[p, at : at + 2, :]
    sums = sum_over_row(place, received)
    tile_out[...] = jnp.zeros(tile_out.shape, F32)
    edges = pick_edges(mobility_out[...])
    tile_out[4:5, :] = sums[2:3]
    tile_out[5:6, :] = sums[3:4]
    tile_out[0:4, 0:32] = edges[0:4]


def add_sources(place, received, loaded, window, rows):
    j = place[0]
    peers = received.shape[0]
    window[2:26, :] += loaded[...]
    for off in range(1, 4):
        kept = rows - 8 * (off - 1)
        if kept <= 0:
            continue
        p = lax.rem(j + off, peers)
        at = HALO + 8 * (off - 1)
        window[at : at + kept, :] += received[p, 0:kept, :]
        p = lax.rem(j - off + peers, peers)
        at = HALO + 8 - rows
        window[at : at + kept, :] += received[p, rows - kept : rows, :]


def between_kernel(place, received, loaded, pressure, window_out, tile_out):
    window_out[...] = pressure[...]
    add_sources(place, received, loaded, window_out, WIDE)
    sums = sum_over_row(place, received)
    tile_out[...] = jnp.zeros(tile_out.shape, F32)
    edges = pick_edges(window_out[...])
    tile_out[0:4, 0:32] = edges[0:4]
    tile_out[4:5, :] = sums[2:3]
    tile_out[5:6, :] = sums[3:4]


def last_kernel(place, received, loaded, pressure, window_out, tile_out):
    window_out[...] = pressure[...]
    add_sources(place, received, loaded, window_out, NARROW)
    tile_out[...] = jnp.zeros(tile_out.shape, F32)
    tile_out[0:4, 0:32] = pick_edges(window_out[...])[0:4]


def beside(place, left, right):
    g = place[1]
    row = iota((8, 128), 0)
    edges = jnp.where((row < 2) & (g < place[3] - 1), right, 0.0)
    edges += jnp.where((row >= 2) & (row < 4) & (g > 0), left, 0.0)
    return spread_edges(edges, 128)


def flow(place, window, window_side, mobility, mobility_side):
    j = place[0]
    p = jnp.concatenate([window, window_side], axis=1)
    lane = iota((32, 128), 1)
    m_side = jnp.where((lane == 0) | (lane == 127), mobility_side, 0.0)
    m = jnp.concatenate([mobility, m_side], axis=1)
    rows = place[4]
    row = lax.rem(iota((32, 256), 0) + (j * 8 - HALO + rows), jnp.full((32, 256), 0, jnp.int32) + rows)
    for step in range(2):
        up = jnp.where(row == 0, 0.0, pltpu.roll(p, 1, 0))
        down = jnp.where(row == rows - 1, 0.0, pltpu.roll(p, 31, 0))
        sides = pltpu.roll(p, 1, 1) + pltpu.roll(p, 255, 1)
        p = p + m * (up + down + sides - 4.0 * p)
    return p[:, 0:128]


def update(place, received, tile, near, refs, window, slip_out, loaded_out):
    (slip, prestress, basis, normal, friction, compliance, state, dilation, pick, weight, h) = refs
    g = place[1]
    row, lane = iota((8, 128), 0), iota((8, 128), 1)
    level = lane // RK + jnp.where(row == 5, 8, 0)
    bit = jnp.maximum(level - GX_BITS, 0)
    own = jnp.right_shift(jnp.zeros((8, 128), jnp.int32) + g, bit)
    total = jnp.where((level < GX_BITS) & (row == 4), tile[...], 0.0)
    within = (level >= GX_BITS) & (level < LV) & ((row == 4) | (row == 5))
    for p in range(received.shape[0]):
        theirs = jnp.right_shift(jnp.full((8, 128), p, jnp.int32), bit)
        total += jnp.where(within & (theirs == jnp.bitwise_xor(own, 1)), received[p], 0.0)
    parts = jnp.where(iota((8, RK), 0) == 4, dot(total, h[0:128, :]), 0.0)
    parts += jnp.where(iota((8, RK), 0) == 5, dot(total, h[128:256, :]), 0.0)
    incoming = dot(parts, jnp.ones((8, 128), F32), TN)

    cells = window[2:26, :]
    both = jnp.concatenate([cells, pltpu.roll(cells, 127, 1)], axis=0)
    split = thirds(both)
    found = dot(split, pick[...], NN, None)
    found = (found[0:48] + found[48:96] + found[96:144]) * weight[...]
    at_row = jnp.sum(found, axis=0, keepdims=True)

    for c in range(8):
        for i in range(3):
            far = jnp.sum(basis[c, i] * incoming, axis=0, keepdims=True)
            slip_out[i, c : c + 1, :] = far
    at_elements = jnp.concatenate([at_row[:, c * 128 : (c + 1) * 128] for c in range(8)], axis=0)
    stress = [prestress[i] - (near[i] + slip_out[i]) for i in range(3)]
    effective = normal[...] - at_elements
    magnitude = jnp.sqrt(stress[0] * stress[0] + stress[1] * stress[1] + stress[2] * stress[2] + 1.0)
    factor = jnp.maximum(1.0 - friction[...] * effective / magnitude, 0.0)
    scaled = state[...].astype(F32) * compliance[...] * factor
    steps = [scaled * stress[i] for i in range(3)]
    for i in range(3):
        slip_out[i] = slip[i] + steps[i]
    dilated = dilation[...] * (steps[0] * steps[0] + steps[1] * steps[1] + steps[2] * steps[2])
    dilated_row = jnp.concatenate([dilated[c : c + 1, :] for c in range(8)], axis=1)
    spread = dot(thirds(weight[...] * dilated_row), pick[...], NT, None)
    spread = spread[0:48] + spread[48:96] + spread[96:144]
    loaded_out[...] = spread[0:24] + pltpu.roll(spread[24:48], 1, 1)


def send_tiles(ahead_out, behind_out, loaded, rows):
    ahead_out[...] = jnp.zeros(ahead_out.shape, F32)
    behind_out[...] = jnp.zeros(behind_out.shape, F32)
    ahead_out[0:rows, :] = loaded[0:rows, :]
    behind_out[0:rows, :] = loaded[24 - rows : 24, :]


def first_update_kernel(place, received, tile, near, *refs):
    refs, (window, lifts), outs = refs[:11], refs[11:13], refs[13:]
    slip_out, loaded_out, ahead_out, behind_out = outs
    update(place, received, tile, near, refs, window, slip_out, loaded_out)
    low, high = project(refs[2], lambda i, c: slip_out[i, c : c + 1, :], lifts)
    send_tiles(ahead_out, behind_out, loaded_out, WIDE)
    for out in (ahead_out, behind_out):
        out[18:19, :] = low[0:1]
        out[19:20, :] = high[0:1]


def second_update_kernel(place, received, tile, near, *refs):
    refs, (window, mobility, mobility_side), outs = refs[:11], refs[11:14], refs[14:]
    slip_out, loaded_out, ahead_out, behind_out, window_out = outs
    g = place[1]
    left = received[jnp.maximum(g - 1, 0)]
    right = received[jnp.minimum(g + 1, received.shape[0] - 1)]
    side = beside(place, left, right)
    window_out[...] = flow(place, window[...], side, mobility[...], mobility_side[...])
    update(place, received, tile, near, refs, window_out, slip_out, loaded_out)
    send_tiles(ahead_out, behind_out, loaded_out, NARROW)


def side_kernel(place, received, side_out):
    g = place[1]
    left = received[jnp.maximum(g - 1, 0)]
    right = received[jnp.minimum(g + 1, received.shape[0] - 1)]
    side_out[...] = beside(place, left, right)


def final_kernel(place, window, left, right, mobility, mobility_side, out):
    side = beside(place, left[...], right[...])
    done = flow(place, window[...], side, mobility[...], mobility_side[...])
    out[...] = done[HALO : HALO + 8, :]


def shift(x, axis, steps):
    n = lax.axis_size(axis)
    return lax.ppermute(x, axis, [(i, (i + steps) % n) for i in range(n)])


def shards(
    slip_field,
    positions,
    neighbours,
    near_counts,
    cluster_basis,
    transfer,
    coupling,
    prestress,
    normal_stress,
    friction,
    compliance,
    slip_state,
    cell_index,
    cell_weight,
    dilation,
    pressure,
    mobility,
):
    nx, ny = lax.axis_size("gx"), lax.axis_size("gy")
    j, g = lax.axis_index("gx"), lax.axis_index("gy")
    rows = 8 * nx
    place = jnp.stack([j, g, g * nx + j, jnp.int32(ny), jnp.int32(rows)]).astype(jnp.int32)
    slip = slip_field.transpose(1, 0, 2)
    points = positions.transpose(1, 0, 2)
    strained = prestress.transpose(1, 0, 2)
    basis = cluster_basis.transpose(0, 2, 1, 3)
    lift_table = transfer.transpose(1, 2, 0).reshape(RK * RK, -1)
    cross_table = coupling.transpose(1, 2, 0).reshape(RK * RK, -1)
    slots = (neighbours - j * 8 + 8 + rows) % rows
    first_cell = cell_index[:, 0, :]
    cell_row = (first_cell // 128 - j * 8 + 8 + rows) % rows
    cell_col = first_cell % 128
    weights = cell_weight.transpose(1, 0, 2)
    ahead_of = (j - jnp.arange(nx, dtype=jnp.int32)) % nx < nx // 2

    both = jnp.concatenate([points, slip], axis=0)
    from_low = shift(both, "gx", 1)
    from_high = shift(both, "gx", -1)
    all_points = jnp.stack([from_low[0:3], points, from_high[0:3]])
    all_slips = jnp.stack([from_low[3:6], slip, from_high[3:6]])

    g_mat, h_mat, tile = call(
        setup_kernel,
        [((256, RK), F32), ((256, RK), F32), ((24, 128), F32)],
        [place, slip, basis, lift_table, cross_table, pressure, mobility],
        smem=1,
    )
    received = lax.all_to_all(jnp.broadcast_to(tile[None], (nx, 24, 128)), "gx", 0, 0, tiled=True)
    pick, weight = call(
        cells_kernel,
        [((128, 1024), BF16), ((48, 1024), F32)],
        [cell_row, cell_col, weights],
        flops=1 << 20,
    )
    window, mobility_window, tile = call(
        first_kernel,
        [((32, 128), F32), ((32, 128), F32), ((8, 128), F32)],
        [place, received],
        smem=1,
    )
    mobility_side = None

    for outer_step in range(2):
        received = lax.all_to_all(
            jnp.broadcast_to(tile[None], (ny, 8, 128)), "gy", 0, 0, tiled=True
        )
        (near,) = call(
            near_kernel,
            [((3, 8, 128), F32)],
            [near_counts, slots, all_points, all_slips],
            scratch=[pltpu.VMEM((3, 128, 128), F32), pltpu.VMEM((3, 128, 128), F32)],
            smem=2,
            flops=1 << 30,
        )
        common = [slip, strained, basis, normal_stress, friction, compliance, slip_state]
        common += [dilation, pick, weight, h_mat]
        if outer_step == 0:
            (mobility_side,) = call(side_kernel, [((32, 128), F32)], [place, received], smem=1)
            slip, loaded, ahead, behind = call(
                first_update_kernel,
                [((3, 8, 128), F32), ((24, 128), F32), ((24, 128), F32), ((24, 128), F32)],
                [place, received, tile, near, *common, window, g_mat],
                smem=1,
            )
        else:
            slip, loaded, ahead, behind, window = call(
                second_update_kernel,
                [
                    ((3, 8, 128), F32),
                    ((24, 128), F32),
                    ((16, 128), F32),
                    ((16, 128), F32),
                    ((32, 128), F32),
                ],
                [place, received, tile, near, *common, window, mobility_window, mobility_side],
                smem=1,
            )
        sent = jnp.where(ahead_of[:, None, None], ahead[None], behind[None])
        received = lax.all_to_all(sent, "gx", 0, 0, tiled=True)
        if outer_step == 0:
            from_low = shift(slip, "gx", 1)
            from_high = shift(slip, "gx", -1)
            all_slips = jnp.stack([from_low, slip, from_high])
        window, tile = call(
            between_kernel if outer_step == 0 else last_kernel,
            [((32, 128), F32), ((8, 128), F32)],
            [place, received, loaded, window],
            smem=1,
        )
    left = shift(tile, "gy", 1)
    right = shift(tile, "gy", -1)
    (final_pressure,) = call(
        final_kernel,
        [((8, 128), F32)],
        [place, window, left, right, mobility_window, mobility_side],
        smem=1,
    )
    return (slip.transpose(1, 0, 2), final_pressure)


def solution(mesh):
    split = ("gy", "gx")
    in_specs = (
        P(split, None, None),
        P(split, None, None),
        P(split, None),
        P(split),
        P(split, None, None, None),
        P(),
        P(),
        P(split, None, None),
        P(split, None),
        P(split, None),
        P(split, None),
        P(split, None),
        P(split, None, None),
        P(split, None, None),
        P(split, None),
        P("gx", "gy"),
        P("gx", "gy"),
    )
    out_specs = (P(split, None, None), P("gx", "gy"))
    return jax.shard_map(shards, mesh=mesh, in_specs=in_specs, out_specs=out_specs, check_vma=False)
```

time: 553 us -> 130 us (0.24)
  the two profiles are of different devices: /device:TPU:95 before, /device:TPU:16 now
where the time goes in v1:
time: 130 us; the launch traced here: 129 us
  starting transfers between devices  49.1 us (38%)
  waiting for transfers between devices  29.4 us (23%)
  Pallas kernels  21.9 us (17%)
  blocking collectives  17.8 us (14%)
  local copies, waits for them, and re-layouts  8.15 us (6%)
  other arithmetic  1.75 us (1%)
    pallas_call x11, Pallas kernels, call(): pl.pallas_call(kernel, out_shape=[jax.ShapeDtypeStruct(s, d) for s, d in...  21.9 us
    all_to_all x1, blocking collectives, shards(): received = lax.all_to_all(sent, 'gx', 0, 0, tiled=True)  17.8 us
    all_to_all x2, starting transfers between devices, shards(): lax.all_to_all(jnp.broadcast_to(tile[None], (ny, 8, 128)), 'gy', 0, 0, ti...  17.3 us
    ppermute x6, starting transfers between devices, shift(): return lax.ppermute(x, axis, [(i, (i + steps) % n) for i in range(n)])  14 us
    all_to_all x1, waiting for transfers between devices, shards(): lax.all_to_all(jnp.broadcast_to(tile[None], (nx, 24, 128)), 'gx', 0, 0, t...  12.6 us
    all_to_all x1, starting transfers between devices, shards(): lax.all_to_all(jnp.broadcast_to(tile[None], (nx, 24, 128)), 'gx', 0, 0, t...  11.4 us
    all_to_all x1, waiting for transfers between devices, shards(): received = lax.all_to_all(sent, 'gx', 0, 0, tiled=True)  7.51 us
    all_to_all x1, starting transfers between devices, shards(): received = lax.all_to_all(sent, 'gx', 0, 0, tiled=True)  6.41 us
  transfers between devices with their start and end apart: 10, of which 6 were waited for; matrix products, arithmetic and copies ran while one was open for 1% of the time, Pallas kernels for 12%

profile of v1, /device:TPU:16, one launch (start us, length us, event | category | flops | bytes accessed | tf_op | source)
XLA Modules:
  0.0 129.1 jit_solution(9911706305341635986)
XLA Ops:
  1.4 4.5 %collective-permute-start.1 = (f32[6,8,128]{2,1,0:T(8,128)S(1)}, f32[6,8,128]{2,1,0:T(8,128)S(1)}, u32[]{:S(2)}, u32[]{:S(2)}) collective-permute-start(f32[6,8,128]{2,1,0:T(8,128)S(1)} %pad_maximum_fusion.3), channel_id=1, source_target_pairs={{0,496},{16,0},{32,16},{48,32},{64,48},{80,64},{96,80},{112,96},{1... | collective-permute-start | bytes 73736 | tf_op jit(solution)/shard_map/ppermute | solution.py:337
  5.9 1.9 %collective-permute-start = (f32[6,8,128]{2,1,0:T(8,128)S(1)}, f32[6,8,128]{2,1,0:T(8,128)S(1)}, u32[]{:S(2)}, u32[]{:S(2)}) collective-permute-start(f32[6,8,128]{2,1,0:T(8,128)S(1)} %pad_maximum_fusion.3), channel_id=1, source_target_pairs={{0,16},{16,32},{32,48},{48,64},{64,80},{80,96},{96,112},{112,128},... | collective-permute-start | bytes 73736 | tf_op jit(solution)/shard_map/ppermute | solution.py:337
  9.5 1.2 copy-done.2
  10.7 1.2 copy-done.3
  11.9 4.0 %shard_map.176 = (f32[256,16]{1,0:T(8,128)S(1)}, f32[256,16]{1,0:T(8,128)S(1)}, f32[24,128]{1,0:T(8,128)S(1)}) custom-call(s32[5]{0:T(128)S(1)} %stack.51.place, f32[3,8,128]{2,1,0:T(8,128)S(1)} %bitcast.41, f32[8,3,16,128]{3,2,1,0:T(8,128)S(1)} %bitcast.35, f32[256,1022]{1,0:T(8,128)S(1)} %bitcast.38, f32[256,1022]{1,0:T(8,128)S(1)} %bitcast.39, ...), custom_call_target="tpu_custom_call" | custom-call | bytes 1048576 | tf_op jit(solution)/shard_map/pallas_call | solution.py:44
  16.7 11.4 %all-to-all-start = ((f32[32,24,128]{2,1,0:T(8,128)}), f32[32,24,128]{2,1,0:T(8,128)S(1)}, u32[]{:S(2)}, u32[]{:S(2)}) async-start(f32[32,24,128]{2,1,0:T(8,128)} %broadcast_in_dim.73), calls=%async_computation | async-start | bytes 786432 | tf_op jit(solution)/shard_map/all_to_all | solution.py:388
  29.0 12.6 %all-to-all-done.received = f32[32,24,128]{2,1,0:T(8,128)S(1)} async-done(((f32[32,24,128]{2,1,0:T(8,128)}), f32[32,24,128]{2,1,0:T(8,128)S(1)}, u32[]{:S(2)}, u32[]{:S(2)}) %all-to-all-start) | async-done | bytes 393248 | tf_op jit(solution)/shard_map/all_to_all | solution.py:388
  43.0 10.6 %all-to-all-start.1 = ((f32[16,8,128]{2,1,0:T(8,128)}), f32[16,8,128]{2,1,0:T(8,128)S(1)}, u32[]{:S(2)}, u32[]{:S(2)}) async-start(f32[16,8,128]{2,1,0:T(8,128)} %broadcast_in_dim.74), calls=%async_computation.1 | async-start | bytes 131072 | tf_op jit(solution)/shard_map/all_to_all | solution.py:404
  54.2 5.0 %shard_map.178.near = f32[3,8,128]{2,1,0:T(8,128)S(1)} custom-call(s32[8]{0:T(128)S(1)} %copy-done.13, s32[8,8]{1,0:T(8,128)S(1)} %add_select_fusion.3.slots, f32[3,3,8,128]{3,2,1,0:T(8,128)S(1)} %get-tuple-element.50.points, f32[3,3,8,128]{3,2,1,0:T(8,128)S(1)} %get-tuple-element.51.slips), custom_call_target="tpu_custom_call" | custom-call | flops 1073741824 | bytes 1048576 | tf_op jit(solution)/shard_map/pallas_call | solution.py:44
  59.2 2.2 %all-to-all-done.1.received = f32[16,8,128]{2,1,0:T(8,128)S(1)} async-done(((f32[16,8,128]{2,1,0:T(8,128)}), f32[16,8,128]{2,1,0:T(8,128)S(1)}, u32[]{:S(2)}, u32[]{:S(2)}) %all-to-all-start.1) | async-done | bytes 65568 | tf_op jit(solution)/shard_map/all_to_all | solution.py:404
  62.1 1.6 %shard_map.180 = (f32[3,8,128]{2,1,0:T(8,128)S(1)}, f32[24,128]{1,0:T(8,128)S(1)}, f32[24,128]{1,0:T(8,128)S(1)}, f32[24,128]{1,0:T(8,128)S(1)}) custom-call(s32[5]{0:T(128)S(1)} %stack.51.place, f32[16,8,128]{2,1,0:T(8,128)S(1)} %all-to-all-done.1.received, f32[8,128]{1,0:T(8,128)S(1)} %get-tuple-element.24.tile, f32[3,8,128]{2,1,0:T(8,128)S(1)} %shard_map.178.near, ...), custom_call_target="tpu_custom_call" | custom-call | bytes 1048576 | tf_op jit(solution)/shard_map/pallas_call | solution.py:44
  64.6 6.4 %all-to-all-start.2 = ((f32[32,24,128]{2,1,0:T(8,128)}), f32[32,24,128]{2,1,0:T(8,128)S(1)}, u32[]{:S(2)}, u32[]{:S(2)}) async-start(f32[32,24,128]{2,1,0:T(8,128)} %broadcast_select_fusion), calls=%async_computation.2 | async-start | bytes 786432 | tf_op jit(solution)/shard_map/all_to_all | solution.py:439
  71.0 4.6 %collective-permute-start.3 = (f32[3,8,128]{2,1,0:T(8,128)S(1)}, f32[3,8,128]{2,1,0:T(8,128)S(1)}, u32[]{:S(2)}, u32[]{:S(2)}) collective-permute-start(f32[3,8,128]{2,1,0:T(8,128)S(1)} %get-tuple-element.34.refs_0_), channel_id=1, source_target_pairs={{0,496},{16,0},{32,16},{48,32},{64,48},{80,64},{96,80},{112,96},{1... | collective-permute-start | bytes 36872 | tf_op jit(solution)/shard_map/ppermute | solution.py:337
  75.6 1.9 %collective-permute-start.2 = (f32[3,8,128]{2,1,0:T(8,128)S(1)}, f32[3,8,128]{2,1,0:T(8,128)S(1)}, u32[]{:S(2)}, u32[]{:S(2)}) collective-permute-start(f32[3,8,128]{2,1,0:T(8,128)S(1)} %get-tuple-element.34.refs_0_), channel_id=1, source_target_pairs={{0,16},{16,32},{32,48},{48,64},{64,80},{80,96},{96,112},{112,128},... | collective-permute-start | bytes 36872 | tf_op jit(solution)/shard_map/ppermute | solution.py:337
  78.3 7.5 %all-to-all-done.2.received = f32[32,24,128]{2,1,0:T(8,128)S(1)} async-done(((f32[32,24,128]{2,1,0:T(8,128)}), f32[32,24,128]{2,1,0:T(8,128)S(1)}, u32[]{:S(2)}, u32[]{:S(2)}) %all-to-all-start.2) | async-done | bytes 393248 | tf_op jit(solution)/shard_map/all_to_all | solution.py:439
  87.1 6.8 %all-to-all-start.3 = ((f32[16,8,128]{2,1,0:T(8,128)}), f32[16,8,128]{2,1,0:T(8,128)S(1)}, u32[]{:S(2)}, u32[]{:S(2)}) async-start(f32[16,8,128]{2,1,0:T(8,128)} %broadcast_in_dim.77), calls=%async_computation.3 | async-start | bytes 131072 | tf_op jit(solution)/shard_map/all_to_all | solution.py:404
  93.9 5.0 %shard_map.182.near = f32[3,8,128]{2,1,0:T(8,128)S(1)} custom-call(s32[8]{0:T(128)S(1)} %copy-done.13, s32[8,8]{1,0:T(8,128)S(1)} %add_select_fusion.3.slots, f32[3,3,8,128]{3,2,1,0:T(8,128)S(1)} %get-tuple-element.50.points, f32[3,3,8,128]{3,2,1,0:T(8,128)S(1)} %pad_maximum_fusion.2.slips), custom_call_target="tpu_custom_call" | custom-call | flops 1073741824 | bytes 1048576 | tf_op jit(solution)/shard_map/pallas_call | solution.py:44
  98.9 2.9 %all-to-all-done.3.received = f32[16,8,128]{2,1,0:T(8,128)S(1)} async-done(((f32[16,8,128]{2,1,0:T(8,128)}), f32[16,8,128]{2,1,0:T(8,128)S(1)}, u32[]{:S(2)}, u32[]{:S(2)}) %all-to-all-start.3) | async-done | bytes 65568 | tf_op jit(solution)/shard_map/all_to_all | solution.py:404
  101.7 2.0 %shard_map.184 = (f32[3,8,128]{2,1,0:T(8,128)}, f32[24,128]{1,0:T(8,128)S(1)}, f32[16,128]{1,0:T(8,128)S(1)}, f32[16,128]{1,0:T(8,128)S(1)}, f32[32,128]{1,0:T(8,128)S(1)}) custom-call(s32[5]{0:T(128)S(1)} %stack.51.place, f32[16,8,128]{2,1,0:T(8,128)S(1)} %all-to-all-done.3.received, f32[8,128]{1,0:T(8,128)S(1)} %get-tuple-element.33.tile, ...), custom_call_target="tpu_custom_call" | custom-call | bytes 1048576 | tf_op jit(solution)/shard_map/pallas_call | solution.py:44
  103.8 17.8 %all_to_all.25.received = f32[32,16,128]{2,1,0:T(8,128)S(1)} all-to-all(f32[32,16,128]{2,1,0:T(8,128)S(1)} %broadcast_select_fusion.1), channel_id=1, replica_groups=mesh['gx'=32,'gy'=16] {'gx'}, dimensions={0} | all-to-all | bytes 524288 | tf_op jit(solution)/shard_map/all_to_all | solution.py:439
  122.3 1.0 collective-permute-start.5
  123.4 1.3 %collective-permute-done.5.right = f32[8,128]{1,0:T(8,128)S(1)} collective-permute-done((f32[8,128]{1,0:T(8,128)S(1)}, f32[8,128]{1,0:T(8,128)S(1)}, u32[]{:S(2)}, u32[]{:S(2)}) %collective-permute-start.5) | collective-permute-done | bytes 4128 | tf_op jit(solution)/shard_map/ppermute | solution.py:337
  124.7 2.9 %collective-permute-done.4.left = f32[8,128]{1,0:T(8,128)S(1)} collective-permute-done((f32[8,128]{1,0:T(8,128)S(1)}, f32[8,128]{1,0:T(8,128)S(1)}, u32[]{:S(2)}, u32[]{:S(2)}) %collective-permute-start.4) | collective-permute-done | bytes 4128 | tf_op jit(solution)/shard_map/ppermute | solution.py:337
  127.6 1.5 %shard_map.186 = f32[8,128]{1,0:T(8,128)} custom-call(s32[5]{0:T(128)S(1)} %stack.51.place, f32[32,128]{1,0:T(8,128)S(1)} %get-tuple-element.42.window, f32[8,128]{1,0:T(8,128)S(1)} %collective-permute-done.4.left, f32[8,128]{1,0:T(8,128)S(1)} %collective-permute-done.5.right, f32[32,128]{1,0:T(8,128)S(1)} %get-tuple-element.36.refs_12_.mobility, ...), custom_call_target="tpu_custom_call" | custom-call | bytes 1048576 | tf_op jit(solution)/shard_map/pallas_call | solution.py:44
  (59 shorter events, 10.4 us)
Async XLA Ops:
  1.4 27.6 %collective-permute-start.1 = (f32[6,8,128]{2,1,0:T(8,128)S(1)}, f32[6,8,128]{2,1,0:T(8,128)S(1)}, u32[]{:S(2)}, u32[]{:S(2)}) collective-permute-start(f32[6,8,128]{2,1,0:T(8,128)S(1)} %pad_maximum_fusion.3), channel_id=1, source_target_pairs={{0,496},{16,0},{32,16},{48,32},{64,48},{80,64},{96,80},{112,96},{1... | collective-permute-start | bytes 73736 | tf_op jit(solution)/shard_map/ppermute | solution.py:337
  5.9 23.1 %collective-permute-start = (f32[6,8,128]{2,1,0:T(8,128)S(1)}, f32[6,8,128]{2,1,0:T(8,128)S(1)}, u32[]{:S(2)}, u32[]{:S(2)}) collective-permute-start(f32[6,8,128]{2,1,0:T(8,128)S(1)} %pad_maximum_fusion.3), channel_id=1, source_target_pairs={{0,16},{16,32},{32,48},{48,64},{64,80},{80,96},{96,112},{112,128},... | collective-permute-start | bytes 73736 | tf_op jit(solution)/shard_map/ppermute | solution.py:337
  7.8 0.7 copy-start.4
  7.9 0.7 copy-start.11
  8.6 0.9 copy-start
  9.5 1.2 copy-start.2
  10.7 1.2 copy-start.3
  16.7 12.1 %copy-start.16 = (s32[8,8]{1,0:T(8,128)S(1)}, s32[8,8]{1,0:T(8,128)}, u32[]{:S(2)}) copy-start(s32[8,8]{1,0:T(8,128)} %param.19) | copy-start | bytes 772
  16.7 24.9 %all-to-all-start = ((f32[32,24,128]{2,1,0:T(8,128)}), f32[32,24,128]{2,1,0:T(8,128)S(1)}, u32[]{:S(2)}, u32[]{:S(2)}) async-start(f32[32,24,128]{2,1,0:T(8,128)} %broadcast_in_dim.73), calls=%async_computation | async-start | bytes 786432 | tf_op jit(solution)/shard_map/all_to_all | solution.py:388
  28.1 0.7 copy-start.15
  43.0 10.6 %copy-start.14 = (f32[8,3,128]{2,0,1:T(8,128)S(1)}, f32[8,3,128]{2,0,1:T(8,128)}, u32[]{:S(2)}) copy-start(f32[8,3,128]{2,0,1:T(8,128)} %param.18) | copy-start | bytes 36868
  43.0 18.4 %all-to-all-start.1 = ((f32[16,8,128]{2,1,0:T(8,128)}), f32[16,8,128]{2,1,0:T(8,128)S(1)}, u32[]{:S(2)}, u32[]{:S(2)}) async-start(f32[16,8,128]{2,1,0:T(8,128)} %broadcast_in_dim.74), calls=%async_computation.1 | async-start | bytes 131072 | tf_op jit(solution)/shard_map/all_to_all | solution.py:404
  54.2 7.2 %copy-start.1 = (f32[8,16,3,128]{3,1,2,0:T(8,128)S(1)}, f32[8,16,3,128]{3,1,2,0:T(8,128)}, u32[]{:S(2)}) copy-start(f32[8,16,3,128]{3,1,2,0:T(8,128)} %param.21) | copy-start | bytes 589828
  54.2 7.2 %copy-start.5 = (f32[8,3,128]{2,0,1:T(8,128)S(1)}, f32[8,3,128]{2,0,1:T(8,128)}, u32[]{:S(2)}) copy-start(f32[8,3,128]{2,0,1:T(8,128)} %param.24) | copy-start | bytes 36868
  54.2 7.2 %copy-start.8 = (f32[8,128]{1,0:T(8,128)S(1)}, f32[8,128]{1,0:T(8,128)}, u32[]{:S(2)}) copy-start(f32[8,128]{1,0:T(8,128)} %refs_5_.3) | copy-start | bytes 12292
  54.2 7.2 %copy-start.9 = (s32[8,128]{1,0:T(8,128)S(1)}, s32[8,128]{1,0:T(8,128)}, u32[]{:S(2)}) copy-start(s32[8,128]{1,0:T(8,128)} %refs_6_.3) | copy-start | bytes 12292
  54.2 7.2 %copy-start.10 = (f32[8,128]{1,0:T(8,128)S(1)}, f32[8,128]{1,0:T(8,128)}, u32[]{:S(2)}) copy-start(f32[8,128]{1,0:T(8,128)} %refs_7_.3) | copy-start | bytes 12292
  61.4 0.7 copy-start.6
  64.6 21.2 %all-to-all-start.2 = ((f32[32,24,128]{2,1,0:T(8,128)}), f32[32,24,128]{2,1,0:T(8,128)S(1)}, u32[]{:S(2)}, u32[]{:S(2)}) async-start(f32[32,24,128]{2,1,0:T(8,128)} %broadcast_select_fusion), calls=%async_computation.2 | async-start | bytes 786432 | tf_op jit(solution)/shard_map/all_to_all | solution.py:439
  71.0 22.9 %collective-permute-start.3 = (f32[3,8,128]{2,1,0:T(8,128)S(1)}, f32[3,8,128]{2,1,0:T(8,128)S(1)}, u32[]{:S(2)}, u32[]{:S(2)}) collective-permute-start(f32[3,8,128]{2,1,0:T(8,128)S(1)} %get-tuple-element.34.refs_0_), channel_id=1, source_target_pairs={{0,496},{16,0},{32,16},{48,32},{64,48},{80,64},{96,80},{112,96},{1... | collective-permute-start | bytes 36872 | tf_op jit(solution)/shard_map/ppermute | solution.py:337
  75.6 18.3 %collective-permute-start.2 = (f32[3,8,128]{2,1,0:T(8,128)S(1)}, f32[3,8,128]{2,1,0:T(8,128)S(1)}, u32[]{:S(2)}, u32[]{:S(2)}) collective-permute-start(f32[3,8,128]{2,1,0:T(8,128)S(1)} %get-tuple-element.34.refs_0_), channel_id=1, source_target_pairs={{0,16},{16,32},{32,48},{48,64},{64,80},{80,96},{96,112},{112,128},... | collective-permute-start | bytes 36872 | tf_op jit(solution)/shard_map/ppermute | solution.py:337
  87.1 14.6 %all-to-all-start.3 = ((f32[16,8,128]{2,1,0:T(8,128)}), f32[16,8,128]{2,1,0:T(8,128)S(1)}, u32[]{:S(2)}, u32[]{:S(2)}) async-start(f32[16,8,128]{2,1,0:T(8,128)} %broadcast_in_dim.77), calls=%async_computation.3 | async-start | bytes 131072 | tf_op jit(solution)/shard_map/all_to_all | solution.py:404
  122.3 2.4 %collective-permute-start.5 = (f32[8,128]{1,0:T(8,128)S(1)}, f32[8,128]{1,0:T(8,128)S(1)}, u32[]{:S(2)}, u32[]{:S(2)}) collective-permute-start(f32[8,128]{1,0:T(8,128)S(1)} %get-tuple-element.43), channel_id=1, source_target_pairs={{0,15},{1,0},{2,1},{3,2},{4,3},{5,4},{6,5},{7,6},{8,7},{9,8},{10,9... | collective-permute-start | bytes 12296 | tf_op jit(solution)/shard_map/ppermute | solution.py:337
  123.4 4.2 %collective-permute-start.4 = (f32[8,128]{1,0:T(8,128)S(1)}, f32[8,128]{1,0:T(8,128)S(1)}, u32[]{:S(2)}, u32[]{:S(2)}) collective-permute-start(f32[8,128]{1,0:T(8,128)S(1)} %get-tuple-element.43), channel_id=1, source_target_pairs={{0,1},{1,2},{2,3},{3,4},{4,5},{5,6},{6,7},{7,8},{8,9},{9,10},{10,1... | collective-permute-start | bytes 12296 | tf_op jit(solution)/shard_map/ppermute | solution.py:337
  (4 other events, 2.7 us)

commit v2 on v1

--- a/solution.py
+++ b/solution.py
@@ -13,8 +13,6 @@
 LV = 9
 RK = 16
 GX_BITS = 5
-WIDE = 18
-NARROW = 10
 HALO = 10
 
 NN = (((1,), (0,)), ((), ()))
@@ -38,16 +36,17 @@
     return jnp.concatenate([hi, mid, low], axis=0)
 
 
-def call(kernel, outs, args, scratch=(), smem=0, flops=0):
+def call(kernel, outs, args, scratch=(), smem=0, far=0, flops=0, room=32):
     specs = [pl.BlockSpec(memory_space=pltpu.SMEM)] * smem
-    specs += [pl.BlockSpec(memory_space=pltpu.VMEM)] * (len(args) - smem)
+    specs += [pl.BlockSpec(memory_space=pl.ANY)] * far
+    specs += [pl.BlockSpec(memory_space=pltpu.VMEM)] * (len(args) - smem - far)
     return pl.pallas_call(
         kernel,
         out_shape=[jax.ShapeDtypeStruct(s, d) for s, d in outs],
         in_specs=specs,
         out_specs=[pl.BlockSpec(memory_space=pltpu.VMEM)] * len(outs),
         scratch_shapes=list(scratch),
-        compiler_params=pltpu.CompilerParams(vmem_limit_bytes=32 * 1024 * 1024),
+        compiler_params=pltpu.CompilerParams(vmem_limit_bytes=room * 1024 * 1024),
         cost_estimate=pl.CostEstimate(flops=flops, bytes_accessed=1 << 20, transcendentals=0),
     )(*args)
 
@@ -62,23 +61,61 @@
 
 
 def setup_kernel(
-    place, slip, basis, transfer, coupling, pressure, mobility, g_out, h_out, tile_out
+    place,
+    transfer,
+    coupling,
+    transfer_end,
+    coupling_end,
+    slip,
+    basis,
+    pressure,
+    mobility,
+    g_out,
+    h_out,
+    sent,
+    held,
+    sems,
 ):
     flat = place[2]
-    nodes = transfer.shape[1]
-    spot = iota((nodes, 256), 0)
-    level = iota((nodes, 256), 1) // RK
-    first = 1024 - jnp.right_shift(jnp.full(level.shape, 1024, jnp.int32), level)
-    wanted = first + jnp.right_shift(jnp.full(level.shape, 0, jnp.int32) + flat, level)
-    pick = jnp.where((spot == wanted) & (level < LV), 1.0, 0.0).astype(F32)
+    blocks = [pl.multiple_of(flat // 128 * 128, 128), pl.multiple_of(512 + flat // 256 * 128, 128)]
+    blocks += [768, 896]
+    copies = []
+    for t, table in enumerate((transfer, coupling)):
+        for b, start in enumerate(blocks[:3]):
+            copies.append(
+                pltpu.make_async_copy(
+                    table.at[:, pl.ds(start, 128)], held.at[t, b], sems.at[t * 3 + b]
+                )
+            )
+            copies[-1].start()
+    total = jnp.zeros((RK, 128), F32)
+    for c in range(8):
+        for i in range(3):
+            total += basis[c, i] * slip[i, c : c + 1, :]
+    moment = dot(jnp.ones((8, 128), F32), total, NT)
+
+    shape = (128, 256)
+    level = iota(shape, 1) // RK
+    first = 1024 - jnp.right_shift(jnp.full(shape, 1024, jnp.int32), level)
+    wanted = first + jnp.right_shift(jnp.zeros(shape, jnp.int32) + flat, level)
+    picks = []
+    for b, start in enumerate(blocks):
+        used = (level == b) if b < 3 else (level >= 3) & (level < LV)
+        picks.append(jnp.where((iota(shape, 0) + start == wanted) & used, 1.0, 0.0).astype(BF16))
     mine = (iota((256, 256), 1) % RK) == (iota((256, 256), 0) // RK)
-
-    def path_matrices(table):
-        spread = jnp.where(mine, dot(table[...], pick), 0.0)
-        return jnp.sum(spread.reshape(RK, RK, 256), axis=0)
-
-    lifts = path_matrices(transfer)
-    across = path_matrices(coupling)
+    for copy in copies:
+        copy.wait()
+
+    def path_matrices(t, end):
+        spread = jnp.zeros((768, 256), F32)
+        for b in range(4):
+            block = held[t, b] if b < 3 else end[...]
+            spread += dot(thirds(block), picks[b], NN, None)
+        spread = spread[0:256] + spread[256:512] + spread[512:768]
+        return jnp.sum(jnp.where(mine, spread, 0.0).reshape(RK, RK, 256), axis=0)
+
+    lifts = path_matrices(0, transfer_end)
+    across = path_matrices(1, coupling_end)
     eye = jnp.where(iota((RK, RK), 0) == iota((RK, RK), 1), 1.0, 0.0).astype(F32)
     g_out[...] = jnp.zeros(g_out.shape, F32)
     h_out[...] = jnp.zeros(h_out.shape, F32)
@@ -88,12 +125,17 @@
         h_out[l * RK : (l + 1) * RK, :] = dot(across[:, l * RK : (l + 1) * RK], chain)
         if l + 1 < LV:
             chain = dot(lifts[:, l * RK : (l + 1) * RK], chain)
-    low, high = project(basis, lambda i, c: slip[i, c : c + 1, :], g_out)
-    tile_out[...] = jnp.zeros(tile_out.shape, F32)
-    tile_out[0:8, :] = pressure[...]
-    tile_out[8:16, :] = mobility[...]
-    tile_out[18:19, :] = low[0:1]
-    tile_out[19:20, :] = high[0:1]
+    low = dot(moment, g_out[0:128, :], NT)
+    high = dot(moment, g_out[128:256, :], NT)
+    row = iota((8, 128), 0)
+    tile = jnp.where(row == 6, low, jnp.where(row == 7, high, 0.0))
+    sent[0] = tile
+    sent[0, 0:2, :] = pressure[0:2, :]
+    sent[0, 2:4, :] = pressure[6:8, :]
+    sent[0, 4:5, :] = mobility[0:1, :]
+    sent[0, 5:6, :] = mobility[7:8, :]
+    for p in range(1, sent.shape[0]):
+        sent[p] = sent[0]
 
 
 def cells_kernel(row_in, col_in, weight, pick_out, weight_out):
@@ -109,12 +151,18 @@
             ) + jnp.where(at == row + 1, weight[2 * side + 1, c : c + 1, :], 0.0)
 
 
-def near_kernel(counts, slots, points, slips, near_out, target, total):
-    ones = jnp.ones((128, 128), F32)
+def near_kernel(counts, slots, own_points, low_points, high_points, own, low, high, near_out, points, slips, target, total):
+    ones = jnp.ones((128, 128), BF16)
     diagonal = iota((128, 128), 0) == iota((128, 128), 1)
+    for b, (p, s) in enumerate(((low_points, low), (own_points, own), (high_points, high))):
+        for i in range(3):
+            points[b, i] = p[i]
+            slips[b, i] = s[i]
     for c in range(8):
         for i in range(3):
-            target[i] = jnp.transpose(jnp.broadcast_to(points[1, i, c : c + 1, :], (128, 128)))
+            wide = jnp.where(diagonal, own_points[i, c : c + 1, :], 0.0)
+            wide = dot(thirds(wide), ones, NN, None)
+            target[i] = wide[0:128] + wide[128:256] + wide[256:384]
         total[...] = jnp.zeros(total.shape, F32)
 
         def one_source(k, _):
@@ -134,7 +182,8 @@
 
         lax.fori_loop(0, counts[c], one_source, 0)
         for i in range(3):
-            summed = dot(total[i], ones)
+            summed = dot(thirds(total[i]), ones, NN, None)
+            summed = summed[0:128] + summed[128:256] + summed[256:384]
             near_out[i, c : c + 1, :] = SCALE * jnp.sum(
                 jnp.where(diagonal, summed, 0.0), axis=0, keepdims=True
             )
@@ -154,72 +203,80 @@
     return dot(edges[:, 0:32], pick, TN)
 
 
-def sum_over_row(place, received):
+def sum_over_row(place, received, at, first):
     j = place[0]
     row, lane = iota((8, 128), 0), iota((8, 128), 1)
-    level = lane // RK + jnp.where(row == 3, 8, 0)
+    level = lane // RK + jnp.where(row == first + 1, 8, 0)
     own = jnp.right_shift(jnp.zeros((8, 128), jnp.int32) + j, level)
     total = jnp.zeros((8, 128), F32)
     for p in range(received.shape[0]):
         theirs = jnp.right_shift(jnp.full((8, 128), p, jnp.int32), level)
         used = (level >= GX_BITS) | (theirs == jnp.bitwise_xor(own, 1))
-        total += jnp.where(used, received[p, 16:24, :], 0.0)
+        total += jnp.where(used, received[p, at : at + 8, :], 0.0)
     return total
 
 
-def first_kernel(place, received, pressure_out, mobility_out, tile_out):
+def copies_of(tile, sent):
+    for p in range(sent.shape[0]):
+        sent[p] = tile[...]
+
+
+def first_kernel(place, received, low, high, pressure, mobility, pressure_out, mobility_out, tile_out, sent):
     j = place[0]
     peers = received.shape[0]
+    before = lax.rem(j - 2 + peers, peers)
+    after = lax.rem(j + 2, peers)
     pressure_out[...] = jnp.zeros(pressure_out.shape, F32)
     mobility_out[...] = jnp.zeros(mobility_out.shape, F32)
-    for out, at in ((pressure_out, 0), (mobility_out, 8)):
-        for off in (-1, 0, 1):
-            p = lax.rem(j + off + peers, peers)
-            out[HALO + 8 * off : HALO + 8 * off + 8, :] = received[p, at : at + 8, :]
-        p = lax.rem(j - 2 + peers, peers)
-        out[0:2, :] = received[p, at + 6 : at + 8, :]
-        p = lax.rem(j + 2, peers)
-        out[26:28, :] = received[p, at : at + 2, :]
-    sums = sum_over_row(place, received)
+    pressure_out[0:2, :] = received[before, 2:4, :]
+    pressure_out[2:10, :] = low[6]
+    pressure_out[10:18, :] = pressure[...]
+    pressure_out[18:26, :] = high[6]
+    pressure_out[26:28, :] = received[after, 0:2, :]
+    mobility_out[1:2, :] = received[before, 5:6, :]
+    mobility_out[2:10, :] = low[7]
+    mobility_out[10:18, :] = mobility[...]
+    mobility_out[18:26, :] = high[7]
+    mobility_out[26:27, :] = received[after, 4:5, :]
+    sums = sum_over_row(place, received, 0, 6)
     tile_out[...] = jnp.zeros(tile_out.shape, F32)
     edges = pick_edges(mobility_out[...])
-    tile_out[4:5, :] = sums[2:3]
-    tile_out[5:6, :] = sums[3:4]
+    tile_out[4:6, :] = sums[6:8]
     tile_out[0:4, 0:32] = edges[0:4]
-
-
-def add_sources(place, received, loaded, window, rows):
+    copies_of(tile_out, sent)
+
+
+def between_kernel(place, received, low, high, loaded, pressure, window, tile_out, sent):
     j = place[0]
     peers = received.shape[0]
+    window[...] = pressure[...]
     window[2:26, :] += loaded[...]
-    for off in range(1, 4):
-        kept = rows - 8 * (off - 1)
-        if kept <= 0:
-            continue
-        p = lax.rem(j + off, peers)
-        at = HALO + 8 * (off - 1)
-        window[at : at + kept, :] += received[p, 0:kept, :]
-        p = lax.rem(j - off + peers, peers)
-        at = HALO + 8 - rows
-        window[at : at + kept, :] += received[p, rows - kept : rows, :]
-
-
-def between_kernel(place, received, loaded, pressure, window_out, tile_out):
-    window_out[...] = pressure[...]
-    add_sources(place, received, loaded, window_out, WIDE)
-    sums = sum_over_row(place, received)
+    for i, at, size in ((3, 0, 8), (4, 8, 8), (5, 16, 2)):
+        window[at : at + size, :] += low[i, 0:size, :]
+        window[at + 10 : at + 10 + size, :] += high[i, 0:size, :]
+    window[18:28, :] += received[lax.rem(j + 2, peers), 0:10, :]
+    window[0:10, :] += received[lax.rem(j - 2 + peers, peers), 0:10, :]
+    window[26:28, :] += received[lax.rem(j + 3, peers), 0:2, :]
+    window[0:2, :] += received[lax.rem(j - 3 + peers, peers), 8:10, :]
+    sums = sum_over_row(place, received, 8, 2)
     tile_out[...] = jnp.zeros(tile_out.shape, F32)
-    edges = pick_edges(window_out[...])
+    edges = pick_edges(window[...])
     tile_out[0:4, 0:32] = edges[0:4]
-    tile_out[4:5, :] = sums[2:3]
-    tile_out[5:6, :] = sums[3:4]
-
-
-def last_kernel(place, received, loaded, pressure, window_out, tile_out):
-    window_out[...] = pressure[...]
-    add_sources(place, received, loaded, window_out, NARROW)
+    tile_out[4:6, :] = sums[2:4]
+    copies_of(tile_out, sent)
+
+
+def last_kernel(place, received, loaded, pressure, window, tile_out):
+    j = place[0]
+    peers = received.shape[0]
+    window[...] = pressure[...]
+    window[2:26, :] += loaded[...]
+    window[10:20, :] += received[lax.rem(j + 1, peers), 0:10, :]
+    window[8:18, :] += received[lax.rem(j - 1 + peers, peers), 0:10, :]
+    window[18:20, :] += received[lax.rem(j + 2, peers), 0:2, :]
+    window[8:10, :] += received[lax.rem(j - 2 + peers, peers), 8:10, :]
     tile_out[...] = jnp.zeros(tile_out.shape, F32)
-    tile_out[0:4, 0:32] = pick_edges(window_out[...])[0:4]
+    tile_out[0:4, 0:32] = pick_edges(window[...])[0:4]
 
 
 def beside(place, left, right):
@@ -289,34 +346,46 @@
     loaded_out[...] = spread[0:24] + pltpu.roll(spread[24:48], 1, 1)
 
 
-def send_tiles(ahead_out, behind_out, loaded, rows):
-    ahead_out[...] = jnp.zeros(ahead_out.shape, F32)
-    behind_out[...] = jnp.zeros(behind_out.shape, F32)
-    ahead_out[0:rows, :] = loaded[0:rows, :]
-    behind_out[0:rows, :] = loaded[24 - rows : 24, :]
+def send_sources(place, loaded, ahead, behind, sent):
+    j = place[0]
+    peers = sent.shape[0]
+    ahead[0:10, :] = loaded[0:10, :]
+    behind[0:10, :] = loaded[14:24, :]
+    for p in range(peers):
+        back = lax.rem(j - p + peers, peers) < peers // 2
+        sent[p] = jnp.where(back, ahead[...], behind[...])
 
 
 def first_update_kernel(place, received, tile, near, *refs):
     refs, (window, lifts), outs = refs[:11], refs[11:13], refs[13:]
-    slip_out, loaded_out, ahead_out, behind_out = outs
-    update(place, received, tile, near, refs, window, slip_out, loaded_out)
+    slip_out, loaded, down_out, up_out, sent, ahead, behind = outs
+    update(place, received, tile, near, refs, window, slip_out, loaded)
     low, high = project(refs[2], lambda i, c: slip_out[i, c : c + 1, :], lifts)
-    send_tiles(ahead_out, behind_out, loaded_out, WIDE)
-    for out in (ahead_out, behind_out):
-        out[18:19, :] = low[0:1]
-        out[19:20, :] = high[0:1]
+    for out in (ahead, behind):
+        out[...] = jnp.zeros(out.shape, F32)
+        out[10:11, :] = low[0:1]
+        out[11:12, :] = high[0:1]
+    send_sources(place, loaded, ahead, behind, sent)
+    for out, at in ((down_out, 0), (up_out, 6)):
+        out[0:3] = slip_out[...]
+        out[3] = loaded[at : at + 8, :]
+        out[4] = loaded[at + 8 : at + 16, :]
+        out[5] = jnp.zeros((8, 128), F32)
+        out[5, 0:2, :] = loaded[at + 16 : at + 18, :]
 
 
 def second_update_kernel(place, received, tile, near, *refs):
     refs, (window, mobility, mobility_side), outs = refs[:11], refs[11:14], refs[14:]
-    slip_out, loaded_out, ahead_out, behind_out, window_out = outs
+    slip_out, loaded, window_out, sent, ahead, behind = outs
     g = place[1]
     left = received[jnp.maximum(g - 1, 0)]
     right = received[jnp.minimum(g + 1, received.shape[0] - 1)]
     side = beside(place, left, right)
     window_out[...] = flow(place, window[...], side, mobility[...], mobility_side[...])
-    update(place, received, tile, near, refs, window_out, slip_out, loaded_out)
-    send_tiles(ahead_out, behind_out, loaded_out, NARROW)
+    update(place, received, tile, near, refs, window_out, slip_out, loaded)
+    for out in (ahead, behind):
+        out[...] = jnp.zeros(out.shape, F32)
+    send_sources(place, loaded, ahead, behind, sent)
 
 
 def side_kernel(place, received, side_out):
@@ -366,87 +435,105 @@
     basis = cluster_basis.transpose(0, 2, 1, 3)
     lift_table = transfer.transpose(1, 2, 0).reshape(RK * RK, -1)
     cross_table = coupling.transpose(1, 2, 0).reshape(RK * RK, -1)
+    lift_end = jnp.pad(lift_table[:, 896:], ((0, 0), (0, 1024 - lift_table.shape[1])))
+    cross_end = jnp.pad(cross_table[:, 896:], ((0, 0), (0, 1024 - cross_table.shape[1])))
     slots = (neighbours - j * 8 + 8 + rows) % rows
     first_cell = cell_index[:, 0, :]
     cell_row = (first_cell // 128 - j * 8 + 8 + rows) % rows
     cell_col = first_cell % 128
     weights = cell_weight.transpose(1, 0, 2)
-    ahead_of = (j - jnp.arange(nx, dtype=jnp.int32)) % nx < nx // 2
-
-    both = jnp.concatenate([points, slip], axis=0)
-    from_low = shift(both, "gx", 1)
-    from_high = shift(both, "gx", -1)
-    all_points = jnp.stack([from_low[0:3], points, from_high[0:3]])
-    all_slips = jnp.stack([from_low[3:6], slip, from_high[3:6]])
-
-    g_mat, h_mat, tile = call(
+
+    g_mat, h_mat, sent = call(
         setup_kernel,
-        [((256, RK), F32), ((256, RK), F32), ((24, 128), F32)],
-        [place, slip, basis, lift_table, cross_table, pressure, mobility],
+        [((256, RK), F32), ((256, RK), F32), ((nx, 8, 128), F32)],
+        [place, lift_table, cross_table, lift_end, cross_end, slip, basis, pressure, mobility],
+        scratch=[pltpu.VMEM((2, 3, 256, 128), F32), pltpu.SemaphoreType.DMA((6,))],
         smem=1,
+        far=2,
+        room=60,
     )
-    received = lax.all_to_all(jnp.broadcast_to(tile[None], (nx, 24, 128)), "gx", 0, 0, tiled=True)
+    both = jnp.concatenate([slip, points, pressure[None], mobility[None]], axis=0)
+    both, sent = lax.optimization_barrier((both, sent))
+    received = lax.all_to_all(sent, "gx", 0, 0, tiled=True)
+    low = shift(both, "gx", 1)
+    high = shift(both, "gx", -1)
+    low_points, high_points = low[3:6], high[3:6]
     pick, weight = call(
         cells_kernel,
         [((128, 1024), BF16), ((48, 1024), F32)],
         [cell_row, cell_col, weights],
         flops=1 << 20,
     )
-    window, mobility_window, tile = call(
-        first_kernel,
-        [((32, 128), F32), ((32, 128), F32), ((8, 128), F32)],
-        [place, received],
-        smem=1,
-    )
     mobility_side = None
+    window = mobility_window = loaded = None
 
     for outer_step in range(2):
-        received = lax.all_to_all(
-            jnp.broadcast_to(tile[None], (ny, 8, 128)), "gy", 0, 0, tiled=True
-        )
         (near,) = call(
             near_kernel,
             [((3, 8, 128), F32)],
-            [near_counts, slots, all_points, all_slips],
-            scratch=[pltpu.VMEM((3, 128, 128), F32), pltpu.VMEM((3, 128, 128), F32)],
+            [near_counts, slots, points, low_points, high_points, slip, low, high],
+            scratch=[
+                pltpu.VMEM((3, 3, 8, 128), F32),
+                pltpu.VMEM((3, 3, 8, 128), F32),
+                pltpu.VMEM((3, 128, 128), F32),
+                pltpu.VMEM((3, 128, 128), F32),
+            ],
             smem=2,
-            flops=1 << 30,
+            flops=1 << 28,
         )
-        common = [slip, strained, basis, normal_stress, friction, compliance, slip_state]
-        common += [dilation, pick, weight, h_mat]
         if outer_step == 0:
-            (mobility_side,) = call(side_kernel, [((32, 128), F32)], [place, received], smem=1)
-            slip, loaded, ahead, behind = call(
-                first_update_kernel,
-                [((3, 8, 128), F32), ((24, 128), F32), ((24, 128), F32), ((24, 128), F32)],
-                [place, received, tile, near, *common, window, g_mat],
+            window, mobility_window, tile, sent = call(
+                first_kernel,
+                [((32, 128), F32), ((32, 128), F32), ((8, 128), F32), ((ny, 8, 128), F32)],
+                [place, received, low, high, pressure, mobility],
                 smem=1,
             )
         else:
-            slip, loaded, ahead, behind, window = call(
-                second_update_kernel,
+            window, tile, sent = call(
+                between_kernel,
+                [((32, 128), F32), ((8, 128), F32), ((ny, 8, 128), F32)],
+                [place, received, low, high, loaded, window],
+                smem=1,
+            )
+        early = (near, sent, pick, weight, mobility_side)
+        near, sent, pick, weight, mobility_side = lax.optimization_barrier(early)
+        received = lax.all_to_all(sent, "gy", 0, 0, tiled=True)
+        common = [slip, strained, basis, normal_stress, friction, compliance, slip_state]
+        common += [dilation, pick, weight, h_mat]
+        pieces = [pltpu.VMEM((16, 128), F32), pltpu.VMEM((16, 128), F32)]
+        if outer_step == 0:
+            slip, loaded, down, up, sent = call(
+                first_update_kernel,
                 [
                     ((3, 8, 128), F32),
                     ((24, 128), F32),
-                    ((16, 128), F32),
-                    ((16, 128), F32),
-                    ((32, 128), F32),
+                    ((6, 8, 128), F32),
+                    ((6, 8, 128), F32),
+                    ((nx, 16, 128), F32),
                 ],
-                [place, received, tile, near, *common, window, mobility_window, mobility_side],
+                [place, received, tile, near, *common, window, g_mat],
+                scratch=pieces,
                 smem=1,
             )
-        sent = jnp.where(ahead_of[:, None, None], ahead[None], behind[None])
-        received = lax.all_to_all(sent, "gx", 0, 0, tiled=True)
-        if outer_step == 0:
-            from_low = shift(slip, "gx", 1)
-            from_high = shift(slip, "gx", -1)
-            all_slips = jnp.stack([from_low, slip, from_high])
-        window, tile = call(
-            between_kernel if outer_step == 0 else last_kernel,
-            [((32, 128), F32), ((8, 128), F32)],
-            [place, received, loaded, window],
-            smem=1,
-        )
+            (mobility_side,) = call(side_kernel, [((32, 128), F32)], [place, received], smem=1)
+            received = lax.all_to_all(sent, "gx", 0, 0, tiled=True)
+            low = shift(up, "gx", 1)
+            high = shift(down, "gx", -1)
+        else:
+            slip, loaded, window, sent = call(
+                second_update_kernel,
+                [((3, 8, 128), F32), ((24, 128), F32), ((32, 128), F32), ((nx, 16, 128), F32)],
+                [place, received, tile, near, *common, window, mobility_window, mobility_side],
+                scratch=pieces,
+                smem=1,
+            )
+            received = lax.all_to_all(sent, "gx", 0, 0, tiled=True)
+    window, tile = call(
+        last_kernel,
+        [((32, 128), F32), ((8, 128), F32)],
+        [place, received, loaded, window],
+        smem=1,
+    )
     left = shift(tile, "gy", 1)
     right = shift(tile, "gy", -1)
     (final_pressure,) = call(

time: 130 us -> 129 us (level)
  the two profiles are of different devices: /device:TPU:16 before, /device:TPU:8 now
where the time goes in v2:
time: 129 us
  blocking collectives  55.6 us (43%)
  starting transfers between devices  34 us (26%)
  Pallas kernels  24 us (19%)
  waiting for transfers between devices  7.51 us (6%)
  local copies, waits for them, and re-layouts  6.54 us (5%)
    all_to_all x2, blocking collectives, shards(): received = lax.all_to_all(sent, 'gy', 0, 0, tiled=True)  29.4 us
    all_to_all x1, blocking collectives, shards(): received = lax.all_to_all(sent, 'gx', 0, 0, tiled=True)  26.2 us
    pallas_call x11, Pallas kernels, call(): pl.pallas_call(kernel, out_shape=[jax.ShapeDtypeStruct(s, d) for s, d in...  24 us
    all_to_all x2, starting transfers between devices, shards(): received = lax.all_to_all(sent, 'gx', 0, 0, tiled=True)  19 us
    ppermute x6, starting transfers between devices, shift(): return lax.ppermute(x, axis, [(i, (i + steps) % n) for i in range(n)])  14.9 us
    ppermute x6, waiting for transfers between devices, shift(): return lax.ppermute(x, axis, [(i, (i + steps) % n) for i in range(n)])  4.48 us
    all_to_all x2, waiting for transfers between devices, shards(): received = lax.all_to_all(sent, 'gx', 0, 0, tiled=True)  3.03 us
  transfers between devices with their start and end apart: 8, of which 4 were waited for; matrix products, arithmetic and copies ran while one was open for 0% of the time, Pallas kernels for 8%

profile of v2, /device:TPU:8, one launch (start us, length us, event | category | flops | bytes accessed | tf_op | source)
XLA Modules:
  0.0 128.6 jit_solution(3299530321725945999)
XLA Ops:
  0.6 0.9 slice.20
  1.6 0.9 slice.21
  5.1 5.2 %shard_map.176 = (f32[256,16]{1,0:T(8,128)}, f32[256,16]{1,0:T(8,128)}, f32[32,8,128]{2,1,0:T(8,128)}) custom-call(s32[5]{0:T(128)} %stack.15.place, f32[256,1022]{1,0:T(8,128)} %bitcast.38, f32[256,1022]{1,0:T(8,128)} %bitcast.40, f32[256,128]{1,0:T(8,128)} %pad.7.transfer_end, f32[256,128]{1,0:T(8,128)} %pad.8.coupling_end, f32[3,8,128]{2,1,0:T(8,128)} %bitcast.25, ...), custom_call_target="tpu_custom_call" | custom-call | bytes 1048576 | tf_op jit(solution)/shard_map/pallas_call | solution.py:43
  10.4 4.6 %collective-permute-start.1 = (f32[8,8,128]{2,1,0:T(8,128)S(1)}, f32[8,8,128]{2,1,0:T(8,128)S(1)}, u32[]{:S(2)}, u32[]{:S(2)}) collective-permute-start(f32[8,8,128]{2,1,0:T(8,128)S(1)} %pad_maximum_fusion), channel_id=1, source_target_pairs={{0,496},{16,0},{32,16},{48,32},{64,48},{80,64},{96,80},{112,96},{1... | collective-permute-start | bytes 98312 | tf_op jit(solution)/shard_map/ppermute | solution.py:406
  14.9 1.9 %collective-permute-start = (f32[8,8,128]{2,1,0:T(8,128)S(1)}, f32[8,8,128]{2,1,0:T(8,128)S(1)}, u32[]{:S(2)}, u32[]{:S(2)}) collective-permute-start(f32[8,8,128]{2,1,0:T(8,128)S(1)} %pad_maximum_fusion), channel_id=1, source_target_pairs={{0,16},{16,32},{32,48},{48,64},{64,80},{80,96},{96,112},{112,128},... | collective-permute-start | bytes 98312 | tf_op jit(solution)/shard_map/ppermute | solution.py:406
  16.9 11.4 %all-to-all-start = ((f32[32,8,128]{2,1,0:T(8,128)}), f32[32,8,128]{2,1,0:T(8,128)S(1)}, u32[]{:S(2)}, u32[]{:S(2)}) async-start(f32[32,8,128]{2,1,0:T(8,128)} %get-tuple-element.38), calls=%async_computation | async-start | bytes 262144 | tf_op jit(solution)/shard_map/all_to_all | solution.py:457
  29.9 4.8 %shard_map.177.near = f32[3,8,128]{2,1,0:T(8,128)S(1)} custom-call(s32[8]{0:T(128)S(1)} %copy-done.17, s32[8,8]{1,0:T(8,128)S(1)} %add_select_fusion.3.slots, f32[3,8,128]{2,1,0:T(8,128)S(1)} %bitcast.35, f32[3,8,128]{2,1,0:T(8,128)S(1)} %slice.22.low_points, f32[3,8,128]{2,1,0:T(8,128)S(1)} %slice.23.high_points, f32[3,8,128]{2,1,0:T(8,128)S(1)} %bitcast.27, ...), custom_call_target="tpu_custom_call" | custom-call | flops 268435456 | bytes 1048576 | tf_op jit(solution)/shard_map/pallas_call | solution.py:43
  34.8 3.0 %all-to-all-done.received = f32[32,8,128]{2,1,0:T(8,128)S(1)} async-done(((f32[32,8,128]{2,1,0:T(8,128)}), f32[32,8,128]{2,1,0:T(8,128)S(1)}, u32[]{:S(2)}, u32[]{:S(2)}) %all-to-all-start) | async-done | bytes 131104 | tf_op jit(solution)/shard_map/all_to_all | solution.py:457
  37.8 0.7 shard_map.178
  38.5 18.2 %all_to_all.25.received = f32[16,8,128]{2,1,0:T(8,128)S(1)} all-to-all(f32[16,8,128]{2,1,0:T(8,128)S(1)} %get-tuple-element.42), channel_id=1, replica_groups=mesh['gx'=32,'gy'=16] {'gy'}, dimensions={0} | all-to-all | bytes 131072 | tf_op jit(solution)/shard_map/all_to_all | solution.py:500
  57.5 2.3 %shard_map.180 = (f32[3,8,128]{2,1,0:T(8,128)S(1)}, f32[24,128]{1,0:T(8,128)S(1)}, f32[6,8,128]{2,1,0:T(8,128)S(1)}, f32[6,8,128]{2,1,0:T(8,128)S(1)}, f32[32,16,128]{2,1,0:T(8,128)}) custom-call(s32[5]{0:T(128)S(1)} %copy-done.6, f32[16,8,128]{2,1,0:T(8,128)S(1)} %all_to_all.25.received, f32[8,128]{1,0:T(8,128)S(1)} %get-tuple-element.43.tile, ...), custom_call_target="tpu_custom_call" | custom-call | bytes 1048576 | tf_op jit(solution)/shard_map/pallas_call | solution.py:43
  59.8 7.6 %all-to-all-start.2 = ((f32[32,16,128]{2,1,0:T(8,128)}), f32[32,16,128]{2,1,0:T(8,128)S(1)}, u32[]{:S(2)}, u32[]{:S(2)}) async-start(f32[32,16,128]{2,1,0:T(8,128)} %get-tuple-element.53), calls=%async_computation.2 | async-start | bytes 524288 | tf_op jit(solution)/shard_map/all_to_all | solution.py:519
  67.5 3.4 %collective-permute-start.2 = (f32[6,8,128]{2,1,0:T(8,128)S(1)}, f32[6,8,128]{2,1,0:T(8,128)S(1)}, u32[]{:S(2)}, u32[]{:S(2)}) collective-permute-start(f32[6,8,128]{2,1,0:T(8,128)S(1)} %get-tuple-element.51), channel_id=1, source_target_pairs={{0,16},{16,32},{32,48},{48,64},{64,80},{80,96},{96,112},{112,128},... | collective-permute-start | bytes 73736 | tf_op jit(solution)/shard_map/ppermute | solution.py:406
  70.8 4.6 %collective-permute-start.3 = (f32[6,8,128]{2,1,0:T(8,128)S(1)}, f32[6,8,128]{2,1,0:T(8,128)S(1)}, u32[]{:S(2)}, u32[]{:S(2)}) collective-permute-start(f32[6,8,128]{2,1,0:T(8,128)S(1)} %get-tuple-element.52), channel_id=1, source_target_pairs={{0,496},{16,0},{32,16},{48,32},{64,48},{80,64},{96,80},{112,96},{1... | collective-permute-start | bytes 73736 | tf_op jit(solution)/shard_map/ppermute | solution.py:406
  75.4 0.7 shard_map.183.refs_13_.mobility_side
  76.2 0.7 collective-permute-done.3.high
  76.9 4.8 %shard_map.181.near = f32[3,8,128]{2,1,0:T(8,128)S(1)} custom-call(s32[8]{0:T(128)S(1)} %copy-done.17, s32[8,8]{1,0:T(8,128)S(1)} %add_select_fusion.3.slots, f32[3,8,128]{2,1,0:T(8,128)S(1)} %bitcast.36, f32[3,8,128]{2,1,0:T(8,128)S(1)} %slice.22.low_points, f32[3,8,128]{2,1,0:T(8,128)S(1)} %slice.23.high_points, ...), custom_call_target="tpu_custom_call" | custom-call | flops 268435456 | bytes 1048576 | tf_op jit(solution)/shard_map/pallas_call | solution.py:43
  81.8 0.7 shard_map.182
  82.5 11.1 %all_to_all.26.received = f32[16,8,128]{2,1,0:T(8,128)S(1)} all-to-all(f32[16,8,128]{2,1,0:T(8,128)S(1)} %get-tuple-element.56), channel_id=1, replica_groups=mesh['gx'=32,'gy'=16] {'gy'}, dimensions={0} | all-to-all | bytes 131072 | tf_op jit(solution)/shard_map/all_to_all | solution.py:500
  93.6 2.2 %shard_map.184 = (f32[3,8,128]{2,1,0:T(8,128)}, f32[24,128]{1,0:T(8,128)S(1)}, f32[32,128]{1,0:T(8,128)S(1)}, f32[32,16,128]{2,1,0:T(8,128)S(1)}) custom-call(s32[5]{0:T(128)S(1)} %copy-done.6, f32[16,8,128]{2,1,0:T(8,128)S(1)} %all_to_all.26.received, f32[8,128]{1,0:T(8,128)S(1)} %get-tuple-element.57.tile, f32[3,8,128]{2,1,0:T(8,128)S(1)} %shard_map.181.near, ...), custom_call_target="tpu_custom_call" | custom-call | bytes 1048576 | tf_op jit(solution)/shard_map/pallas_call | solution.py:43
  95.9 26.2 %all_to_all.27.received = f32[32,16,128]{2,1,0:T(8,128)S(1)} all-to-all(f32[32,16,128]{2,1,0:T(8,128)S(1)} %get-tuple-element.65), channel_id=1, replica_groups=mesh['gx'=32,'gy'=16] {'gx'}, dimensions={0} | all-to-all | bytes 524288 | tf_op jit(solution)/shard_map/all_to_all | solution.py:530
  123.3 0.8 collective-permute-done.5.right
  124.1 2.9 %collective-permute-done.4.left = f32[8,128]{1,0:T(8,128)S(1)} collective-permute-done((f32[8,128]{1,0:T(8,128)S(1)}, f32[8,128]{1,0:T(8,128)S(1)}, u32[]{:S(2)}, u32[]{:S(2)}) %collective-permute-start.4) | collective-permute-done | bytes 4128 | tf_op jit(solution)/shard_map/ppermute | solution.py:406
  127.1 1.5 %shard_map.186 = f32[8,128]{1,0:T(8,128)} custom-call(s32[5]{0:T(128)S(1)} %copy-done.6, f32[32,128]{1,0:T(8,128)S(1)} %get-tuple-element.68.window, f32[8,128]{1,0:T(8,128)S(1)} %collective-permute-done.4.left, f32[8,128]{1,0:T(8,128)S(1)} %collective-permute-done.5.right, f32[32,128]{1,0:T(8,128)S(1)} %get-tuple-element.62.refs_12_.mobility, ...), custom_call_target="tpu_custom_call" | custom-call | bytes 1048576 | tf_op jit(solution)/shard_map/pallas_call | solution.py:43
  (59 shorter events, 6.1 us)
Async XLA Ops:
  3.1 0.7 copy-start.3
  3.1 0.7 copy-start.16
  3.8 0.7 copy-start.7
  10.4 18.8 %collective-permute-start.1 = (f32[8,8,128]{2,1,0:T(8,128)S(1)}, f32[8,8,128]{2,1,0:T(8,128)S(1)}, u32[]{:S(2)}, u32[]{:S(2)}) collective-permute-start(f32[8,8,128]{2,1,0:T(8,128)S(1)} %pad_maximum_fusion), channel_id=1, source_target_pairs={{0,496},{16,0},{32,16},{48,32},{64,48},{80,64},{96,80},{112,96},{1... | collective-permute-start | bytes 98312 | tf_op jit(solution)/shard_map/ppermute | solution.py:406
  14.9 14.2 %collective-permute-start = (f32[8,8,128]{2,1,0:T(8,128)S(1)}, f32[8,8,128]{2,1,0:T(8,128)S(1)}, u32[]{:S(2)}, u32[]{:S(2)}) collective-permute-start(f32[8,8,128]{2,1,0:T(8,128)S(1)} %pad_maximum_fusion), channel_id=1, source_target_pairs={{0,16},{16,32},{32,48},{48,64},{64,80},{80,96},{96,112},{112,128},... | collective-permute-start | bytes 98312 | tf_op jit(solution)/shard_map/ppermute | solution.py:406
  16.9 12.1 %copy-start.19 = (s32[8,8]{1,0:T(8,128)S(1)}, s32[8,8]{1,0:T(8,128)}, u32[]{:S(2)}) copy-start(s32[8,8]{1,0:T(8,128)} %param.19) | copy-start | bytes 772
  16.9 20.9 %all-to-all-start = ((f32[32,8,128]{2,1,0:T(8,128)}), f32[32,8,128]{2,1,0:T(8,128)S(1)}, u32[]{:S(2)}, u32[]{:S(2)}) async-start(f32[32,8,128]{2,1,0:T(8,128)} %get-tuple-element.38), calls=%async_computation | async-start | bytes 262144 | tf_op jit(solution)/shard_map/all_to_all | solution.py:457
  28.3 0.7 copy-start.18
  29.2 0.7 copy-start.4
  29.9 8.0 %copy-start.6 = (s32[5]{0:T(128)S(1)}, s32[5]{0:T(128)}, u32[]{:S(2)}) copy-start(s32[5]{0:T(128)} %stack.15.place) | copy-start | bytes 64
  29.9 8.0 %copy-start.8 = (f32[8,128]{1,0:T(8,128)S(1)}, f32[8,128]{1,0:T(8,128)}, u32[]{:S(2)}) copy-start(f32[8,128]{1,0:T(8,128)} %pressure.3) | copy-start | bytes 12292
  29.9 8.0 %copy-start.10 = (f32[8,128]{1,0:T(8,128)S(1)}, f32[8,128]{1,0:T(8,128)}, u32[]{:S(2)}) copy-start(f32[8,128]{1,0:T(8,128)} %mobility.3) | copy-start | bytes 12292
  29.9 26.9 %copy-start.2 = (f32[256,16]{1,0:T(8,128)S(1)}, f32[256,16]{1,0:T(8,128)}, u32[]{:S(2)}) copy-start(f32[256,16]{1,0:T(8,128)} %get-tuple-element.49.refs_12_) | copy-start | bytes 49156
  29.9 26.9 %copy-start.13 = (f32[8,128]{1,0:T(8,128)S(1)}, f32[8,128]{1,0:T(8,128)}, u32[]{:S(2)}) copy-start(f32[8,128]{1,0:T(8,128)} %refs_5_.3) | copy-start | bytes 12292
  29.9 26.9 %copy-start.14 = (s32[8,128]{1,0:T(8,128)S(1)}, s32[8,128]{1,0:T(8,128)}, u32[]{:S(2)}) copy-start(s32[8,128]{1,0:T(8,128)} %refs_6_.3) | copy-start | bytes 12292
  29.9 26.9 %copy-start.15 = (f32[8,128]{1,0:T(8,128)S(1)}, f32[8,128]{1,0:T(8,128)}, u32[]{:S(2)}) copy-start(f32[8,128]{1,0:T(8,128)} %refs_7_.3) | copy-start | bytes 12292
  34.8 22.0 %copy-start = (f32[8,16,3,128]{3,1,2,0:T(8,128)S(1)}, f32[8,16,3,128]{3,1,2,0:T(8,128)}, u32[]{:S(2)}) copy-start(f32[8,16,3,128]{3,1,2,0:T(8,128)} %param.21) | copy-start | bytes 589828
  34.8 22.0 %copy-start.1 = (f32[256,16]{1,0:T(8,128)S(1)}, f32[256,16]{1,0:T(8,128)}, u32[]{:S(2)}) copy-start(f32[256,16]{1,0:T(8,128)} %get-tuple-element.47.refs_10_) | copy-start | bytes 49156
  38.5 18.3 %copy-start.5 = (f32[8,3,128]{2,0,1:T(8,128)S(1)}, f32[8,3,128]{2,0,1:T(8,128)}, u32[]{:S(2)}) copy-start(f32[8,3,128]{2,0,1:T(8,128)} %param.24) | copy-start | bytes 36868
  59.8 22.0 %all-to-all-start.2 = ((f32[32,16,128]{2,1,0:T(8,128)}), f32[32,16,128]{2,1,0:T(8,128)S(1)}, u32[]{:S(2)}, u32[]{:S(2)}) async-start(f32[32,16,128]{2,1,0:T(8,128)} %get-tuple-element.53), calls=%async_computation.2 | async-start | bytes 524288 | tf_op jit(solution)/shard_map/all_to_all | solution.py:519
  67.5 8.7 %collective-permute-start.2 = (f32[6,8,128]{2,1,0:T(8,128)S(1)}, f32[6,8,128]{2,1,0:T(8,128)S(1)}, u32[]{:S(2)}, u32[]{:S(2)}) collective-permute-start(f32[6,8,128]{2,1,0:T(8,128)S(1)} %get-tuple-element.51), channel_id=1, source_target_pairs={{0,16},{16,32},{32,48},{48,64},{64,80},{80,96},{96,112},{112,128},... | collective-permute-start | bytes 73736 | tf_op jit(solution)/shard_map/ppermute | solution.py:406
  70.8 6.1 %collective-permute-start.3 = (f32[6,8,128]{2,1,0:T(8,128)S(1)}, f32[6,8,128]{2,1,0:T(8,128)S(1)}, u32[]{:S(2)}, u32[]{:S(2)}) collective-permute-start(f32[6,8,128]{2,1,0:T(8,128)S(1)} %get-tuple-element.52), channel_id=1, source_target_pairs={{0,496},{16,0},{32,16},{48,32},{64,48},{80,64},{96,80},{112,96},{1... | collective-permute-start | bytes 73736 | tf_op jit(solution)/shard_map/ppermute | solution.py:406
  122.8 1.3 %collective-permute-start.5 = (f32[8,128]{1,0:T(8,128)S(1)}, f32[8,128]{1,0:T(8,128)S(1)}, u32[]{:S(2)}, u32[]{:S(2)}) collective-permute-start(f32[8,128]{1,0:T(8,128)S(1)} %get-tuple-element.69), channel_id=1, source_target_pairs={{0,15},{1,0},{2,1},{3,2},{4,3},{5,4},{6,5},{7,6},{8,7},{9,8},{10,9... | collective-permute-start | bytes 12296 | tf_op jit(solution)/shard_map/ppermute | solution.py:406
  122.8 4.3 %collective-permute-start.4 = (f32[8,128]{1,0:T(8,128)S(1)}, f32[8,128]{1,0:T(8,128)S(1)}, u32[]{:S(2)}, u32[]{:S(2)}) collective-permute-start(f32[8,128]{1,0:T(8,128)S(1)} %get-tuple-element.69), channel_id=1, source_target_pairs={{0,1},{1,2},{2,3},{3,4},{4,5},{5,6},{6,7},{7,8},{8,9},{9,10},{10,1... | collective-permute-start | bytes 12296 | tf_op jit(solution)/shard_map/ppermute | solution.py:406
  (5 other events, 3.5 us)

commit v3 on v2

v3 whole, which is shorter than its diff:
```python
import jax
import jax.numpy as jnp
from jax import lax
from jax.experimental import pallas as pl
from jax.experimental.pallas import tpu as pltpu
from jax.sharding import PartitionSpec as P

HI = lax.Precision.HIGHEST
F32 = jnp.float32
BF16 = jnp.bfloat16
SCALE = 0.04
SOFT = 0.25
LV = 9
RK = 16
GX_BITS = 5
HALO = 10

NN = (((1,), (0,)), ((), ()))
NT = (((1,), (1,)), ((), ()))
TN = (((0,), (0,)), ((), ()))


def dot(a, b, dims=NN, precision=HI):
    return lax.dot_general(a, b, dims, precision=precision, preferred_element_type=F32)


def iota(shape, dim):
    return lax.broadcasted_iota(jnp.int32, shape, dim)


def thirds(x):
    hi = x.astype(BF16)
    rest = x - hi.astype(F32)
    mid = rest.astype(BF16)
    low = (rest - mid.astype(F32)).astype(BF16)
    return jnp.concatenate([hi, mid, low], axis=0)


def split_lanes(x):
    hi = x.astype(BF16)
    rest = x - hi.astype(F32)
    mid = rest.astype(BF16)
    low = (rest - mid.astype(F32)).astype(BF16)
    return jnp.concatenate([hi, mid, low], axis=1)


def call(kernel, outs, args, scratch=(), smem=0, far=0, ends=(), flops=0, room=32):
    specs = [pl.BlockSpec(memory_space=pltpu.SMEM)] * smem
    specs += [pl.BlockSpec(memory_space=pl.ANY)] * far
    specs += [pl.BlockSpec(memory_space=pltpu.VMEM)] * (len(args) - smem - far)
    for at in ends:
        specs[at] = pl.BlockSpec((args[at].shape[0], 128), lambda i: (0, 7))
    return pl.pallas_call(
        kernel,
        out_shape=[jax.ShapeDtypeStruct(s, d) for s, d in outs],
        grid=(1,) if ends else (),
        in_specs=specs,
        out_specs=[pl.BlockSpec(memory_space=pltpu.VMEM)] * len(outs),
        scratch_shapes=list(scratch),
        compiler_params=pltpu.CompilerParams(vmem_limit_bytes=room * 1024 * 1024),
        cost_estimate=pl.CostEstimate(flops=flops, bytes_accessed=1 << 20, transcendentals=0),
    )(*args)


def setup_kernel(
    transfer,
    coupling,
    transfer_end,
    coupling_end,
    slip,
    basis,
    g_out,
    h_out,
    sent,
    held,
    sems,
):
    flat = lax.axis_index("gy") * lax.axis_size("gx") + lax.axis_index("gx")
    blocks = [pl.multiple_of(flat // 128 * 128, 128), pl.multiple_of(512 + flat // 256 * 128, 128)]
    blocks += [768, 896]
    copies = []
    for t, table in enumerate((transfer, coupling)):
        for b, start in enumerate(blocks[:3]):
            copies.append(
                pltpu.make_async_copy(
                    table.at[:, pl.ds(start, 128)], held.at[t, b], sems.at[t * 3 + b]
                )
            )
            copies[-1].start()
    total = jnp.zeros((RK, 128), F32)
    for c in range(8):
        for i in range(3):
            total += basis[c, i] * slip[i, c : c + 1, :]
    moment = dot(jnp.ones((8, 128), F32), total, NT)

    shape = (128, 256)
    level = iota(shape, 1) // RK
    first = 1024 - jnp.right_shift(jnp.full(shape, 1024, jnp.int32), level)
    wanted = first + jnp.right_shift(jnp.zeros(shape, jnp.int32) + flat, level)
    far_half = 1016 + 2 * jnp.bitwise_xor(flat // 256, 1) - LV
    wanted = jnp.where(level < LV, wanted, far_half + level)
    picks = []
    for b, start in enumerate(blocks):
        used = (level == b) if b < 3 else (level >= 3) & (level < LV + 2)
        pick = jnp.where((iota(shape, 0) + start == wanted) & used, 1.0, 0.0).astype(BF16)
        picks += [pick, pick, pick]
    picks = jnp.concatenate(picks, axis=0)
    mine = (iota((256, 256), 1) % RK) == (iota((256, 256), 0) // RK)
    inside = iota((256, 128), 1) < transfer.shape[1] - 896
    for copy in copies:
        copy.wait()

    def path_matrices(t, end):
        parts = [split_lanes(held[t, b]) for b in range(3)]
        parts.append(split_lanes(jnp.where(inside, end[...], 0.0)))
        spread = dot(jnp.concatenate(parts, axis=1), picks, NN, None)
        return jnp.sum(jnp.where(mine, spread, 0.0).reshape(RK, RK, 256), axis=0)

    lifts = path_matrices(0, transfer_end)
    across = path_matrices(1, coupling_end)
    chain = [lifts[:, l * RK : (l + 1) * RK] for l in range(LV - 1)]
    for apart in (1, 2, 4):
        chain = [
            chain[l] if l < apart else dot(chain[l], chain[l - apart]) for l in range(LV - 1)
        ]
    eye = jnp.where(iota((RK, RK), 0) == iota((RK, RK), 1), 1.0, 0.0).astype(F32)
    chain = [eye] + chain
    g_out[...] = jnp.zeros(g_out.shape, F32)
    h_out[...] = jnp.zeros(h_out.shape, F32)
    for l in range(LV):
        g_out[l * RK : (l + 1) * RK, :] = chain[l]
        h_out[l * RK : (l + 1) * RK, :] = dot(across[:, l * RK : (l + 1) * RK], chain[l])
    top = h_out[8 * RK : 9 * RK, :]
    for side in range(2):
        at = 256 + 128 * side + 7 * RK
        lane = (LV + side) * RK
        h_out[at : at + RK, :] = dot(lifts[:, lane : lane + RK], top, TN)
    low = dot(moment, g_out[0:128, :], NT)
    for p in range(sent.shape[0] // 8):
        sent[8 * p : 8 * p + 8, :] = low


def project(basis_ref, slip_rows, g_ref):
    total = jnp.zeros((RK, 128), F32)
    for c in range(8):
        for i in range(3):
            total += basis_ref[c, i] * slip_rows(i, c)
    moment = dot(jnp.ones((8, 128), F32), total, NT)
    return dot(moment, g_ref[0:128, :], NT), dot(moment, g_ref[128:256, :], NT)


def cells_kernel(row_in, col_in, weight, pick_out, weight_out):
    for c in range(8):
        lanes = slice(c * 128, (c + 1) * 128)
        row = row_in[c : c + 1, :]
        col = col_in[c : c + 1, :]
        pick_out[:, lanes] = jnp.where(iota((128, 128), 0) == col, 1.0, 0.0).astype(BF16)
        at = iota((24, 128), 0)
        for side in range(2):
            weight_out[side * 24 : side * 24 + 24, lanes] = jnp.where(
                at == row, weight[2 * side, c : c + 1, :], 0.0
            ) + jnp.where(at == row + 1, weight[2 * side + 1, c : c + 1, :], 0.0)


def near_kernel(
    counts,
    slots,
    own_points,
    low_points,
    high_points,
    own,
    low,
    high,
    near_out,
    points,
    slips,
    target,
    total,
):
    ones = jnp.ones((384, 128), BF16)
    diagonal = iota((128, 128), 0) == iota((128, 128), 1)
    for b, (p, s) in enumerate(((low_points, low), (own_points, own), (high_points, high))):
        for i in range(3):
            points[b, i] = p[i]
            slips[b, i] = s[i]
    for c in range(8):
        for i in range(3):
            wide = jnp.where(diagonal, own_points[i, c : c + 1, :], 0.0)
            target[c, i] = dot(split_lanes(wide), ones, NN, None)
    total[...] = jnp.zeros(total.shape, F32)

    def one_target(c, _):
        def one_source(k, _):
            slot = slots[c, k]
            block = slot // 8
            row = pl.ds(slot % 8, 1)
            y = [points[block, i, row, :] for i in range(3)]
            s = [slips[block, i, row, :] for i in range(3)]
            for part in range(8):
                rows = slice(part * 16, part * 16 + 16)
                r = [target[c, i, rows, :] - y[i] for i in range(3)]
                inverse = lax.rsqrt(r[0] * r[0] + r[1] * r[1] + r[2] * r[2] + SOFT)
                along = (r[0] * s[0] + r[1] * s[1] + r[2] * s[2]) * (inverse * inverse)
                for i in range(3):
                    total[c, i, rows, :] += inverse * (s[i] + along * r[i])
            return 0

        return lax.fori_loop(0, counts[c], one_source, 0)

    lax.fori_loop(0, 8, one_target, 0)
    for c in range(8):
        for i in range(3):
            summed = dot(split_lanes(total[c, i]), ones, NN, None)
            near_out[i, c : c + 1, :] = SCALE * jnp.sum(
                jnp.where(diagonal, summed, 0.0), axis=0, keepdims=True
            )


def pick_edges(window):
    row, lane = iota((8, 128), 0), iota((8, 128), 1)
    wanted = jnp.where(row < 2, row, row + 124)
    pick = jnp.where((lane == wanted) & (row < 4), 1.0, 0.0).astype(F32)
    return dot(pick, window, NT)


def sum_over_row(received, at, first):
    j = lax.axis_index("gx")
    row, lane = iota((8, 128), 0), iota((8, 128), 1)
    level = lane // RK + jnp.where(row == first + 1, 8, 0)
    own = jnp.right_shift(jnp.zeros((8, 128), jnp.int32) + j, level)
    total = jnp.zeros((8, 128), F32)
    for p in range(received.shape[0]):
        theirs = jnp.right_shift(jnp.full((8, 128), p, jnp.int32), level)
        used = (level >= GX_BITS) | (theirs == jnp.bitwise_xor(own, 1))
        total += jnp.where(used, received[p, at : at + 8, :], 0.0)
    return total


def copies_of(tile, sent):
    for p in range(sent.shape[0]):
        sent[p] = tile[...]


def between_kernel(
    received,
    low,
    high,
    first_low,
    first_high,
    loaded,
    pressure,
    mobility,
    window,
    mobility_out,
    tile_out,
    sent,
):
    j = lax.axis_index("gx")
    peers = received.shape[0]
    before = lax.rem(j - 2 + peers, peers)
    after = lax.rem(j + 2, peers)
    for out, own, at in ((window, pressure, 6), (mobility_out, mobility, 7)):
        out[...] = jnp.zeros(out.shape, F32)
        out[2:10, :] = first_low[at]
        out[10:18, :] = own[...]
        out[18:26, :] = first_high[at]
    mobility_out[1:2, :] = received[before, 12:13, :]
    mobility_out[26:27, :] = received[after, 12:13, :]
    window[2:26, :] += loaded[...]
    for i, at, size in ((3, 0, 8), (4, 8, 8), (5, 16, 2)):
        window[at : at + size, :] += low[i, 0:size, :]
        window[at + 10 : at + 10 + size, :] += high[i, 0:size, :]
    window[18:28, :] += received[after, 0:10, :]
    window[0:10, :] += received[before, 0:10, :]
    window[26:28, :] += received[lax.rem(j + 3, peers), 0:2, :]
    window[0:2, :] += received[lax.rem(j - 3 + peers, peers), 8:10, :]
    sums = sum_over_row(received, 8, 2)
    tile_out[...] = jnp.zeros(tile_out.shape, F32)
    edges = pick_edges(window[...])
    tile_out[0:4, 0:32] = edges[0:4]
    tile_out[4:6, :] = sums[2:4]
    edges = pick_edges(mobility_out[...])
    tile_out[6:7, 0:32] = edges[0:1]
    tile_out[7:8, 0:32] = edges[3:4]
    copies_of(tile_out, sent)


def last_kernel(received, loaded, pressure, window, tile_out):
    j = lax.axis_index("gx")
    peers = received.shape[0]
    window[...] = pressure[...]
    window[2:26, :] += loaded[...]
    window[10:20, :] += received[lax.rem(j + 1, peers), 0:10, :]
    window[8:18, :] += received[lax.rem(j - 1 + peers, peers), 0:10, :]
    window[18:20, :] += received[lax.rem(j + 2, peers), 0:2, :]
    window[8:10, :] += received[lax.rem(j - 2 + peers, peers), 8:10, :]
    tile_out[...] = jnp.zeros(tile_out.shape, F32)
    tile_out[0:4, 0:32] = pick_edges(window[...])[0:4]


def beside(left, right):
    g = lax.axis_index("gy")
    row, lane = iota((8, 128), 0), iota((8, 128), 1)
    from_right = (row < 2) | (row == 6)
    inside = (from_right & (g < lax.axis_size("gy") - 1)) | (~from_right & (g > 0))
    edges = jnp.where(inside, jnp.where(from_right, right, left), 0.0)[:, 0:32]
    wanted = jnp.where(row < 2, row, row + 124)
    pick = jnp.where((lane == wanted) & (row < 4), 1.0, 0.0).astype(F32)
    wanted = jnp.where(row == 6, 0, 127)
    pick_mobility = jnp.where((lane == wanted) & (row > 5), 1.0, 0.0).astype(F32)
    return dot(edges, pick, TN), dot(edges, pick_mobility, TN)


def flow(window, window_side, mobility, mobility_side):
    j = lax.axis_index("gx")
    p = jnp.concatenate([window, window_side], axis=1)
    m = jnp.concatenate([mobility, mobility_side], axis=1)
    rows = 8 * lax.axis_size("gx")
    row = lax.rem(iota((32, 256), 0) + (j * 8 - HALO + rows), jnp.full((32, 256), 0, jnp.int32) + rows)
    for step in range(2):
        up = jnp.where(row == 0, 0.0, pltpu.roll(p, 1, 0))
        down = jnp.where(row == rows - 1, 0.0, pltpu.roll(p, 31, 0))
        sides = pltpu.roll(p, 1, 1) + pltpu.roll(p, 255, 1)
        p = p + m * (up + down + sides - 4.0 * p)
    return p[:, 0:128]


def incoming_of_row(received, tile, h):
    g = lax.axis_index("gy")
    row, lane = iota((8, 128), 0), iota((8, 128), 1)
    level = lane // RK + jnp.where(row == 5, 8, 0)
    bit = jnp.maximum(level - GX_BITS, 0)
    own = jnp.right_shift(jnp.zeros((8, 128), jnp.int32) + g, bit)
    total = jnp.where((level < GX_BITS) & (row == 4), tile[...], 0.0)
    within = (level >= GX_BITS) & (level < LV) & ((row == 4) | (row == 5))
    for p in range(received.shape[0]):
        theirs = jnp.right_shift(jnp.full((8, 128), p, jnp.int32), bit)
        total += jnp.where(within & (theirs == jnp.bitwise_xor(own, 1)), received[p], 0.0)
    parts = jnp.where(iota((8, RK), 0) == 4, dot(total, h[0:128, :]), 0.0)
    return parts + jnp.where(iota((8, RK), 0) == 5, dot(total, h[128:256, :]), 0.0)


def incoming_of_all(received, h):
    ny = lax.axis_size("gy")
    flat = lax.axis_index("gy") * lax.axis_size("gx") + lax.axis_index("gx")
    row, level = iota((8, 128), 0), iota((8, 128), 1) // RK
    sibling = jnp.bitwise_xor(jnp.right_shift(jnp.zeros((8, 128), jnp.int32) + flat, level), 1)
    half = jnp.bitwise_xor(flat // 256, 1)
    sums = [jnp.zeros((8, 128), F32) for _ in range(3)]
    for at in range(0, received.shape[0], 8):
        theirs = received[at : at + 8, :]
        node = (at % ny + row) * lax.axis_size("gx") + at // ny
        upper = jnp.right_shift(node, 7)
        sums[0] += jnp.where(jnp.right_shift(node, level) == sibling, theirs, 0.0)
        sums[1] += jnp.where(upper == 2 * half, theirs, 0.0)
        sums[2] += jnp.where(upper == 2 * half + 1, theirs, 0.0)
    parts = dot(sums[0], h[0:128, :]) + dot(sums[1], h[256:384, :])
    return parts + dot(sums[2], h[384:512, :])


def update(parts, cells, near, refs, slip_out, loaded_out):
    (slip, prestress, basis, normal, friction, compliance, state, dilation, pick, weight) = refs
    incoming = dot(parts, jnp.ones((8, 128), F32), TN)

    both = jnp.concatenate([cells, pltpu.roll(cells, 127, 1)], axis=0)
    split = thirds(both)
    found = dot(split, pick[...], NN, None)
    found = (found[0:48] + found[48:96] + found[96:144]) * weight[...]
    at_row = jnp.sum(found, axis=0, keepdims=True)

    for c in range(8):
        for i in range(3):
            far = jnp.sum(basis[c, i] * incoming, axis=0, keepdims=True)
            slip_out[i, c : c + 1, :] = far
    at_elements = jnp.concatenate([at_row[:, c * 128 : (c + 1) * 128] for c in range(8)], axis=0)
    stress = [prestress[i] - (near[i] + slip_out[i]) for i in range(3)]
    effective = normal[...] - at_elements
    magnitude = jnp.sqrt(stress[0] * stress[0] + stress[1] * stress[1] + stress[2] * stress[2] + 1.0)
    factor = jnp.maximum(1.0 - friction[...] * effective / magnitude, 0.0)
    scaled = state[...].astype(F32) * compliance[...] * factor
    steps = [scaled * stress[i] for i in range(3)]
    for i in range(3):
        slip_out[i] = slip[i] + steps[i]
    dilated = dilation[...] * (steps[0] * steps[0] + steps[1] * steps[1] + steps[2] * steps[2])
    dilated_row = jnp.concatenate([dilated[c : c + 1, :] for c in range(8)], axis=1)
    spread = dot(thirds(weight[...] * dilated_row), pick[...], NT, None)
    spread = spread[0:48] + spread[48:96] + spread[96:144]
    loaded_out[...] = spread[0:24] + pltpu.roll(spread[24:48], 1, 1)


def send_sources(ahead, behind, sent):
    j = lax.axis_index("gx")
    peers = sent.shape[0]
    for p in range(peers):
        back = lax.rem(j - p + peers, peers) < peers // 2
        sent[p] = jnp.where(back, ahead[...], behind[...])


def first_update_kernel(received, low, high, pressure, mobility, lifts, h, near, *refs):
    refs, outs = refs[:10], refs[10:]
    slip_out, loaded, down_out, up_out, sent, ahead, behind = outs
    cells = jnp.concatenate([low[6], pressure[...], high[6]], axis=0)
    update(incoming_of_all(received, h), cells, near, refs, slip_out, loaded)
    low_row, high_row = project(refs[2], lambda i, c: slip_out[i, c : c + 1, :], lifts)
    ahead[...] = jnp.zeros(ahead.shape, F32)
    behind[...] = jnp.zeros(behind.shape, F32)
    ahead[0:10, :] = loaded[0:10, :]
    behind[0:10, :] = loaded[14:24, :]
    ahead[8:10, :] += pressure[0:2, :]
    behind[0:2, :] += pressure[6:8, :]
    ahead[12:13, :] = mobility[0:1, :]
    behind[12:13, :] = mobility[7:8, :]
    for out in (ahead, behind):
        out[10:11, :] = low_row[0:1]
        out[11:12, :] = high_row[0:1]
    send_sources(ahead, behind, sent)
    for out, at in ((down_out, 0), (up_out, 6)):
        out[0:3] = slip_out[...]
        out[3] = loaded[at : at + 8, :]
        out[4] = loaded[at + 8 : at + 16, :]
        out[5] = jnp.zeros((8, 128), F32)
        out[5, 0:2, :] = loaded[at + 16 : at + 18, :]


def second_update_kernel(received, tile, window, mobility, h, near, *refs):
    refs, outs = refs[:10], refs[10:]
    slip_out, loaded, window_out, side_out, sent, ahead, behind = outs
    g = lax.axis_index("gy")
    left = received[jnp.maximum(g - 1, 0)]
    right = received[jnp.minimum(g + 1, received.shape[0] - 1)]
    side, mobility_side = beside(left, right)
    side_out[...] = mobility_side
    window_out[...] = flow(window[...], side, mobility[...], mobility_side)
    parts = incoming_of_row(received, tile, h)
    update(parts, window_out[2:26, :], near, refs, slip_out, loaded)
    ahead[...] = jnp.zeros(ahead.shape, F32)
    behind[...] = jnp.zeros(behind.shape, F32)
    ahead[0:10, :] = loaded[0:10, :]
    behind[0:10, :] = loaded[14:24, :]
    send_sources(ahead, behind, sent)


def final_kernel(window, left, right, mobility, mobility_side, out):
    side, _ = beside(left[...], right[...])
    done = flow(window[...], side, mobility[...], mobility_side[...])
    out[...] = done[HALO : HALO + 8, :]


def shift(x, axis, steps):
    n = lax.axis_size(axis)
    return lax.ppermute(x, axis, [(i, (i + steps) % n) for i in range(n)])


def shards(
    slip_field,
    positions,
    neighbours,
    near_counts,
    cluster_basis,
    transfer,
    coupling,
    prestress,
    normal_stress,
    friction,
    compliance,
    slip_state,
    cell_index,
    cell_weight,
    dilation,
    pressure,
    mobility,
):
    nx, ny = lax.axis_size("gx"), lax.axis_size("gy")
    j, g = lax.axis_index("gx"), lax.axis_index("gy")
    rows = 8 * nx
    slip = slip_field.transpose(1, 0, 2)
    points = positions.transpose(1, 0, 2)
    strained = prestress.transpose(1, 0, 2)
    basis = cluster_basis.transpose(0, 2, 1, 3)
    lift_table = transfer.transpose(1, 2, 0).reshape(RK * RK, -1)
    cross_table = coupling.transpose(1, 2, 0).reshape(RK * RK, -1)
    slots = (neighbours - j * 8 + 8 + rows) % rows

    g_mat, h_mat, sent = call(
        setup_kernel,
        [((256, RK), F32), ((512, RK), F32), ((nx * ny, 128), F32)],
        [lift_table, cross_table, lift_table, cross_table, slip, basis],
        scratch=[pltpu.VMEM((2, 3, 256, 128), F32), pltpu.SemaphoreType.DMA((6,))],
        far=2,
        ends=(2, 3),
        room=60,
    )
    both = jnp.concatenate([slip, points, pressure[None], mobility[None]], axis=0)
    sent, cell_index, cell_weight = lax.optimization_barrier((sent, cell_index, cell_weight))
    first_cell = cell_index[:, 0, :]
    cell_row = (first_cell // 128 - j * 8 + 8 + rows) % rows
    cell_col = first_cell % 128
    weights = cell_weight.transpose(1, 0, 2)
    received = lax.all_to_all(
        sent.reshape(nx * ny, 1, 128), ("gx", "gy"), 0, 0, tiled=True
    ).reshape(nx * ny, 128)
    pick, weight = call(
        cells_kernel,
        [((128, 1024), BF16), ((48, 1024), F32)],
        [cell_row, cell_col, weights],
        flops=1 << 28,
    )
    both, pick = lax.optimization_barrier((both, pick))
    first_low = shift(both, "gx", 1)
    first_high = shift(both, "gx", -1)
    low_points, high_points = first_low[3:6], first_high[3:6]

    def near_field(slip, low, high):
        return call(
            near_kernel,
            [((3, 8, 128), F32)],
            [near_counts, slots, points, low_points, high_points, slip, low, high],
            scratch=[
                pltpu.VMEM((3, 3, 8, 128), F32),
                pltpu.VMEM((3, 3, 8, 128), F32),
                pltpu.VMEM((8, 3, 128, 128), F32),
                pltpu.VMEM((8, 3, 128, 128), F32),
            ],
            smem=2,
            flops=1 << 28,
        )[0]

    pieces = [pltpu.VMEM((16, 128), F32), pltpu.VMEM((16, 128), F32)]
    common = [strained, basis, normal_stress, friction, compliance, slip_state, dilation]
    common += [pick, weight]
    near = near_field(slip, first_low, first_high)
    slip, loaded, down, up, sent = call(
        first_update_kernel,
        [
            ((3, 8, 128), F32),
            ((24, 128), F32),
            ((6, 8, 128), F32),
            ((6, 8, 128), F32),
            ((nx, 16, 128), F32),
        ],
        [received, first_low, first_high, pressure, mobility, g_mat, h_mat, near, slip, *common],
        scratch=pieces,
    )
    received = lax.all_to_all(sent, "gx", 0, 0, tiled=True)
    low = shift(up, "gx", 1)
    high = shift(down, "gx", -1)
    window, mobility_window, tile, sent = call(
        between_kernel,
        [((32, 128), F32), ((32, 128), F32), ((8, 128), F32), ((ny, 8, 128), F32)],
        [received, low, high, first_low, first_high, loaded, pressure, mobility],
    )
    received = lax.all_to_all(sent, "gy", 0, 0, tiled=True)
    near_slip, sent = lax.optimization_barrier((slip, sent))
    near = near_field(near_slip, low, high)
    slip, loaded, window, mobility_side, sent = call(
        second_update_kernel,
        [
            ((3, 8, 128), F32),
            ((24, 128), F32),
            ((32, 128), F32),
            ((32, 128), F32),
            ((nx, 16, 128), F32),
        ],
        [received, tile, window, mobility_window, h_mat, near, slip, *common],
        scratch=pieces,
    )
    received = lax.all_to_all(sent, "gx", 0, 0, tiled=True)
    window, tile = call(
        last_kernel,
        [((32, 128), F32), ((8, 128), F32)],
        [received, loaded, window],
    )
    left = shift(tile, "gy", 1)
    right = shift(tile, "gy", -1)
    (final_pressure,) = call(
        final_kernel,
        [((8, 128), F32)],
        [window, left, right, mobility_window, mobility_side],
    )
    return (slip.transpose(1, 0, 2), final_pressure)


def solution(mesh):
    split = ("gy", "gx")
    in_specs = (
        P(split, None, None),
        P(split, None, None),
        P(split, None),
        P(split),
        P(split, None, None, None),
        P(),
        P(),
        P(split, None, None),
        P(split, None),
        P(split, None),
        P(split, None),
        P(split, None),
        P(split, None, None),
        P(split, None, None),
        P(split, None),
        P("gx", "gy"),
        P("gx", "gy"),
    )
    out_specs = (P(split, None, None), P("gx", "gy"))
    return jax.shard_map(shards, mesh=mesh, in_specs=in_specs, out_specs=out_specs, check_vma=False)
```

time: 129 us -> 117 us (0.907)
  blocking collectives: 55.6 us -> 22.6 us
  starting transfers between devices: 34 us -> 54.1 us
  waiting for transfers between devices: 7.51 us -> 18 us
  Pallas kernels: 24 us -> 18.5 us
  local copies, waits for them, and re-layouts: 6.54 us -> 2.06 us
    all_to_all x0 -> x2, starting transfers between devices: none -> 30.6 us  [the longest x1 21.1 us: shards(): lax.all_to_all(sent.reshape(nx * ny, 1, 128), ('gx', 'gy'), 0, 0, tiled=T...]
    all_to_all x2 -> x0, blocking collectives: 29.4 us -> none  [shards(): received = lax.all_to_all(sent, 'gy', 0, 0, tiled=True)]
    all_to_all x2 -> x1, starting transfers between devices: 19 us -> 8.46 us  [shards(): received = lax.all_to_all(sent, 'gx', 0, 0, tiled=True)]
    ppermute x6, waiting for transfers between devices: 4.48 us -> 11.2 us  [shift(): return lax.ppermute(x, axis, [(i, (i + steps) % n) for i in range(n)])]
    pallas_call x11 -> x9, Pallas kernels: 24 us -> 18.5 us  [call(): pl.pallas_call(kernel, out_shape=[jax.ShapeDtypeStruct(s, d) for s, d in...]
    all_to_all x0 -> x2, waiting for transfers between devices: none -> 3.9 us  [the longest x1 3.9 us: shards(): received = lax.all_to_all(sent, 'gy', 0, 0, tiled=True)]
    all_to_all x1, blocking collectives: 26.2 us -> 22.6 us  [shards(): received = lax.all_to_all(sent, 'gx', 0, 0, tiled=True)]
    slice x6 -> x2, local copies, waits for them, and re-layouts: 2.51 us -> 0.01 us  [shards(): low_points, high_points = (first_low[3:6], first_high[3:6])]
  transfers between devices with their start and end apart: 8 -> 9, of which waited for: 4 -> 7; matrix products, arithmetic and copies ran while one was open for 0% -> 0% of each run, Pallas kernels for 8% -> 7%
where the time goes in v3:
time: 117 us; the launch traced here: 116 us
  starting transfers between devices  54.1 us (46%)
  blocking collectives  22.6 us (19%)
  Pallas kernels  18.5 us (16%)
  waiting for transfers between devices  18 us (15%)
  local copies, waits for them, and re-layouts  2.06 us (2%)
    all_to_all x1, blocking collectives, shards(): received = lax.all_to_all(sent, 'gx', 0, 0, tiled=True)  22.6 us
    all_to_all x1, starting transfers between devices, shards(): lax.all_to_all(sent.reshape(nx * ny, 1, 128), ('gx', 'gy'), 0, 0, tiled=T...  21.1 us
    pallas_call x9, Pallas kernels, call(): pl.pallas_call(kernel, out_shape=[jax.ShapeDtypeStruct(s, d) for s, d in...  18.5 us
    ppermute x6, starting transfers between devices, shift(): return lax.ppermute(x, axis, [(i, (i + steps) % n) for i in range(n)])  15.1 us
    ppermute x6, waiting for transfers between devices, shift(): return lax.ppermute(x, axis, [(i, (i + steps) % n) for i in range(n)])  11.2 us
    all_to_all x1, starting transfers between devices, shards(): received = lax.all_to_all(sent, 'gy', 0, 0, tiled=True)  9.47 us
    all_to_all x1, starting transfers between devices, shards(): received = lax.all_to_all(sent, 'gx', 0, 0, tiled=True)  8.46 us
    all_to_all x1, waiting for transfers between devices, shards(): received = lax.all_to_all(sent, 'gy', 0, 0, tiled=True)  3.9 us
  transfers between devices with their start and end apart: 9, of which 7 were waited for; matrix products, arithmetic and copies ran while one was open for 0% of the time, Pallas kernels for 7%

profile of v3, /device:TPU:8, one launch (start us, length us, event | category | flops | bytes accessed | tf_op | source)
XLA Modules:
  0.0 116.3 jit_solution(5718718660220969413)
XLA Ops:
  0.6 4.8 %shard_map.176 = (f32[256,16]{1,0:T(8,128)}, f32[512,16]{1,0:T(8,128)}, f32[512,128]{1,0:T(8,128)}) custom-call(f32[256,1022]{1,0:T(8,128)} %bitcast.57, f32[256,1022]{1,0:T(8,128)} %bitcast.59, f32[256,1022]{1,0:T(8,128)} %bitcast.58, f32[256,1022]{1,0:T(8,128)} %bitcast.60, f32[3,8,128]{2,1,0:T(8,128)} %bitcast.45, f32[8,3,16,128]{3,2,1,0:T(8,128)} %bitcast.41), custom_call_target="tpu_custom_call" | custom-call | bytes 1048576 | tf_op jit(solution)/shard_map/pallas_call | solution.py:53
  5.4 21.1 %all-to-all-start = ((f32[512,1,128]{2,1,0:T(1,128)}), f32[512,1,128]{2,1,0:T(1,128)S(1)}, u32[]{:S(2)}, u32[]{:S(2)}) async-start(f32[512,1,128]{2,1,0:T(1,128)} %bitcast.61), calls=%async_computation | async-start | bytes 524288 | tf_op jit(solution)/shard_map/all_to_all | solution.py:499
  26.6 0.7 copy-done.15
  27.4 0.6 copy-done.3
  28.1 4.7 %collective-permute-start.1 = (f32[8,8,128]{2,1,0:T(8,128)S(1)}, f32[8,8,128]{2,1,0:T(8,128)S(1)}, u32[]{:S(2)}, u32[]{:S(2)}) collective-permute-start(f32[8,8,128]{2,1,0:T(8,128)S(1)} %pad_maximum_fusion), channel_id=1, source_target_pairs={{0,496},{16,0},{32,16},{48,32},{64,48},{80,64},{96,80},{112,96},{1... | collective-permute-start | bytes 98312 | tf_op jit(solution)/shard_map/ppermute | solution.py:451
  32.8 1.9 %collective-permute-start = (f32[8,8,128]{2,1,0:T(8,128)S(1)}, f32[8,8,128]{2,1,0:T(8,128)S(1)}, u32[]{:S(2)}, u32[]{:S(2)}) collective-permute-start(f32[8,8,128]{2,1,0:T(8,128)S(1)} %pad_maximum_fusion), channel_id=1, source_target_pairs={{0,16},{16,32},{32,48},{48,64},{64,80},{80,96},{96,112},{112,128},... | collective-permute-start | bytes 98312 | tf_op jit(solution)/shard_map/ppermute | solution.py:451
  34.8 6.0 %collective-permute-done.low.first_low = f32[8,8,128]{2,1,0:T(8,128)S(1)} collective-permute-done((f32[8,8,128]{2,1,0:T(8,128)S(1)}, f32[8,8,128]{2,1,0:T(8,128)S(1)}, u32[]{:S(2)}, u32[]{:S(2)}) %collective-permute-start) | collective-permute-done | bytes 32800 | tf_op jit(solution)/shard_map/ppermute | solution.py:451
  40.9 4.0 %shard_map.178.near = f32[3,8,128]{2,1,0:T(8,128)S(1)} custom-call(s32[8]{0:T(128)S(1)} %copy-done.13, s32[8,8]{1,0:T(8,128)S(1)} %add_select_fusion.slots, f32[3,8,128]{2,1,0:T(8,128)S(1)} %bitcast.55, f32[3,8,128]{2,1,0:T(8,128)S(1)} %slice.13.low_points, f32[3,8,128]{2,1,0:T(8,128)S(1)} %slice.14.high_points, f32[3,8,128]{2,1,0:T(8,128)S(1)} %bitcast.47, ...), custom_call_target="tpu_custom_call" | custom-call | flops 268435456 | bytes 1048576 | tf_op jit(solution)/shard_map/pallas_call | solution.py:53
  45.0 0.6 copy-done.8
  45.6 2.1 %shard_map.179 = (f32[3,8,128]{2,1,0:T(8,128)S(1)}, f32[24,128]{1,0:T(8,128)S(1)}, f32[6,8,128]{2,1,0:T(8,128)S(1)}, f32[6,8,128]{2,1,0:T(8,128)S(1)}, f32[32,16,128]{2,1,0:T(8,128)}) custom-call(f32[512,128]{1,0:T(8,128)S(1)} %bitcast.44, f32[8,8,128]{2,1,0:T(8,128)S(1)} %collective-permute-done.low.first_low, ...), custom_call_target="tpu_custom_call" | custom-call | bytes 1048576 | tf_op jit(solution)/shard_map/pallas_call | solution.py:53
  47.6 8.5 %all-to-all-start.1 = ((f32[32,16,128]{2,1,0:T(8,128)}), f32[32,16,128]{2,1,0:T(8,128)S(1)}, u32[]{:S(2)}, u32[]{:S(2)}) async-start(f32[32,16,128]{2,1,0:T(8,128)} %get-tuple-element.39), calls=%async_computation.1 | async-start | bytes 524288 | tf_op jit(solution)/shard_map/all_to_all | solution.py:544
  56.1 3.4 %collective-permute-start.2 = (f32[6,8,128]{2,1,0:T(8,128)S(1)}, f32[6,8,128]{2,1,0:T(8,128)S(1)}, u32[]{:S(2)}, u32[]{:S(2)}) collective-permute-start(f32[6,8,128]{2,1,0:T(8,128)S(1)} %get-tuple-element.40), channel_id=1, source_target_pairs={{0,16},{16,32},{32,48},{48,64},{64,80},{80,96},{96,112},{112,128},... | collective-permute-start | bytes 73736 | tf_op jit(solution)/shard_map/ppermute | solution.py:451
  59.5 4.6 %collective-permute-start.3 = (f32[6,8,128]{2,1,0:T(8,128)S(1)}, f32[6,8,128]{2,1,0:T(8,128)S(1)}, u32[]{:S(2)}, u32[]{:S(2)}) collective-permute-start(f32[6,8,128]{2,1,0:T(8,128)S(1)} %get-tuple-element.41), channel_id=1, source_target_pairs={{0,496},{16,0},{32,16},{48,32},{64,48},{80,64},{96,80},{112,96},{1... | collective-permute-start | bytes 73736 | tf_op jit(solution)/shard_map/ppermute | solution.py:451
  64.2 1.4 %collective-permute-done.3.high = f32[6,8,128]{2,1,0:T(8,128)S(1)} collective-permute-done((f32[6,8,128]{2,1,0:T(8,128)S(1)}, f32[6,8,128]{2,1,0:T(8,128)S(1)}, u32[]{:S(2)}, u32[]{:S(2)}) %collective-permute-start.3) | collective-permute-done | bytes 24608 | tf_op jit(solution)/shard_map/ppermute | solution.py:451
  65.6 2.9 %all-to-all-done.1.received = f32[32,16,128]{2,1,0:T(8,128)S(1)} async-done(((f32[32,16,128]{2,1,0:T(8,128)}), f32[32,16,128]{2,1,0:T(8,128)S(1)}, u32[]{:S(2)}, u32[]{:S(2)}) %all-to-all-start.1) | async-done | bytes 262176 | tf_op jit(solution)/shard_map/all_to_all | solution.py:544
  68.5 0.8 shard_map.180
  69.3 9.5 %all-to-all-start.2 = ((f32[16,8,128]{2,1,0:T(8,128)}), f32[16,8,128]{2,1,0:T(8,128)S(1)}, u32[]{:S(2)}, u32[]{:S(2)}) async-start(f32[16,8,128]{2,1,0:T(8,128)} %get-tuple-element.43), calls=%async_computation.2 | async-start | bytes 131072 | tf_op jit(solution)/shard_map/all_to_all | solution.py:552
  78.8 4.0 %shard_map.181.near = f32[3,8,128]{2,1,0:T(8,128)S(1)} custom-call(s32[8]{0:T(128)S(1)} %copy-done.13, s32[8,8]{1,0:T(8,128)S(1)} %add_select_fusion.slots, f32[3,8,128]{2,1,0:T(8,128)S(1)} %bitcast.56, f32[3,8,128]{2,1,0:T(8,128)S(1)} %slice.13.low_points, f32[3,8,128]{2,1,0:T(8,128)S(1)} %slice.14.high_points, ...), custom_call_target="tpu_custom_call" | custom-call | flops 268435456 | bytes 1048576 | tf_op jit(solution)/shard_map/pallas_call | solution.py:53
  82.8 3.9 %all-to-all-done.2.received = f32[16,8,128]{2,1,0:T(8,128)S(1)} async-done(((f32[16,8,128]{2,1,0:T(8,128)}), f32[16,8,128]{2,1,0:T(8,128)S(1)}, u32[]{:S(2)}, u32[]{:S(2)}) %all-to-all-start.2) | async-done | bytes 65568 | tf_op jit(solution)/shard_map/all_to_all | solution.py:552
  86.6 1.7 %shard_map.182 = (f32[3,8,128]{2,1,0:T(8,128)}, f32[24,128]{1,0:T(8,128)S(1)}, f32[32,128]{1,0:T(8,128)S(1)}, f32[32,128]{1,0:T(8,128)S(1)}, f32[32,16,128]{2,1,0:T(8,128)S(1)}) custom-call(f32[16,8,128]{2,1,0:T(8,128)S(1)} %all-to-all-done.2.received, f32[8,128]{1,0:T(8,128)S(1)} %get-tuple-element.44.tile, f32[32,128]{1,0:T(8,128)S(1)} %get-tuple-element.45.window, ...), custom_call_target="tpu_custom_call" | custom-call | bytes 1048576 | tf_op jit(solution)/shard_map/pallas_call | solution.py:53
  88.3 22.6 %all_to_all.20.received = f32[32,16,128]{2,1,0:T(8,128)S(1)} all-to-all(f32[32,16,128]{2,1,0:T(8,128)S(1)} %get-tuple-element.50), channel_id=1, replica_groups=mesh['gx'=32,'gy'=16] {'gx'}, dimensions={0} | all-to-all | bytes 524288 | tf_op jit(solution)/shard_map/all_to_all | solution.py:567
  111.6 0.8 collective-permute-done.5.right
  112.5 2.9 %collective-permute-done.4.left = f32[8,128]{1,0:T(8,128)S(1)} collective-permute-done((f32[8,128]{1,0:T(8,128)S(1)}, f32[8,128]{1,0:T(8,128)S(1)}, u32[]{:S(2)}, u32[]{:S(2)}) %collective-permute-start.4) | collective-permute-done | bytes 4128 | tf_op jit(solution)/shard_map/ppermute | solution.py:451
  115.4 1.0 shard_map.184
  (46 shorter events, 1.2 us)
Async XLA Ops:
  5.4 21.1 %copy-start.14 = (s32[8,4,128]{2,1,0:T(4,128)S(1)}, s32[8,4,128]{2,1,0:T(4,128)}, u32[]{:S(2)}) copy-start(s32[8,4,128]{2,1,0:T(4,128)} %param.29) | copy-start | bytes 49156
  5.4 39.4 %all-to-all-start = ((f32[512,1,128]{2,1,0:T(1,128)}), f32[512,1,128]{2,1,0:T(1,128)S(1)}, u32[]{:S(2)}, u32[]{:S(2)}) async-start(f32[512,1,128]{2,1,0:T(1,128)} %bitcast.61), calls=%async_computation | async-start | bytes 524288 | tf_op jit(solution)/shard_map/all_to_all | solution.py:499
  26.6 0.7 copy-start.15
  27.3 0.7 copy-start.3
  27.3 0.7 copy-start.6
  27.3 0.7 copy-start.12
  28.1 6.6 %copy-start.16 = (s32[8,8]{1,0:T(8,128)S(1)}, s32[8,8]{1,0:T(8,128)}, u32[]{:S(2)}) copy-start(s32[8,8]{1,0:T(8,128)} %param.19) | copy-start | bytes 772
  28.1 6.7 %collective-permute-start.1 = (f32[8,8,128]{2,1,0:T(8,128)S(1)}, f32[8,8,128]{2,1,0:T(8,128)S(1)}, u32[]{:S(2)}, u32[]{:S(2)}) collective-permute-start(f32[8,8,128]{2,1,0:T(8,128)S(1)} %pad_maximum_fusion), channel_id=1, source_target_pairs={{0,496},{16,0},{32,16},{48,32},{64,48},{80,64},{96,80},{112,96},{1... | collective-permute-start | bytes 98312 | tf_op jit(solution)/shard_map/ppermute | solution.py:451
  32.8 8.0 %collective-permute-start = (f32[8,8,128]{2,1,0:T(8,128)S(1)}, f32[8,8,128]{2,1,0:T(8,128)S(1)}, u32[]{:S(2)}, u32[]{:S(2)}) collective-permute-start(f32[8,8,128]{2,1,0:T(8,128)S(1)} %pad_maximum_fusion), channel_id=1, source_target_pairs={{0,16},{16,32},{32,48},{48,64},{64,80},{80,96},{96,112},{112,128},... | collective-permute-start | bytes 98312 | tf_op jit(solution)/shard_map/ppermute | solution.py:451
  34.8 6.0 %copy-start.13 = (s32[8]{0:T(128)S(1)}, s32[8]{0:T(128)}, u32[]{:S(2)}) copy-start(s32[8]{0:T(128)} %counts.3) | copy-start | bytes 100
  40.8 4.1 %copy-start = (f32[8,16,3,128]{3,1,2,0:T(8,128)S(1)}, f32[8,16,3,128]{3,1,2,0:T(8,128)}, u32[]{:S(2)}) copy-start(f32[8,16,3,128]{3,1,2,0:T(8,128)} %param.21) | copy-start | bytes 589828
  40.8 4.1 %copy-start.1 = (f32[512,16]{1,0:T(8,128)S(1)}, f32[512,16]{1,0:T(8,128)}, u32[]{:S(2)}) copy-start(f32[512,16]{1,0:T(8,128)} %get-tuple-element.36.h) | copy-start | bytes 98308
  40.8 4.1 %copy-start.2 = (f32[256,16]{1,0:T(8,128)S(1)}, f32[256,16]{1,0:T(8,128)}, u32[]{:S(2)}) copy-start(f32[256,16]{1,0:T(8,128)} %get-tuple-element.35.lifts) | copy-start | bytes 49156
  40.8 4.1 %copy-start.4 = (f32[8,3,128]{2,0,1:T(8,128)S(1)}, f32[8,3,128]{2,0,1:T(8,128)}, u32[]{:S(2)}) copy-start(f32[8,3,128]{2,0,1:T(8,128)} %param.24) | copy-start | bytes 36868
  40.8 4.1 %copy-start.9 = (f32[8,128]{1,0:T(8,128)S(1)}, f32[8,128]{1,0:T(8,128)}, u32[]{:S(2)}) copy-start(f32[8,128]{1,0:T(8,128)} %refs_5_.3) | copy-start | bytes 12292
  40.9 4.1 %copy-start.10 = (s32[8,128]{1,0:T(8,128)S(1)}, s32[8,128]{1,0:T(8,128)}, u32[]{:S(2)}) copy-start(s32[8,128]{1,0:T(8,128)} %refs_6_.3) | copy-start | bytes 12292
  40.9 4.1 %copy-start.11 = (f32[8,128]{1,0:T(8,128)S(1)}, f32[8,128]{1,0:T(8,128)}, u32[]{:S(2)}) copy-start(f32[8,128]{1,0:T(8,128)} %refs_7_.3) | copy-start | bytes 12292
  44.9 0.7 copy-start.7
  47.6 20.8 %all-to-all-start.1 = ((f32[32,16,128]{2,1,0:T(8,128)}), f32[32,16,128]{2,1,0:T(8,128)S(1)}, u32[]{:S(2)}, u32[]{:S(2)}) async-start(f32[32,16,128]{2,1,0:T(8,128)} %get-tuple-element.39), calls=%async_computation.1 | async-start | bytes 524288 | tf_op jit(solution)/shard_map/all_to_all | solution.py:544
  56.1 8.1 %collective-permute-start.2 = (f32[6,8,128]{2,1,0:T(8,128)S(1)}, f32[6,8,128]{2,1,0:T(8,128)S(1)}, u32[]{:S(2)}, u32[]{:S(2)}) collective-permute-start(f32[6,8,128]{2,1,0:T(8,128)S(1)} %get-tuple-element.40), channel_id=1, source_target_pairs={{0,16},{16,32},{32,48},{48,64},{64,80},{80,96},{96,112},{112,128},... | collective-permute-start | bytes 73736 | tf_op jit(solution)/shard_map/ppermute | solution.py:451
  59.5 6.1 %collective-permute-start.3 = (f32[6,8,128]{2,1,0:T(8,128)S(1)}, f32[6,8,128]{2,1,0:T(8,128)S(1)}, u32[]{:S(2)}, u32[]{:S(2)}) collective-permute-start(f32[6,8,128]{2,1,0:T(8,128)S(1)} %get-tuple-element.41), channel_id=1, source_target_pairs={{0,496},{16,0},{32,16},{48,32},{64,48},{80,64},{96,80},{112,96},{1... | collective-permute-start | bytes 73736 | tf_op jit(solution)/shard_map/ppermute | solution.py:451
  69.3 17.3 %all-to-all-start.2 = ((f32[16,8,128]{2,1,0:T(8,128)}), f32[16,8,128]{2,1,0:T(8,128)S(1)}, u32[]{:S(2)}, u32[]{:S(2)}) async-start(f32[16,8,128]{2,1,0:T(8,128)} %get-tuple-element.43), calls=%async_computation.2 | async-start | bytes 131072 | tf_op jit(solution)/shard_map/all_to_all | solution.py:552
  111.1 1.3 %collective-permute-start.5 = (f32[8,128]{1,0:T(8,128)S(1)}, f32[8,128]{1,0:T(8,128)S(1)}, u32[]{:S(2)}, u32[]{:S(2)}) collective-permute-start(f32[8,128]{1,0:T(8,128)S(1)} %get-tuple-element.54), channel_id=1, source_target_pairs={{0,15},{1,0},{2,1},{3,2},{4,3},{5,4},{6,5},{7,6},{8,7},{9,8},{10,9... | collective-permute-start | bytes 12296 | tf_op jit(solution)/shard_map/ppermute | solution.py:451
  111.1 4.3 %collective-permute-start.4 = (f32[8,128]{1,0:T(8,128)S(1)}, f32[8,128]{1,0:T(8,128)S(1)}, u32[]{:S(2)}, u32[]{:S(2)}) collective-permute-start(f32[8,128]{1,0:T(8,128)S(1)} %get-tuple-element.54), channel_id=1, source_target_pairs={{0,1},{1,2},{2,3},{3,4},{4,5},{5,6},{6,7},{7,8},{8,9},{9,10},{10,1... | collective-permute-start | bytes 12296 | tf_op jit(solution)/shard_map/ppermute | solution.py:451
  (2 other events, 1.4 us)

commit v4 on v3

--- a/solution.py
+++ b/solution.py
@@ -1,3 +1,5 @@
+import functools
+
 import jax
 import jax.numpy as jnp
 from jax import lax
@@ -162,58 +164,70 @@
             ) + jnp.where(at == row + 1, weight[2 * side + 1, c : c + 1, :], 0.0)
 
 
-def near_kernel(
-    counts,
-    slots,
-    own_points,
-    low_points,
-    high_points,
-    own,
-    low,
-    high,
-    near_out,
-    points,
-    slips,
-    target,
-    total,
-):
+def add_pairs(counts, slots, target, total, points, slips, wanted):
+    def one_target(c, _):
+        def one_source(k, _):
+            slot = slots[c, k]
+            block = slot // 8
+            row = pl.ds(slot % 8, 1)
+
+            def add():
+                y = [points(block)[i, row, :] for i in range(3)]
+                s = [slips(block)[i, row, :] for i in range(3)]
+                for part in range(8):
+                    rows = slice(part * 16, part * 16 + 16)
+                    r = [target[c, i, rows, :] - y[i] for i in range(3)]
+                    inverse = lax.rsqrt(r[0] * r[0] + r[1] * r[1] + r[2] * r[2] + SOFT)
+                    along = (r[0] * s[0] + r[1] * s[1] + r[2] * s[2]) * (inverse * inverse)
+                    for i in range(3):
+                        total[c, i, rows, :] += inverse * (s[i] + along * r[i])
+
+            if wanted is None:
+                add()
+            else:
+                pl.when(wanted(block))(add)
+            return 0
+
+        return lax.fori_loop(0, counts[c], one_source, 0)
+
+    lax.fori_loop(0, 8, one_target, 0)
+
+
+def near_own_kernel(counts, slots, own_points, own, target, total):
     ones = jnp.ones((384, 128), BF16)
     diagonal = iota((128, 128), 0) == iota((128, 128), 1)
-    for b, (p, s) in enumerate(((low_points, low), (own_points, own), (high_points, high))):
-        for i in range(3):
-            points[b, i] = p[i]
-            slips[b, i] = s[i]
     for c in range(8):
         for i in range(3):
             wide = jnp.where(diagonal, own_points[i, c : c + 1, :], 0.0)
             target[c, i] = dot(split_lanes(wide), ones, NN, None)
     total[...] = jnp.zeros(total.shape, F32)
-
-    def one_target(c, _):
-        def one_source(k, _):
-            slot = slots[c, k]
-            block = slot // 8
-            row = pl.ds(slot % 8, 1)
-            y = [points[block, i, row, :] for i in range(3)]
-            s = [slips[block, i, row, :] for i in range(3)]
-            for part in range(8):
-                rows = slice(part * 16, part * 16 + 16)
-                r = [target[c, i, rows, :] - y[i] for i in range(3)]
-                inverse = lax.rsqrt(r[0] * r[0] + r[1] * r[1] + r[2] * r[2] + SOFT)
-                along = (r[0] * s[0] + r[1] * s[1] + r[2] * s[2]) * (inverse * inverse)
-                for i in range(3):
-                    total[c, i, rows, :] += inverse * (s[i] + along * r[i])
-            return 0
-
-        return lax.fori_loop(0, counts[c], one_source, 0)
-
-    lax.fori_loop(0, 8, one_target, 0)
+    add_pairs(counts, slots, target, total, lambda b: own_points, lambda b: own, lambda b: b == 1)
+
+
+def near_rest_kernel(whole, counts, slots, target, partial, *refs):
+    (own_points, low_points, high_points, own, low, high, near_out, points, slips, total) = refs
+    for b, (p, s) in enumerate(((low_points, low), (own_points, own), (high_points, high))):
+        for i in range(3):
+            points[b, i] = p[i]
+            slips[b, i] = s[i]
+    total[...] = jnp.zeros(total.shape, F32) if whole else partial[...]
+    wanted = None if whole else lambda b: b != 1
+    add_pairs(counts, slots, target, total, lambda b: points.at[b], lambda b: slips.at[b], wanted)
+    ones = jnp.ones((384, 128), BF16)
+    diagonal = iota((128, 128), 0) == iota((128, 128), 1)
     for c in range(8):
         for i in range(3):
             summed = dot(split_lanes(total[c, i]), ones, NN, None)
             near_out[i, c : c + 1, :] = SCALE * jnp.sum(
                 jnp.where(diagonal, summed, 0.0), axis=0, keepdims=True
             )
+
+
+def pack_kernel(after, slip, points, pressure, mobility, out):
+    out[0:3] = slip[...]
+    out[3:6] = points[...]
+    out[6] = pressure[...]
+    out[7] = mobility[...]
 
 
 def pick_edges(window):
@@ -285,15 +299,16 @@
     copies_of(tile_out, sent)
 
 
-def last_kernel(received, loaded, pressure, window, tile_out):
+def last_kernel(received, low, high, loaded, pressure, window, tile_out):
     j = lax.axis_index("gx")
     peers = received.shape[0]
     window[...] = pressure[...]
     window[2:26, :] += loaded[...]
-    window[10:20, :] += received[lax.rem(j + 1, peers), 0:10, :]
-    window[8:18, :] += received[lax.rem(j - 1 + peers, peers), 0:10, :]
+    for i, size in ((0, 8), (1, 2)):
+        window[8 + 8 * i : 8 + 8 * i + size, :] += low[i, 0:size, :]
+        window[10 + 8 * i : 10 + 8 * i + size, :] += high[i, 0:size, :]
     window[18:20, :] += received[lax.rem(j + 2, peers), 0:2, :]
-    window[8:10, :] += received[lax.rem(j - 2 + peers, peers), 8:10, :]
+    window[8:10, :] += received[lax.rem(j - 2 + peers, peers), 0:2, :]
     tile_out[...] = jnp.zeros(tile_out.shape, F32)
     tile_out[0:4, 0:32] = pick_edges(window[...])[0:4]
 
@@ -424,7 +439,7 @@
 
 def second_update_kernel(received, tile, window, mobility, h, near, *refs):
     refs, outs = refs[:10], refs[10:]
-    slip_out, loaded, window_out, side_out, sent, ahead, behind = outs
+    slip_out, loaded, window_out, side_out, down_out, up_out, sent, ahead, behind = outs
     g = lax.axis_index("gy")
     left = received[jnp.maximum(g - 1, 0)]
     right = received[jnp.minimum(g + 1, received.shape[0] - 1)]
@@ -435,9 +450,13 @@
     update(parts, window_out[2:26, :], near, refs, slip_out, loaded)
     ahead[...] = jnp.zeros(ahead.shape, F32)
     behind[...] = jnp.zeros(behind.shape, F32)
-    ahead[0:10, :] = loaded[0:10, :]
-    behind[0:10, :] = loaded[14:24, :]
+    ahead[0:2, :] = loaded[0:2, :]
+    behind[0:2, :] = loaded[22:24, :]
     send_sources(ahead, behind, sent)
+    for out, at in ((down_out, 0), (up_out, 14)):
+        out[0] = loaded[at : at + 8, :]
+        out[1] = jnp.zeros((8, 128), F32)
+        out[1, 0:2, :] = loaded[at + 8 : at + 10, :]
 
 
 def final_kernel(window, left, right, mobility, mobility_side, out):
@@ -490,7 +509,13 @@
         ends=(2, 3),
         room=60,
     )
-    both = jnp.concatenate([slip, points, pressure[None], mobility[None]], axis=0)
+    (both,) = call(
+        pack_kernel,
+        [((8, 8, 128), F32)],
+        [h_mat, slip, points, pressure, mobility],
+        far=1,
+        flops=1 << 28,
+    )
     sent, cell_index, cell_weight = lax.optimization_barrier((sent, cell_index, cell_weight))
     first_cell = cell_index[:, 0, :]
     cell_row = (first_cell // 128 - j * 8 + 8 + rows) % rows
@@ -510,25 +535,32 @@
     first_high = shift(both, "gx", -1)
     low_points, high_points = first_low[3:6], first_high[3:6]
 
-    def near_field(slip, low, high):
+    target, partial = call(
+        near_own_kernel,
+        [((8, 3, 128, 128), F32), ((8, 3, 128, 128), F32)],
+        [near_counts, slots, points, slip],
+        smem=2,
+    )
+
+    def near_field(whole, slip, low, high):
+        args = [near_counts, slots, target, target if whole else partial]
         return call(
-            near_kernel,
+            functools.partial(near_rest_kernel, whole),
             [((3, 8, 128), F32)],
-            [near_counts, slots, points, low_points, high_points, slip, low, high],
+            [*args, points, low_points, high_points, slip, low, high],
             scratch=[
                 pltpu.VMEM((3, 3, 8, 128), F32),
                 pltpu.VMEM((3, 3, 8, 128), F32),
                 pltpu.VMEM((8, 3, 128, 128), F32),
-                pltpu.VMEM((8, 3, 128, 128), F32),
             ],
             smem=2,
-            flops=1 << 28,
+            flops=1 << 28 if whole else 0,
         )[0]
 
     pieces = [pltpu.VMEM((16, 128), F32), pltpu.VMEM((16, 128), F32)]
     common = [strained, basis, normal_stress, friction, compliance, slip_state, dilation]
     common += [pick, weight]
-    near = near_field(slip, first_low, first_high)
+    near = near_field(False, slip, first_low, first_high)
     slip, loaded, down, up, sent = call(
         first_update_kernel,
         [
@@ -551,24 +583,28 @@
     )
     received = lax.all_to_all(sent, "gy", 0, 0, tiled=True)
     near_slip, sent = lax.optimization_barrier((slip, sent))
-    near = near_field(near_slip, low, high)
-    slip, loaded, window, mobility_side, sent = call(
+    near = near_field(True, near_slip, low, high)
+    slip, loaded, window, mobility_side, down, up, sent = call(
         second_update_kernel,
         [
             ((3, 8, 128), F32),
             ((24, 128), F32),
             ((32, 128), F32),
             ((32, 128), F32),
-            ((nx, 16, 128), F32),
+            ((2, 8, 128), F32),
+            ((2, 8, 128), F32),
+            ((nx, 8, 128), F32),
         ],
         [received, tile, window, mobility_window, h_mat, near, slip, *common],
-        scratch=pieces,
+        scratch=[pltpu.VMEM((8, 128), F32), pltpu.VMEM((8, 128), F32)],
     )
     received = lax.all_to_all(sent, "gx", 0, 0, tiled=True)
+    low = shift(up, "gx", 1)
+    high = shift(down, "gx", -1)
     window, tile = call(
         last_kernel,
         [((32, 128), F32), ((8, 128), F32)],
-        [received, loaded, window],
+        [received, low, high, loaded, window],
     )
     left = shift(tile, "gy", 1)
     right = shift(tile, "gy", -1)

time: 117 us -> 114 us (0.974)
  the two profiles are of different devices: /device:TPU:8 before, /device:TPU:30 now
where the time goes in v4:
time: 114 us
  starting transfers between devices  71.6 us (63%)
  waiting for transfers between devices  22.9 us (20%)
  Pallas kernels  18 us (16%)
    ppermute x8, starting transfers between devices, shift(): return lax.ppermute(x, axis, [(i, (i + steps) % n) for i in range(n)])  22.7 us
    all_to_all x1, starting transfers between devices, shards(): lax.all_to_all(sent.reshape(nx * ny, 1, 128), ('gx', 'gy'), 0, 0, tiled=T...  20.9 us
    pallas_call x11, Pallas kernels, call(): pl.pallas_call(kernel, out_shape=[jax.ShapeDtypeStruct(s, d) for s, d in...  18 us
    ppermute x8, waiting for transfers between devices, shift(): return lax.ppermute(x, axis, [(i, (i + steps) % n) for i in range(n)])  17.8 us
    all_to_all x2, starting transfers between devices, shards(): received = lax.all_to_all(sent, 'gx', 0, 0, tiled=True)  16.9 us
    all_to_all x1, starting transfers between devices, shards(): received = lax.all_to_all(sent, 'gy', 0, 0, tiled=True)  11.1 us
    all_to_all x1, waiting for transfers between devices, shards(): received = lax.all_to_all(sent, 'gy', 0, 0, tiled=True)  5.11 us
  transfers between devices with their start and end apart: 12, of which 6 were waited for; matrix products, arithmetic and copies ran while one was open for 0% of the time, Pallas kernels for 7%

profile of v4, /device:TPU:30, one launch (start us, length us, event | category | flops | bytes accessed | tf_op | source)
XLA Modules:
  0.0 113.8 jit_solution(6985040591987441550)
XLA Ops:
  0.7 4.8 %shard_map.176 = (f32[256,16]{1,0:T(8,128)}, f32[512,16]{1,0:T(8,128)}, f32[512,128]{1,0:T(8,128)}) custom-call(f32[256,1022]{1,0:T(8,128)} %bitcast.55, f32[256,1022]{1,0:T(8,128)} %bitcast.57, f32[256,1022]{1,0:T(8,128)} %bitcast.56, f32[256,1022]{1,0:T(8,128)} %bitcast.58, f32[3,8,128]{2,1,0:T(8,128)} %bitcast.43, f32[8,3,16,128]{3,2,1,0:T(8,128)} %bitcast.39), custom_call_target="tpu_custom_call" | custom-call | bytes 1048576 | tf_op jit(solution)/shard_map/pallas_call | solution.py:55
  5.5 20.9 %all-to-all-start = ((f32[512,1,128]{2,1,0:T(1,128)}), f32[512,1,128]{2,1,0:T(1,128)S(1)}, u32[]{:S(2)}, u32[]{:S(2)}) async-start(f32[512,1,128]{2,1,0:T(1,128)} %bitcast.59), calls=%async_computation | async-start | bytes 524288 | tf_op jit(solution)/shard_map/all_to_all | solution.py:524
  26.7 2.7 %collective-permute-start.1 = (f32[8,8,128]{2,1,0:T(8,128)S(1)}, f32[8,8,128]{2,1,0:T(8,128)S(1)}, u32[]{:S(2)}, u32[]{:S(2)}) collective-permute-start(f32[8,8,128]{2,1,0:T(8,128)S(1)} %shard_map.177), channel_id=1, source_target_pairs={{0,496},{16,0},{32,16},{48,32},{64,48},{80,64},{96,80},{112,96},{1... | collective-permute-start | bytes 98312 | tf_op jit(solution)/shard_map/ppermute | solution.py:470
  29.4 6.4 %collective-permute-start = (f32[8,8,128]{2,1,0:T(8,128)S(1)}, f32[8,8,128]{2,1,0:T(8,128)S(1)}, u32[]{:S(2)}, u32[]{:S(2)}) collective-permute-start(f32[8,8,128]{2,1,0:T(8,128)S(1)} %shard_map.177), channel_id=1, source_target_pairs={{0,16},{16,32},{32,48},{48,64},{64,80},{80,96},{96,112},{112,128},... | collective-permute-start | bytes 98312 | tf_op jit(solution)/shard_map/ppermute | solution.py:470
  35.9 2.6 %shard_map.179 = (f32[8,3,128,128]{3,2,1,0:T(8,128)S(1)}, f32[8,3,128,128]{3,2,1,0:T(8,128)S(1)}) custom-call(s32[8]{0:T(128)S(1)} %copy-done.13, s32[8,8]{1,0:T(8,128)S(1)} %add_select_fusion.slots, f32[3,8,128]{2,1,0:T(8,128)S(1)} %bitcast.49, f32[3,8,128]{2,1,0:T(8,128)S(1)} %bitcast.45), custom_call_target="tpu_custom_call" | custom-call | bytes 1048576 | tf_op jit(solution)/shard_map/pallas_call | solution.py:55
  38.6 2.1 %shard_map.180.near = f32[3,8,128]{2,1,0:T(8,128)S(1)} custom-call(s32[8]{0:T(128)S(1)} %copy-done.13, s32[8,8]{1,0:T(8,128)S(1)} %add_select_fusion.slots, f32[8,3,128,128]{3,2,1,0:T(8,128)S(1)} %get-tuple-element.41.target.partial, f32[8,3,128,128]{3,2,1,0:T(8,128)S(1)} %get-tuple-element.42.partial, f32[3,8,128]{2,1,0:T(8,128)S(1)} %bitcast.50, ...), custom_call_target="tpu_custom_call" | custom-call | bytes 1048576 | tf_op jit(solution)/shard_map/pallas_call | solution.py:55
  40.8 2.1 %shard_map.181 = (f32[3,8,128]{2,1,0:T(8,128)S(1)}, f32[24,128]{1,0:T(8,128)S(1)}, f32[6,8,128]{2,1,0:T(8,128)S(1)}, f32[6,8,128]{2,1,0:T(8,128)S(1)}, f32[32,16,128]{2,1,0:T(8,128)}) custom-call(f32[512,128]{1,0:T(8,128)S(1)} %bitcast.42, f32[8,8,128]{2,1,0:T(8,128)S(1)} %collective-permute-done.refs_4_.low.first_low, ...), custom_call_target="tpu_custom_call" | custom-call | bytes 1048576 | tf_op jit(solution)/shard_map/pallas_call | solution.py:55
  42.9 9.5 %all-to-all-start.1 = ((f32[32,16,128]{2,1,0:T(8,128)}), f32[32,16,128]{2,1,0:T(8,128)S(1)}, u32[]{:S(2)}, u32[]{:S(2)}) async-start(f32[32,16,128]{2,1,0:T(8,128)} %get-tuple-element.45), calls=%async_computation.1 | async-start | bytes 524288 | tf_op jit(solution)/shard_map/all_to_all | solution.py:576
  52.4 4.6 %collective-permute-start.2 = (f32[6,8,128]{2,1,0:T(8,128)S(1)}, f32[6,8,128]{2,1,0:T(8,128)S(1)}, u32[]{:S(2)}, u32[]{:S(2)}) collective-permute-start(f32[6,8,128]{2,1,0:T(8,128)S(1)} %get-tuple-element.46), channel_id=1, source_target_pairs={{0,16},{16,32},{32,48},{48,64},{64,80},{80,96},{96,112},{112,128},... | collective-permute-start | bytes 73736 | tf_op jit(solution)/shard_map/ppermute | solution.py:470
  57.0 1.9 %collective-permute-start.3 = (f32[6,8,128]{2,1,0:T(8,128)S(1)}, f32[6,8,128]{2,1,0:T(8,128)S(1)}, u32[]{:S(2)}, u32[]{:S(2)}) collective-permute-start(f32[6,8,128]{2,1,0:T(8,128)S(1)} %get-tuple-element.47), channel_id=1, source_target_pairs={{0,496},{16,0},{32,16},{48,32},{64,48},{80,64},{96,80},{112,96},{1... | collective-permute-start | bytes 73736 | tf_op jit(solution)/shard_map/ppermute | solution.py:470
  58.9 0.6 collective-permute-done.2.low.refs_4_
  59.5 6.5 %collective-permute-done.3.high.refs_5_ = f32[6,8,128]{2,1,0:T(8,128)S(1)} collective-permute-done((f32[6,8,128]{2,1,0:T(8,128)S(1)}, f32[6,8,128]{2,1,0:T(8,128)S(1)}, u32[]{:S(2)}, u32[]{:S(2)}) %collective-permute-start.3) | collective-permute-done | bytes 24608 | tf_op jit(solution)/shard_map/ppermute | solution.py:470
  66.0 0.8 shard_map.182
  66.8 11.1 %all-to-all-start.2 = ((f32[16,8,128]{2,1,0:T(8,128)}), f32[16,8,128]{2,1,0:T(8,128)S(1)}, u32[]{:S(2)}, u32[]{:S(2)}) async-start(f32[16,8,128]{2,1,0:T(8,128)} %get-tuple-element.49), calls=%async_computation.2 | async-start | bytes 131072 | tf_op jit(solution)/shard_map/all_to_all | solution.py:584
  78.0 2.8 %shard_map.183.near = f32[3,8,128]{2,1,0:T(8,128)S(1)} custom-call(s32[8]{0:T(128)S(1)} %copy-done.13, s32[8,8]{1,0:T(8,128)S(1)} %add_select_fusion.slots, f32[8,3,128,128]{3,2,1,0:T(8,128)S(1)} %get-tuple-element.41.target.partial, f32[8,3,128,128]{3,2,1,0:T(8,128)S(1)} %get-tuple-element.41.target.partial, f32[3,8,128]{2,1,0:T(8,128)S(1)} %bitcast.51, ...), custom_call_target="tpu_custom_call" | custom-call | flops 268435456 | bytes 1048576 | tf_op jit(solution)/shard_map/pallas_call | solution.py:55
  80.7 5.1 %all-to-all-done.2.received = f32[16,8,128]{2,1,0:T(8,128)S(1)} async-done(((f32[16,8,128]{2,1,0:T(8,128)}), f32[16,8,128]{2,1,0:T(8,128)S(1)}, u32[]{:S(2)}, u32[]{:S(2)}) %all-to-all-start.2) | async-done | bytes 65568 | tf_op jit(solution)/shard_map/all_to_all | solution.py:584
  85.9 1.7 %shard_map.184 = (f32[3,8,128]{2,1,0:T(8,128)}, f32[24,128]{1,0:T(8,128)S(1)}, f32[32,128]{1,0:T(8,128)S(1)}, f32[32,128]{1,0:T(8,128)S(1)}, f32[2,8,128]{2,1,0:...) custom-call(f32[16,8,128]{2,1,0:T(8,128)S(1)} %all-to-all-done.2.received, ...), custom_call_target="tpu_custom_call" | custom-call | bytes 1048576 | tf_op jit(solution)/shard_map/pallas_call | solution.py:55
  87.6 7.4 %all-to-all-start.3 = ((f32[32,8,128]{2,1,0:T(8,128)}), f32[32,8,128]{2,1,0:T(8,128)S(1)}, u32[]{:S(2)}, u32[]{:S(2)}) async-start(f32[32,8,128]{2,1,0:T(8,128)} %get-tuple-element.56), calls=%async_computation.3 | async-start | bytes 262144 | tf_op jit(solution)/shard_map/all_to_all | solution.py:601
  95.0 4.6 %collective-permute-start.4 = (f32[2,8,128]{2,1,0:T(8,128)S(1)}, f32[2,8,128]{2,1,0:T(8,128)S(1)}, u32[]{:S(2)}, u32[]{:S(2)}) collective-permute-start(f32[2,8,128]{2,1,0:T(8,128)S(1)} %get-tuple-element.57), channel_id=1, source_target_pairs={{0,16},{16,32},{32,48},{48,64},{64,80},{80,96},{96,112},{112,128},... | collective-permute-start | bytes 24584 | tf_op jit(solution)/shard_map/ppermute | solution.py:470
  99.6 1.9 %collective-permute-start.5 = (f32[2,8,128]{2,1,0:T(8,128)S(1)}, f32[2,8,128]{2,1,0:T(8,128)S(1)}, u32[]{:S(2)}, u32[]{:S(2)}) collective-permute-start(f32[2,8,128]{2,1,0:T(8,128)S(1)} %get-tuple-element.58), channel_id=1, source_target_pairs={{0,496},{16,0},{32,16},{48,32},{64,48},{80,64},{96,80},{112,96},{1... | collective-permute-start | bytes 24584 | tf_op jit(solution)/shard_map/ppermute | solution.py:470
  101.5 6.9 %collective-permute-done.5.high = f32[2,8,128]{2,1,0:T(8,128)S(1)} collective-permute-done((f32[2,8,128]{2,1,0:T(8,128)S(1)}, f32[2,8,128]{2,1,0:T(8,128)S(1)}, u32[]{:S(2)}, u32[]{:S(2)}) %collective-permute-start.5) | collective-permute-done | bytes 8224 | tf_op jit(solution)/shard_map/ppermute | solution.py:470
  109.1 0.8 collective-permute-done.7.right
  109.9 2.9 %collective-permute-done.6.left = f32[8,128]{1,0:T(8,128)S(1)} collective-permute-done((f32[8,128]{1,0:T(8,128)S(1)}, f32[8,128]{1,0:T(8,128)S(1)}, u32[]{:S(2)}, u32[]{:S(2)}) %collective-permute-start.6) | collective-permute-done | bytes 4128 | tf_op jit(solution)/shard_map/ppermute | solution.py:470
  112.8 1.0 shard_map.186
  (52 shorter events, 1.0 us)
Async XLA Ops:
  0.6 25.8 %copy-start.14 = (s32[8,4,128]{2,1,0:T(4,128)S(1)}, s32[8,4,128]{2,1,0:T(4,128)}, u32[]{:S(2)}) copy-start(s32[8,4,128]{2,1,0:T(4,128)} %param.29) | copy-start | bytes 49156
  0.6 25.8 %copy-start.15 = (f32[8,4,128]{2,1,0:T(4,128)S(1)}, f32[8,4,128]{2,1,0:T(4,128)}, u32[]{:S(2)}) copy-start(f32[8,4,128]{2,1,0:T(4,128)} %param.30) | copy-start | bytes 49156
  5.4 21.2 %copy-start.1 = (f32[512,16]{1,0:T(8,128)S(1)}, f32[512,16]{1,0:T(8,128)}, u32[]{:S(2)}) copy-start(f32[512,16]{1,0:T(8,128)} %get-tuple-element.35.after.h) | copy-start | bytes 98308
  5.4 21.2 %copy-start.2 = (f32[8,3,128]{2,0,1:T(8,128)S(1)}, f32[8,3,128]{2,0,1:T(8,128)}, u32[]{:S(2)}) copy-start(f32[8,3,128]{2,0,1:T(8,128)} %param.17) | copy-start | bytes 36868
  5.5 21.2 %copy-start.4 = (f32[8,3,128]{2,0,1:T(8,128)S(1)}, f32[8,3,128]{2,0,1:T(8,128)}, u32[]{:S(2)}) copy-start(f32[8,3,128]{2,0,1:T(8,128)} %param.18) | copy-start | bytes 36868
  5.5 21.2 %copy-start.6 = (f32[8,128]{1,0:T(8,128)S(1)}, f32[8,128]{1,0:T(8,128)}, u32[]{:S(2)}) copy-start(f32[8,128]{1,0:T(8,128)} %pressure.5) | copy-start | bytes 12292
  5.5 21.2 %copy-start.7 = (f32[8,128]{1,0:T(8,128)S(1)}, f32[8,128]{1,0:T(8,128)}, u32[]{:S(2)}) copy-start(f32[8,128]{1,0:T(8,128)} %mobility.5) | copy-start | bytes 12292
  5.5 30.4 %copy-start.16 = (s32[8,8]{1,0:T(8,128)S(1)}, s32[8,8]{1,0:T(8,128)}, u32[]{:S(2)}) copy-start(s32[8,8]{1,0:T(8,128)} %param.19) | copy-start | bytes 772
  5.5 30.4 %copy-start.13 = (s32[8]{0:T(128)S(1)}, s32[8]{0:T(128)}, u32[]{:S(2)}) copy-start(s32[8]{0:T(128)} %counts.5) | copy-start | bytes 100
  5.5 35.2 %all-to-all-start = ((f32[512,1,128]{2,1,0:T(1,128)}), f32[512,1,128]{2,1,0:T(1,128)S(1)}, u32[]{:S(2)}, u32[]{:S(2)}) async-start(f32[512,1,128]{2,1,0:T(1,128)} %bitcast.59), calls=%async_computation | async-start | bytes 524288 | tf_op jit(solution)/shard_map/all_to_all | solution.py:524
  26.7 11.8 %collective-permute-start.1 = (f32[8,8,128]{2,1,0:T(8,128)S(1)}, f32[8,8,128]{2,1,0:T(8,128)S(1)}, u32[]{:S(2)}, u32[]{:S(2)}) collective-permute-start(f32[8,8,128]{2,1,0:T(8,128)S(1)} %shard_map.177), channel_id=1, source_target_pairs={{0,496},{16,0},{32,16},{48,32},{64,48},{80,64},{96,80},{112,96},{1... | collective-permute-start | bytes 98312 | tf_op jit(solution)/shard_map/ppermute | solution.py:470
  29.4 9.0 %collective-permute-start = (f32[8,8,128]{2,1,0:T(8,128)S(1)}, f32[8,8,128]{2,1,0:T(8,128)S(1)}, u32[]{:S(2)}, u32[]{:S(2)}) collective-permute-start(f32[8,8,128]{2,1,0:T(8,128)S(1)} %shard_map.177), channel_id=1, source_target_pairs={{0,16},{16,32},{32,48},{48,64},{64,80},{80,96},{96,112},{112,128},... | collective-permute-start | bytes 98312 | tf_op jit(solution)/shard_map/ppermute | solution.py:470
  38.5 2.2 %copy-start = (f32[8,16,3,128]{3,1,2,0:T(8,128)S(1)}, f32[8,16,3,128]{3,1,2,0:T(8,128)}, u32[]{:S(2)}) copy-start(f32[8,16,3,128]{3,1,2,0:T(8,128)} %param.21) | copy-start | bytes 589828
  38.5 2.2 %copy-start.3 = (f32[256,16]{1,0:T(8,128)S(1)}, f32[256,16]{1,0:T(8,128)}, u32[]{:S(2)}) copy-start(f32[256,16]{1,0:T(8,128)} %get-tuple-element.40.lifts) | copy-start | bytes 49156
  38.5 2.2 %copy-start.5 = (f32[8,3,128]{2,0,1:T(8,128)S(1)}, f32[8,3,128]{2,0,1:T(8,128)}, u32[]{:S(2)}) copy-start(f32[8,3,128]{2,0,1:T(8,128)} %param.24) | copy-start | bytes 36868
  42.9 23.2 %all-to-all-start.1 = ((f32[32,16,128]{2,1,0:T(8,128)}), f32[32,16,128]{2,1,0:T(8,128)S(1)}, u32[]{:S(2)}, u32[]{:S(2)}) async-start(f32[32,16,128]{2,1,0:T(8,128)} %get-tuple-element.45), calls=%async_computation.1 | async-start | bytes 524288 | tf_op jit(solution)/shard_map/all_to_all | solution.py:576
  52.4 7.1 %collective-permute-start.2 = (f32[6,8,128]{2,1,0:T(8,128)S(1)}, f32[6,8,128]{2,1,0:T(8,128)S(1)}, u32[]{:S(2)}, u32[]{:S(2)}) collective-permute-start(f32[6,8,128]{2,1,0:T(8,128)S(1)} %get-tuple-element.46), channel_id=1, source_target_pairs={{0,16},{16,32},{32,48},{48,64},{64,80},{80,96},{96,112},{112,128},... | collective-permute-start | bytes 73736 | tf_op jit(solution)/shard_map/ppermute | solution.py:470
  57.0 9.0 %collective-permute-start.3 = (f32[6,8,128]{2,1,0:T(8,128)S(1)}, f32[6,8,128]{2,1,0:T(8,128)S(1)}, u32[]{:S(2)}, u32[]{:S(2)}) collective-permute-start(f32[6,8,128]{2,1,0:T(8,128)S(1)} %get-tuple-element.47), channel_id=1, source_target_pairs={{0,496},{16,0},{32,16},{48,32},{64,48},{80,64},{96,80},{112,96},{1... | collective-permute-start | bytes 73736 | tf_op jit(solution)/shard_map/ppermute | solution.py:470
  66.8 19.0 %all-to-all-start.2 = ((f32[16,8,128]{2,1,0:T(8,128)}), f32[16,8,128]{2,1,0:T(8,128)S(1)}, u32[]{:S(2)}, u32[]{:S(2)}) async-start(f32[16,8,128]{2,1,0:T(8,128)} %get-tuple-element.49), calls=%async_computation.2 | async-start | bytes 131072 | tf_op jit(solution)/shard_map/all_to_all | solution.py:584
  87.6 20.8 %all-to-all-start.3 = ((f32[32,8,128]{2,1,0:T(8,128)}), f32[32,8,128]{2,1,0:T(8,128)S(1)}, u32[]{:S(2)}, u32[]{:S(2)}) async-start(f32[32,8,128]{2,1,0:T(8,128)} %get-tuple-element.56), calls=%async_computation.3 | async-start | bytes 262144 | tf_op jit(solution)/shard_map/all_to_all | solution.py:601
  95.0 6.5 %collective-permute-start.4 = (f32[2,8,128]{2,1,0:T(8,128)S(1)}, f32[2,8,128]{2,1,0:T(8,128)S(1)}, u32[]{:S(2)}, u32[]{:S(2)}) collective-permute-start(f32[2,8,128]{2,1,0:T(8,128)S(1)} %get-tuple-element.57), channel_id=1, source_target_pairs={{0,16},{16,32},{32,48},{48,64},{64,80},{80,96},{96,112},{112,128},... | collective-permute-start | bytes 24584 | tf_op jit(solution)/shard_map/ppermute | solution.py:470
  99.6 8.9 %collective-permute-start.5 = (f32[2,8,128]{2,1,0:T(8,128)S(1)}, f32[2,8,128]{2,1,0:T(8,128)S(1)}, u32[]{:S(2)}, u32[]{:S(2)}) collective-permute-start(f32[2,8,128]{2,1,0:T(8,128)S(1)} %get-tuple-element.58), channel_id=1, source_target_pairs={{0,496},{16,0},{32,16},{48,32},{64,48},{80,64},{96,80},{112,96},{1... | collective-permute-start | bytes 24584 | tf_op jit(solution)/shard_map/ppermute | solution.py:470
  108.6 1.3 %collective-permute-start.7 = (f32[8,128]{1,0:T(8,128)S(1)}, f32[8,128]{1,0:T(8,128)S(1)}, u32[]{:S(2)}, u32[]{:S(2)}) collective-permute-start(f32[8,128]{1,0:T(8,128)S(1)} %get-tuple-element.62), channel_id=1, source_target_pairs={{0,15},{1,0},{2,1},{3,2},{4,3},{5,4},{6,5},{7,6},{8,7},{9,8},{10,9... | collective-permute-start | bytes 12296 | tf_op jit(solution)/shard_map/ppermute | solution.py:470
  108.6 4.3 %collective-permute-start.6 = (f32[8,128]{1,0:T(8,128)S(1)}, f32[8,128]{1,0:T(8,128)S(1)}, u32[]{:S(2)}, u32[]{:S(2)}) collective-permute-start(f32[8,128]{1,0:T(8,128)S(1)} %get-tuple-element.62), channel_id=1, source_target_pairs={{0,1},{1,2},{2,3},{3,4},{4,5},{5,6},{6,7},{7,8},{8,9},{9,10},{10,1... | collective-permute-start | bytes 12296 | tf_op jit(solution)/shard_map/ppermute | solution.py:470
  (5 other events, 10.9 us)

commit v5 on v4

--- a/solution.py
+++ b/solution.py
@@ -470,6 +470,17 @@
     return lax.ppermute(x, axis, [(i, (i + steps) % n) for i in range(n)])
 
 
+def with_neighbours(up, down, axis):
+    n = lax.axis_size(axis)
+    even = lax.axis_index(axis) % 2 == 0
+    alike = up is down
+    first = up if alike else jnp.where(even, up, down)
+    second = up if alike else jnp.where(even, down, up)
+    first = lax.ppermute(first, axis, [(i, i ^ 1) for i in range(n)])
+    second = lax.ppermute(second, axis, [(i, (i + 2 * (i % 2) - 1) % n) for i in range(n)])
+    return jnp.where(even, second, first), jnp.where(even, first, second)
+
+
 def shards(
     slip_field,
     positions,
@@ -531,8 +542,7 @@
         flops=1 << 28,
     )
     both, pick = lax.optimization_barrier((both, pick))
-    first_low = shift(both, "gx", 1)
-    first_high = shift(both, "gx", -1)
+    first_low, first_high = with_neighbours(both, both, "gx")
     low_points, high_points = first_low[3:6], first_high[3:6]
 
     target, partial = call(
@@ -574,8 +584,7 @@
         scratch=pieces,
     )
     received = lax.all_to_all(sent, "gx", 0, 0, tiled=True)
-    low = shift(up, "gx", 1)
-    high = shift(down, "gx", -1)
+    low, high = with_neighbours(up, down, "gx")
     window, mobility_window, tile, sent = call(
         between_kernel,
         [((32, 128), F32), ((32, 128), F32), ((8, 128), F32), ((ny, 8, 128), F32)],
@@ -599,8 +608,7 @@
         scratch=[pltpu.VMEM((8, 128), F32), pltpu.VMEM((8, 128), F32)],
     )
     received = lax.all_to_all(sent, "gx", 0, 0, tiled=True)
-    low = shift(up, "gx", 1)
-    high = shift(down, "gx", -1)
+    low, high = with_neighbours(up, down, "gx")
     window, tile = call(
         last_kernel,
         [((32, 128), F32), ((8, 128), F32)],

time: 114 us -> 111 us (0.974)
  the two profiles are of different devices: /device:TPU:30 before, /device:TPU:32 now
where the time goes in v5:
time: 111 us; the launch traced here: 110 us
  starting transfers between devices  69.3 us (62%)
  waiting for transfers between devices  20.8 us (19%)
  Pallas kernels  19 us (17%)
  between operations  1.14 us (1%)
    all_to_all x1, starting transfers between devices, shards(): lax.all_to_all(sent.reshape(nx * ny, 1, 128), ('gx', 'gy'), 0, 0, tiled=T...  20.9 us
    pallas_call x11, Pallas kernels, call(): pl.pallas_call(kernel, out_shape=[jax.ShapeDtypeStruct(s, d) for s, d in...  19 us
    all_to_all x2, starting transfers between devices, shards(): received = lax.all_to_all(sent, 'gx', 0, 0, tiled=True)  16.6 us
    ppermute x3, waiting for transfers between devices, with_neighbours(): lax.ppermute(second, axis, [(i, (i + 2 * (i % 2) - 1) % n) for i in range...  12.3 us
    ppermute x3, starting transfers between devices, with_neighbours(): lax.ppermute(second, axis, [(i, (i + 2 * (i % 2) - 1) % n) for i in range...  11.9 us
    ppermute x3, starting transfers between devices, with_neighbours(): first = lax.ppermute(first, axis, [(i, i ^ 1) for i in range(n)])  10.1 us
    all_to_all x1, starting transfers between devices, shards(): received = lax.all_to_all(sent, 'gy', 0, 0, tiled=True)  9.21 us
    all_to_all x1, waiting for transfers between devices, shards(): received = lax.all_to_all(sent, 'gy', 0, 0, tiled=True)  4.7 us
  transfers between devices with their start and end apart: 12, of which 6 were waited for; matrix products, arithmetic and copies ran while one was open for 0% of the time, Pallas kernels for 8%

profile of v5, /device:TPU:32, one launch (start us, length us, event | category | flops | bytes accessed | tf_op | source)
XLA Modules:
  0.0 110.4 jit_solution(12421508844920595223)
XLA Ops:
  0.7 4.8 %shard_map.176 = (f32[256,16]{1,0:T(8,128)}, f32[512,16]{1,0:T(8,128)}, f32[512,128]{1,0:T(8,128)}) custom-call(f32[256,1022]{1,0:T(8,128)} %bitcast.55, f32[256,1022]{1,0:T(8,128)} %bitcast.57, f32[256,1022]{1,0:T(8,128)} %bitcast.56, f32[256,1022]{1,0:T(8,128)} %bitcast.58, f32[3,8,128]{2,1,0:T(8,128)} %bitcast.43, f32[8,3,16,128]{3,2,1,0:T(8,128)} %bitcast.39), custom_call_target="tpu_custom_call" | custom-call | bytes 1048576 | tf_op jit(solution)/shard_map/pallas_call | solution.py:55
  5.5 20.9 %all-to-all-start = ((f32[512,1,128]{2,1,0:T(1,128)}), f32[512,1,128]{2,1,0:T(1,128)S(1)}, u32[]{:S(2)}, u32[]{:S(2)}) async-start(f32[512,1,128]{2,1,0:T(1,128)} %bitcast.59), calls=%async_computation | async-start | bytes 524288 | tf_op jit(solution)/shard_map/all_to_all | solution.py:535
  26.7 3.4 %collective-permute-start.1 = (f32[8,8,128]{2,1,0:T(8,128)S(1)}, f32[8,8,128]{2,1,0:T(8,128)S(1)}, u32[]{:S(2)}, u32[]{:S(2)}) collective-permute-start(f32[8,8,128]{2,1,0:T(8,128)S(1)} %shard_map.177), channel_id=1, source_target_pairs={{0,16},{16,0},{32,48},{48,32},{64,80},{80,64},{96,112},{112,96},{1... | collective-permute-start | bytes 98312 | tf_op jit(solution)/shard_map/ppermute | solution.py:479
  30.1 3.9 %collective-permute-start = (f32[8,8,128]{2,1,0:T(8,128)S(1)}, f32[8,8,128]{2,1,0:T(8,128)S(1)}, u32[]{:S(2)}, u32[]{:S(2)}) collective-permute-start(f32[8,8,128]{2,1,0:T(8,128)S(1)} %shard_map.177), channel_id=1, source_target_pairs={{0,496},{16,32},{32,16},{48,64},{64,48},{80,96},{96,80},{112,128},... | collective-permute-start | bytes 98312 | tf_op jit(solution)/shard_map/ppermute | solution.py:480
  34.1 2.7 %shard_map.179 = (f32[8,3,128,128]{3,2,1,0:T(8,128)S(1)}, f32[8,3,128,128]{3,2,1,0:T(8,128)S(1)}) custom-call(s32[8]{0:T(128)S(1)} %copy-done.13, s32[8,8]{1,0:T(8,128)S(1)} %add_select_fusion.slots, f32[3,8,128]{2,1,0:T(8,128)S(1)} %bitcast.49, f32[3,8,128]{2,1,0:T(8,128)S(1)} %bitcast.45), custom_call_target="tpu_custom_call" | custom-call | bytes 1048576 | tf_op jit(solution)/shard_map/pallas_call | solution.py:55
  36.8 2.4 %collective-permute-done = f32[8,8,128]{2,1,0:T(8,128)S(1)} collective-permute-done((f32[8,8,128]{2,1,0:T(8,128)S(1)}, f32[8,8,128]{2,1,0:T(8,128)S(1)}, u32[]{:S(2)}, u32[]{:S(2)}) %collective-permute-start) | collective-permute-done | bytes 32800 | tf_op jit(solution)/shard_map/ppermute | solution.py:480
  39.3 2.5 %shard_map.180.near = f32[3,8,128]{2,1,0:T(8,128)S(1)} custom-call(s32[8]{0:T(128)S(1)} %copy-done.13, s32[8,8]{1,0:T(8,128)S(1)} %add_select_fusion.slots, f32[8,3,128,128]{3,2,1,0:T(8,128)S(1)} %get-tuple-element.41.target.partial, f32[8,3,128,128]{3,2,1,0:T(8,128)S(1)} %get-tuple-element.42.partial, f32[3,8,128]{2,1,0:T(8,128)S(1)} %bitcast.50, ...), custom_call_target="tpu_custom_call" | custom-call | bytes 1048576 | tf_op jit(solution)/shard_map/pallas_call | solution.py:55
  41.9 2.1 %shard_map.181 = (f32[3,8,128]{2,1,0:T(8,128)S(1)}, f32[24,128]{1,0:T(8,128)S(1)}, f32[6,8,128]{2,1,0:T(8,128)S(1)}, f32[6,8,128]{2,1,0:T(8,128)S(1)}, f32[32,16,128]{2,1,0:T(8,128)}) custom-call(f32[512,128]{1,0:T(8,128)S(1)} %bitcast.42, f32[8,8,128]{2,1,0:T(8,128)S(1)} %get-tuple-element.67.refs_4_.low.first_low, ...), custom_call_target="tpu_custom_call" | custom-call | bytes 1048576 | tf_op jit(solution)/shard_map/pallas_call | solution.py:55
  44.0 9.0 %all-to-all-start.1 = ((f32[32,16,128]{2,1,0:T(8,128)}), f32[32,16,128]{2,1,0:T(8,128)S(1)}, u32[]{:S(2)}, u32[]{:S(2)}) async-start(f32[32,16,128]{2,1,0:T(8,128)} %get-tuple-element.45), calls=%async_computation.1 | async-start | bytes 524288 | tf_op jit(solution)/shard_map/all_to_all | solution.py:586
  53.0 3.4 %collective-permute-start.3 = (f32[6,8,128]{2,1,0:T(8,128)S(1)}, f32[6,8,128]{2,1,0:T(8,128)S(1)}, u32[]{:S(2)}, u32[]{:S(2)}) collective-permute-start(f32[6,8,128]{2,1,0:T(8,128)S(1)} %get-tuple-element.70), channel_id=1, source_target_pairs={{0,16},{16,0},{32,48},{48,32},{64,80},{80,64},{96,112},{112,96},{1... | collective-permute-start | bytes 73736 | tf_op jit(solution)/shard_map/ppermute | solution.py:479
  56.4 4.0 %collective-permute-start.2 = (f32[6,8,128]{2,1,0:T(8,128)S(1)}, f32[6,8,128]{2,1,0:T(8,128)S(1)}, u32[]{:S(2)}, u32[]{:S(2)}) collective-permute-start(f32[6,8,128]{2,1,0:T(8,128)S(1)} %get-tuple-element.71), channel_id=1, source_target_pairs={{0,496},{16,32},{32,16},{48,64},{64,48},{80,96},{96,80},{112,128},... | collective-permute-start | bytes 73736 | tf_op jit(solution)/shard_map/ppermute | solution.py:480
  60.4 5.0 %collective-permute-done.2 = f32[6,8,128]{2,1,0:T(8,128)S(1)} collective-permute-done((f32[6,8,128]{2,1,0:T(8,128)S(1)}, f32[6,8,128]{2,1,0:T(8,128)S(1)}, u32[]{:S(2)}, u32[]{:S(2)}) %collective-permute-start.2) | collective-permute-done | bytes 24608 | tf_op jit(solution)/shard_map/ppermute | solution.py:480
  65.4 0.8 shard_map.182
  66.2 9.2 %all-to-all-start.2 = ((f32[16,8,128]{2,1,0:T(8,128)}), f32[16,8,128]{2,1,0:T(8,128)S(1)}, u32[]{:S(2)}, u32[]{:S(2)}) async-start(f32[16,8,128]{2,1,0:T(8,128)} %get-tuple-element.49), calls=%async_computation.2 | async-start | bytes 131072 | tf_op jit(solution)/shard_map/all_to_all | solution.py:593
  75.5 3.2 %shard_map.183.near = f32[3,8,128]{2,1,0:T(8,128)S(1)} custom-call(s32[8]{0:T(128)S(1)} %copy-done.13, s32[8,8]{1,0:T(8,128)S(1)} %add_select_fusion.slots, f32[8,3,128,128]{3,2,1,0:T(8,128)S(1)} %get-tuple-element.41.target.partial, f32[8,3,128,128]{3,2,1,0:T(8,128)S(1)} %get-tuple-element.41.target.partial, f32[3,8,128]{2,1,0:T(8,128)S(1)} %bitcast.51, ...), custom_call_target="tpu_custom_call" | custom-call | flops 268435456 | bytes 1048576 | tf_op jit(solution)/shard_map/pallas_call | solution.py:55
  78.6 4.7 %all-to-all-done.2.received = f32[16,8,128]{2,1,0:T(8,128)S(1)} async-done(((f32[16,8,128]{2,1,0:T(8,128)}), f32[16,8,128]{2,1,0:T(8,128)S(1)}, u32[]{:S(2)}, u32[]{:S(2)}) %all-to-all-start.2) | async-done | bytes 65568 | tf_op jit(solution)/shard_map/all_to_all | solution.py:593
  83.3 1.7 %shard_map.184 = (f32[3,8,128]{2,1,0:T(8,128)}, f32[24,128]{1,0:T(8,128)S(1)}, f32[32,128]{1,0:T(8,128)S(1)}, f32[32,128]{1,0:T(8,128)S(1)}, f32[2,8,128]{2,1,0:...) custom-call(f32[16,8,128]{2,1,0:T(8,128)S(1)} %all-to-all-done.2.received, ...), custom_call_target="tpu_custom_call" | custom-call | bytes 1048576 | tf_op jit(solution)/shard_map/pallas_call | solution.py:55
  85.1 7.7 %all-to-all-start.3 = ((f32[32,8,128]{2,1,0:T(8,128)}), f32[32,8,128]{2,1,0:T(8,128)S(1)}, u32[]{:S(2)}, u32[]{:S(2)}) async-start(f32[32,8,128]{2,1,0:T(8,128)} %get-tuple-element.56), calls=%async_computation.3 | async-start | bytes 262144 | tf_op jit(solution)/shard_map/all_to_all | solution.py:610
  92.7 3.4 %collective-permute-start.5 = (f32[2,8,128]{2,1,0:T(8,128)S(1)}, f32[2,8,128]{2,1,0:T(8,128)S(1)}, u32[]{:S(2)}, u32[]{:S(2)}) collective-permute-start(f32[2,8,128]{2,1,0:T(8,128)S(1)} %get-tuple-element.74), channel_id=1, source_target_pairs={{0,16},{16,0},{32,48},{48,32},{64,80},{80,64},{96,112},{112,96},{1... | collective-permute-start | bytes 24584 | tf_op jit(solution)/shard_map/ppermute | solution.py:479
  96.1 4.0 %collective-permute-start.4 = (f32[2,8,128]{2,1,0:T(8,128)S(1)}, f32[2,8,128]{2,1,0:T(8,128)S(1)}, u32[]{:S(2)}, u32[]{:S(2)}) collective-permute-start(f32[2,8,128]{2,1,0:T(8,128)S(1)} %get-tuple-element.75), channel_id=1, source_target_pairs={{0,496},{16,32},{32,16},{48,64},{64,48},{80,96},{96,80},{112,128},... | collective-permute-start | bytes 24584 | tf_op jit(solution)/shard_map/ppermute | solution.py:480
  100.1 4.9 %collective-permute-done.4 = f32[2,8,128]{2,1,0:T(8,128)S(1)} collective-permute-done((f32[2,8,128]{2,1,0:T(8,128)S(1)}, f32[2,8,128]{2,1,0:T(8,128)S(1)}, u32[]{:S(2)}, u32[]{:S(2)}) %collective-permute-start.4) | collective-permute-done | bytes 8224 | tf_op jit(solution)/shard_map/ppermute | solution.py:480
  105.7 0.8 collective-permute-done.7.right
  106.5 2.9 %collective-permute-done.6.left = f32[8,128]{1,0:T(8,128)S(1)} collective-permute-done((f32[8,128]{1,0:T(8,128)S(1)}, f32[8,128]{1,0:T(8,128)S(1)}, u32[]{:S(2)}, u32[]{:S(2)}) %collective-permute-start.6) | collective-permute-done | bytes 4128 | tf_op jit(solution)/shard_map/ppermute | solution.py:470
  109.4 1.0 shard_map.186
  (57 shorter events, 1.0 us)
Async XLA Ops:
  0.6 25.8 %copy-start.14 = (s32[8,4,128]{2,1,0:T(4,128)S(1)}, s32[8,4,128]{2,1,0:T(4,128)}, u32[]{:S(2)}) copy-start(s32[8,4,128]{2,1,0:T(4,128)} %param.29) | copy-start | bytes 49156
  0.6 25.9 %copy-start.15 = (f32[8,4,128]{2,1,0:T(4,128)S(1)}, f32[8,4,128]{2,1,0:T(4,128)}, u32[]{:S(2)}) copy-start(f32[8,4,128]{2,1,0:T(4,128)} %param.30) | copy-start | bytes 49156
  5.4 21.2 %copy-start.1 = (f32[512,16]{1,0:T(8,128)S(1)}, f32[512,16]{1,0:T(8,128)}, u32[]{:S(2)}) copy-start(f32[512,16]{1,0:T(8,128)} %get-tuple-element.35.after.h) | copy-start | bytes 98308
  5.5 21.2 %copy-start.2 = (f32[8,3,128]{2,0,1:T(8,128)S(1)}, f32[8,3,128]{2,0,1:T(8,128)}, u32[]{:S(2)}) copy-start(f32[8,3,128]{2,0,1:T(8,128)} %param.17) | copy-start | bytes 36868
  5.5 21.2 %copy-start.4 = (f32[8,3,128]{2,0,1:T(8,128)S(1)}, f32[8,3,128]{2,0,1:T(8,128)}, u32[]{:S(2)}) copy-start(f32[8,3,128]{2,0,1:T(8,128)} %param.18) | copy-start | bytes 36868
  5.5 21.2 %copy-start.6 = (f32[8,128]{1,0:T(8,128)S(1)}, f32[8,128]{1,0:T(8,128)}, u32[]{:S(2)}) copy-start(f32[8,128]{1,0:T(8,128)} %pressure.5) | copy-start | bytes 12292
  5.5 21.2 %copy-start.7 = (f32[8,128]{1,0:T(8,128)S(1)}, f32[8,128]{1,0:T(8,128)}, u32[]{:S(2)}) copy-start(f32[8,128]{1,0:T(8,128)} %mobility.5) | copy-start | bytes 12292
  5.5 28.5 %copy-start.16 = (s32[8,8]{1,0:T(8,128)S(1)}, s32[8,8]{1,0:T(8,128)}, u32[]{:S(2)}) copy-start(s32[8,8]{1,0:T(8,128)} %param.19) | copy-start | bytes 772
  5.5 28.5 %copy-start.13 = (s32[8]{0:T(128)S(1)}, s32[8]{0:T(128)}, u32[]{:S(2)}) copy-start(s32[8]{0:T(128)} %counts.5) | copy-start | bytes 100
  5.5 36.3 %all-to-all-start = ((f32[512,1,128]{2,1,0:T(1,128)}), f32[512,1,128]{2,1,0:T(1,128)S(1)}, u32[]{:S(2)}, u32[]{:S(2)}) async-start(f32[512,1,128]{2,1,0:T(1,128)} %bitcast.59), calls=%async_computation | async-start | bytes 524288 | tf_op jit(solution)/shard_map/all_to_all | solution.py:535
  26.7 10.1 %collective-permute-start.1 = (f32[8,8,128]{2,1,0:T(8,128)S(1)}, f32[8,8,128]{2,1,0:T(8,128)S(1)}, u32[]{:S(2)}, u32[]{:S(2)}) collective-permute-start(f32[8,8,128]{2,1,0:T(8,128)S(1)} %shard_map.177), channel_id=1, source_target_pairs={{0,16},{16,0},{32,48},{48,32},{64,80},{80,64},{96,112},{112,96},{1... | collective-permute-start | bytes 98312 | tf_op jit(solution)/shard_map/ppermute | solution.py:479
  30.1 9.1 %collective-permute-start = (f32[8,8,128]{2,1,0:T(8,128)S(1)}, f32[8,8,128]{2,1,0:T(8,128)S(1)}, u32[]{:S(2)}, u32[]{:S(2)}) collective-permute-start(f32[8,8,128]{2,1,0:T(8,128)S(1)} %shard_map.177), channel_id=1, source_target_pairs={{0,496},{16,32},{32,16},{48,64},{64,48},{80,96},{96,80},{112,128},... | collective-permute-start | bytes 98312 | tf_op jit(solution)/shard_map/ppermute | solution.py:480
  39.3 2.6 %copy-start = (f32[8,16,3,128]{3,1,2,0:T(8,128)S(1)}, f32[8,16,3,128]{3,1,2,0:T(8,128)}, u32[]{:S(2)}) copy-start(f32[8,16,3,128]{3,1,2,0:T(8,128)} %param.21) | copy-start | bytes 589828
  39.3 2.6 %copy-start.3 = (f32[256,16]{1,0:T(8,128)S(1)}, f32[256,16]{1,0:T(8,128)}, u32[]{:S(2)}) copy-start(f32[256,16]{1,0:T(8,128)} %get-tuple-element.40.lifts) | copy-start | bytes 49156
  39.3 2.6 %copy-start.5 = (f32[8,3,128]{2,0,1:T(8,128)S(1)}, f32[8,3,128]{2,0,1:T(8,128)}, u32[]{:S(2)}) copy-start(f32[8,3,128]{2,0,1:T(8,128)} %param.24) | copy-start | bytes 36868
  44.0 21.4 %all-to-all-start.1 = ((f32[32,16,128]{2,1,0:T(8,128)}), f32[32,16,128]{2,1,0:T(8,128)S(1)}, u32[]{:S(2)}, u32[]{:S(2)}) async-start(f32[32,16,128]{2,1,0:T(8,128)} %get-tuple-element.45), calls=%async_computation.1 | async-start | bytes 524288 | tf_op jit(solution)/shard_map/all_to_all | solution.py:586
  53.0 7.4 %collective-permute-start.3 = (f32[6,8,128]{2,1,0:T(8,128)S(1)}, f32[6,8,128]{2,1,0:T(8,128)S(1)}, u32[]{:S(2)}, u32[]{:S(2)}) collective-permute-start(f32[6,8,128]{2,1,0:T(8,128)S(1)} %get-tuple-element.70), channel_id=1, source_target_pairs={{0,16},{16,0},{32,48},{48,32},{64,80},{80,64},{96,112},{112,96},{1... | collective-permute-start | bytes 73736 | tf_op jit(solution)/shard_map/ppermute | solution.py:479
  56.4 9.0 %collective-permute-start.2 = (f32[6,8,128]{2,1,0:T(8,128)S(1)}, f32[6,8,128]{2,1,0:T(8,128)S(1)}, u32[]{:S(2)}, u32[]{:S(2)}) collective-permute-start(f32[6,8,128]{2,1,0:T(8,128)S(1)} %get-tuple-element.71), channel_id=1, source_target_pairs={{0,496},{16,32},{32,16},{48,64},{64,48},{80,96},{96,80},{112,128},... | collective-permute-start | bytes 73736 | tf_op jit(solution)/shard_map/ppermute | solution.py:480
  66.2 17.1 %all-to-all-start.2 = ((f32[16,8,128]{2,1,0:T(8,128)}), f32[16,8,128]{2,1,0:T(8,128)S(1)}, u32[]{:S(2)}, u32[]{:S(2)}) async-start(f32[16,8,128]{2,1,0:T(8,128)} %get-tuple-element.49), calls=%async_computation.2 | async-start | bytes 131072 | tf_op jit(solution)/shard_map/all_to_all | solution.py:593
  85.1 19.9 %all-to-all-start.3 = ((f32[32,8,128]{2,1,0:T(8,128)}), f32[32,8,128]{2,1,0:T(8,128)S(1)}, u32[]{:S(2)}, u32[]{:S(2)}) async-start(f32[32,8,128]{2,1,0:T(8,128)} %get-tuple-element.56), calls=%async_computation.3 | async-start | bytes 262144 | tf_op jit(solution)/shard_map/all_to_all | solution.py:610
  92.7 7.4 %collective-permute-start.5 = (f32[2,8,128]{2,1,0:T(8,128)S(1)}, f32[2,8,128]{2,1,0:T(8,128)S(1)}, u32[]{:S(2)}, u32[]{:S(2)}) collective-permute-start(f32[2,8,128]{2,1,0:T(8,128)S(1)} %get-tuple-element.74), channel_id=1, source_target_pairs={{0,16},{16,0},{32,48},{48,32},{64,80},{80,64},{96,112},{112,96},{1... | collective-permute-start | bytes 24584 | tf_op jit(solution)/shard_map/ppermute | solution.py:479
  96.1 8.9 %collective-permute-start.4 = (f32[2,8,128]{2,1,0:T(8,128)S(1)}, f32[2,8,128]{2,1,0:T(8,128)S(1)}, u32[]{:S(2)}, u32[]{:S(2)}) collective-permute-start(f32[2,8,128]{2,1,0:T(8,128)S(1)} %get-tuple-element.75), channel_id=1, source_target_pairs={{0,496},{16,32},{32,16},{48,64},{64,48},{80,96},{96,80},{112,128},... | collective-permute-start | bytes 24584 | tf_op jit(solution)/shard_map/ppermute | solution.py:480
  105.2 1.3 %collective-permute-start.7 = (f32[8,128]{1,0:T(8,128)S(1)}, f32[8,128]{1,0:T(8,128)S(1)}, u32[]{:S(2)}, u32[]{:S(2)}) collective-permute-start(f32[8,128]{1,0:T(8,128)S(1)} %get-tuple-element.62), channel_id=1, source_target_pairs={{0,15},{1,0},{2,1},{3,2},{4,3},{5,4},{6,5},{7,6},{8,7},{9,8},{10,9... | collective-permute-start | bytes 12296 | tf_op jit(solution)/shard_map/ppermute | solution.py:470
  105.2 4.3 %collective-permute-start.6 = (f32[8,128]{1,0:T(8,128)S(1)}, f32[8,128]{1,0:T(8,128)S(1)}, u32[]{:S(2)}, u32[]{:S(2)}) collective-permute-start(f32[8,128]{1,0:T(8,128)S(1)} %get-tuple-element.62), channel_id=1, source_target_pairs={{0,1},{1,2},{2,3},{3,4},{4,5},{5,6},{6,7},{7,8},{8,9},{9,10},{10,1... | collective-permute-start | bytes 12296 | tf_op jit(solution)/shard_map/ppermute | solution.py:470
  (5 other events, 12.8 us)

commit v6 on v5

--- a/solution.py
+++ b/solution.py
@@ -299,16 +299,17 @@
     copies_of(tile_out, sent)
 
 
-def last_kernel(received, low, high, loaded, pressure, window, tile_out):
-    j = lax.axis_index("gx")
-    peers = received.shape[0]
+def last_kernel(first, second, third, loaded, pressure, window, tile_out):
+    even = lax.rem(lax.axis_index("gx"), 2) == 0
     window[...] = pressure[...]
     window[2:26, :] += loaded[...]
     for i, size in ((0, 8), (1, 2)):
-        window[8 + 8 * i : 8 + 8 * i + size, :] += low[i, 0:size, :]
-        window[10 + 8 * i : 10 + 8 * i + size, :] += high[i, 0:size, :]
-    window[18:20, :] += received[lax.rem(j + 2, peers), 0:2, :]
-    window[8:10, :] += received[lax.rem(j - 2 + peers, peers), 0:2, :]
+        one, two = first[i, 0:size, :], second[i, 0:size, :]
+        window[8 + 8 * i : 8 + 8 * i + size, :] += jnp.where(even, two, one)
+        window[10 + 8 * i : 10 + 8 * i + size, :] += jnp.where(even, one, two)
+    relayed, last = second[1, 2:4, :], third[0:2, :]
+    window[8:10, :] += jnp.where(even, relayed, last)
+    window[18:20, :] += jnp.where(even, last, relayed)
     tile_out[...] = jnp.zeros(tile_out.shape, F32)
     tile_out[0:4, 0:32] = pick_edges(window[...])[0:4]
 
@@ -439,7 +440,7 @@
 
 def second_update_kernel(received, tile, window, mobility, h, near, *refs):
     refs, outs = refs[:10], refs[10:]
-    slip_out, loaded, window_out, side_out, down_out, up_out, sent, ahead, behind = outs
+    slip_out, loaded, window_out, side_out, down_out, up_out = outs
     g = lax.axis_index("gy")
     left = received[jnp.maximum(g - 1, 0)]
     right = received[jnp.minimum(g + 1, received.shape[0] - 1)]
@@ -448,11 +449,6 @@
     window_out[...] = flow(window[...], side, mobility[...], mobility_side)
     parts = incoming_of_row(received, tile, h)
     update(parts, window_out[2:26, :], near, refs, slip_out, loaded)
-    ahead[...] = jnp.zeros(ahead.shape, F32)
-    behind[...] = jnp.zeros(behind.shape, F32)
-    ahead[0:2, :] = loaded[0:2, :]
-    behind[0:2, :] = loaded[22:24, :]
-    send_sources(ahead, behind, sent)
     for out, at in ((down_out, 0), (up_out, 14)):
         out[0] = loaded[at : at + 8, :]
         out[1] = jnp.zeros((8, 128), F32)
@@ -479,6 +475,20 @@
     first = lax.ppermute(first, axis, [(i, i ^ 1) for i in range(n)])
     second = lax.ppermute(second, axis, [(i, (i + 2 * (i % 2) - 1) % n) for i in range(n)])
     return jnp.where(even, second, first), jnp.where(even, first, second)
+
+
+def relayed_along_gx(up, down):
+    n = lax.axis_size("gx")
+    even = lax.axis_index("gx") % 2 == 0
+    near_pairs = [(i, i ^ 1) for i in range(n)]
+    first = lax.ppermute(jnp.where(even, up, down), "gx", near_pairs)
+    own = jnp.where(even, down, up)
+    relay = jnp.where(even, first[0, 0:2], first[1, 0:2])
+    tail = jnp.concatenate([own[1, 0:2], relay, own[1, 4:8]], axis=0)
+    pairs = [(i, (i + 2 * (i % 2) - 1) % n) for i in range(n)]
+    second = lax.ppermute(jnp.stack([own[0], tail]), "gx", pairs)
+    third = lax.ppermute(jnp.where(even, second[1], second[0]), "gx", near_pairs)
+    return first, second, third
 
 
 def shards(
@@ -593,7 +603,7 @@
     received = lax.all_to_all(sent, "gy", 0, 0, tiled=True)
     near_slip, sent = lax.optimization_barrier((slip, sent))
     near = near_field(True, near_slip, low, high)
-    slip, loaded, window, mobility_side, down, up, sent = call(
+    slip, loaded, window, mobility_side, down, up = call(
         second_update_kernel,
         [
             ((3, 8, 128), F32),
@@ -602,17 +612,14 @@
             ((32, 128), F32),
             ((2, 8, 128), F32),
             ((2, 8, 128), F32),
-            ((nx, 8, 128), F32),
         ],
         [received, tile, window, mobility_window, h_mat, near, slip, *common],
-        scratch=[pltpu.VMEM((8, 128), F32), pltpu.VMEM((8, 128), F32)],
-    )
-    received = lax.all_to_all(sent, "gx", 0, 0, tiled=True)
-    low, high = with_neighbours(up, down, "gx")
+    )
+    first, second, third = relayed_along_gx(up, down)
     window, tile = call(
         last_kernel,
         [((32, 128), F32), ((8, 128), F32)],
-        [received, low, high, loaded, window],
+        [first, second, third, loaded, window],
     )
     left = shift(tile, "gy", 1)
     right = shift(tile, "gy", -1)

time: 111 us -> 111 us (level)
  waiting for transfers between devices: 20.8 us -> 28.7 us
  starting transfers between devices: 69.3 us -> 62.7 us
  Pallas kernels: 19 us -> 17.6 us
    ppermute x0 -> x3, waiting for transfers between devices: none -> 12 us  [the longest x1 4.88 us: relayed_along_gx(): second = lax.ppermute(jnp.stack([own[0], tail]), 'gx', pairs)]
    ppermute x0 -> x3, starting transfers between devices: none -> 7.8 us  [the longest x1 3.98 us: relayed_along_gx(): second = lax.ppermute(jnp.stack([own[0], tail]), 'gx', pairs)]
    all_to_all x2 -> x1, starting transfers between devices: 16.6 us -> 9.23 us  [shards(): received = lax.all_to_all(sent, 'gx', 0, 0, tiled=True)]
    ppermute x3 -> x2, waiting for transfers between devices: 12.3 us -> 7.74 us  [with_neighbours(): lax.ppermute(second, axis, [(i, (i + 2 * (i % 2) - 1) % n) for i in range...]
    ppermute x3 -> x2, starting transfers between devices: 11.9 us -> 7.88 us  [with_neighbours(): lax.ppermute(second, axis, [(i, (i + 2 * (i % 2) - 1) % n) for i in range...]
    ppermute x3 -> x2, starting transfers between devices: 10.1 us -> 6.77 us  [with_neighbours(): first = lax.ppermute(first, axis, [(i, i ^ 1) for i in range(n)])]
    pallas_call x11, Pallas kernels: 19 us -> 17.6 us  [call(): pl.pallas_call(kernel, out_shape=[jax.ShapeDtypeStruct(s, d) for s, d in...]
  transfers between devices with their start and end apart: 12 -> 12, of which waited for: 6 -> 8; matrix products, arithmetic and copies ran while one was open for 0% -> 0% of each run, Pallas kernels for 8% -> 7%
where the time goes in v6:
time: 111 us; the launch traced here: 110 us
  starting transfers between devices  62.7 us (56%)
  waiting for transfers between devices  28.7 us (26%)
  Pallas kernels  17.6 us (16%)
  between operations  1.15 us (1%)
    all_to_all x1, starting transfers between devices, shards(): lax.all_to_all(sent.reshape(nx * ny, 1, 128), ('gx', 'gy'), 0, 0, tiled=T...  20.9 us
    pallas_call x11, Pallas kernels, call(): pl.pallas_call(kernel, out_shape=[jax.ShapeDtypeStruct(s, d) for s, d in...  17.6 us
    all_to_all x1, starting transfers between devices, shards(): received = lax.all_to_all(sent, 'gy', 0, 0, tiled=True)  9.61 us
    all_to_all x1, starting transfers between devices, shards(): received = lax.all_to_all(sent, 'gx', 0, 0, tiled=True)  9.23 us
    ppermute x2, starting transfers between devices, with_neighbours(): lax.ppermute(second, axis, [(i, (i + 2 * (i % 2) - 1) % n) for i in range...  7.88 us
    ppermute x2, waiting for transfers between devices, with_neighbours(): lax.ppermute(second, axis, [(i, (i + 2 * (i % 2) - 1) % n) for i in range...  7.74 us
    ppermute x2, starting transfers between devices, with_neighbours(): first = lax.ppermute(first, axis, [(i, i ^ 1) for i in range(n)])  6.77 us
    all_to_all x1, waiting for transfers between devices, shards(): received = lax.all_to_all(sent, 'gy', 0, 0, tiled=True)  5.19 us
  transfers between devices with their start and end apart: 12, of which 8 were waited for; matrix products, arithmetic and copies ran while one was open for 0% of the time, Pallas kernels for 7%

profile of v6, /device:TPU:32, one launch (start us, length us, event | category | flops | bytes accessed | tf_op | source)
XLA Modules:
  0.0 110.3 jit_solution(17153666399138215936)
XLA Ops:
  0.7 4.8 %shard_map.176 = (f32[256,16]{1,0:T(8,128)}, f32[512,16]{1,0:T(8,128)}, f32[512,128]{1,0:T(8,128)}) custom-call(f32[256,1022]{1,0:T(8,128)} %bitcast.65, f32[256,1022]{1,0:T(8,128)} %bitcast.67, f32[256,1022]{1,0:T(8,128)} %bitcast.66, f32[256,1022]{1,0:T(8,128)} %bitcast.68, f32[3,8,128]{2,1,0:T(8,128)} %bitcast.53, f32[8,3,16,128]{3,2,1,0:T(8,128)} %bitcast.49), custom_call_target="tpu_custom_call" | custom-call | bytes 1048576 | tf_op jit(solution)/shard_map/pallas_call | solution.py:55
  5.5 20.9 %all-to-all-start = ((f32[512,1,128]{2,1,0:T(1,128)}), f32[512,1,128]{2,1,0:T(1,128)S(1)}, u32[]{:S(2)}, u32[]{:S(2)}) async-start(f32[512,1,128]{2,1,0:T(1,128)} %bitcast.69), calls=%async_computation | async-start | bytes 524288 | tf_op jit(solution)/shard_map/all_to_all | solution.py:545
  26.7 3.4 %collective-permute-start.1 = (f32[8,8,128]{2,1,0:T(8,128)S(1)}, f32[8,8,128]{2,1,0:T(8,128)S(1)}, u32[]{:S(2)}, u32[]{:S(2)}) collective-permute-start(f32[8,8,128]{2,1,0:T(8,128)S(1)} %shard_map.177), channel_id=1, source_target_pairs={{0,16},{16,0},{32,48},{48,32},{64,80},{80,64},{96,112},{112,96},{1... | collective-permute-start | bytes 98312 | tf_op jit(solution)/shard_map/ppermute | solution.py:475
  30.1 3.9 %collective-permute-start = (f32[8,8,128]{2,1,0:T(8,128)S(1)}, f32[8,8,128]{2,1,0:T(8,128)S(1)}, u32[]{:S(2)}, u32[]{:S(2)}) collective-permute-start(f32[8,8,128]{2,1,0:T(8,128)S(1)} %shard_map.177), channel_id=1, source_target_pairs={{0,496},{16,32},{32,16},{48,64},{64,48},{80,96},{96,80},{112,128},... | collective-permute-start | bytes 98312 | tf_op jit(solution)/shard_map/ppermute | solution.py:476
  34.1 2.5 %shard_map.179 = (f32[8,3,128,128]{3,2,1,0:T(8,128)S(1)}, f32[8,3,128,128]{3,2,1,0:T(8,128)S(1)}) custom-call(s32[8]{0:T(128)S(1)} %copy-done.13, s32[8,8]{1,0:T(8,128)S(1)} %add_select_fusion.slots, f32[3,8,128]{2,1,0:T(8,128)S(1)} %bitcast.59, f32[3,8,128]{2,1,0:T(8,128)S(1)} %bitcast.55), custom_call_target="tpu_custom_call" | custom-call | bytes 1048576 | tf_op jit(solution)/shard_map/pallas_call | solution.py:55
  36.5 2.7 %collective-permute-done = f32[8,8,128]{2,1,0:T(8,128)S(1)} collective-permute-done((f32[8,8,128]{2,1,0:T(8,128)S(1)}, f32[8,8,128]{2,1,0:T(8,128)S(1)}, u32[]{:S(2)}, u32[]{:S(2)}) %collective-permute-start) | collective-permute-done | bytes 32800 | tf_op jit(solution)/shard_map/ppermute | solution.py:476
  39.3 2.1 %shard_map.180.near = f32[3,8,128]{2,1,0:T(8,128)S(1)} custom-call(s32[8]{0:T(128)S(1)} %copy-done.13, s32[8,8]{1,0:T(8,128)S(1)} %add_select_fusion.slots, f32[8,3,128,128]{3,2,1,0:T(8,128)S(1)} %get-tuple-element.40.target.partial, f32[8,3,128,128]{3,2,1,0:T(8,128)S(1)} %get-tuple-element.41.partial, f32[3,8,128]{2,1,0:T(8,128)S(1)} %bitcast.60, ...), custom_call_target="tpu_custom_call" | custom-call | bytes 1048576 | tf_op jit(solution)/shard_map/pallas_call | solution.py:55
  41.5 2.1 %shard_map.181 = (f32[3,8,128]{2,1,0:T(8,128)S(1)}, f32[24,128]{1,0:T(8,128)S(1)}, f32[6,8,128]{2,1,0:T(8,128)S(1)}, f32[6,8,128]{2,1,0:T(8,128)S(1)}, f32[32,16,128]{2,1,0:T(8,128)}) custom-call(f32[512,128]{1,0:T(8,128)S(1)} %bitcast.52, f32[8,8,128]{2,1,0:T(8,128)S(1)} %get-tuple-element.65.refs_4_.low.first_low, ...), custom_call_target="tpu_custom_call" | custom-call | bytes 1048576 | tf_op jit(solution)/shard_map/pallas_call | solution.py:55
  43.6 9.2 %all-to-all-start.1 = ((f32[32,16,128]{2,1,0:T(8,128)}), f32[32,16,128]{2,1,0:T(8,128)S(1)}, u32[]{:S(2)}, u32[]{:S(2)}) async-start(f32[32,16,128]{2,1,0:T(8,128)} %get-tuple-element.44), calls=%async_computation.1 | async-start | bytes 524288 | tf_op jit(solution)/shard_map/all_to_all | solution.py:596
  52.8 3.4 %collective-permute-start.3 = (f32[6,8,128]{2,1,0:T(8,128)S(1)}, f32[6,8,128]{2,1,0:T(8,128)S(1)}, u32[]{:S(2)}, u32[]{:S(2)}) collective-permute-start(f32[6,8,128]{2,1,0:T(8,128)S(1)} %get-tuple-element.68), channel_id=1, source_target_pairs={{0,16},{16,0},{32,48},{48,32},{64,80},{80,64},{96,112},{112,96},{1... | collective-permute-start | bytes 73736 | tf_op jit(solution)/shard_map/ppermute | solution.py:475
  56.2 4.0 %collective-permute-start.2 = (f32[6,8,128]{2,1,0:T(8,128)S(1)}, f32[6,8,128]{2,1,0:T(8,128)S(1)}, u32[]{:S(2)}, u32[]{:S(2)}) collective-permute-start(f32[6,8,128]{2,1,0:T(8,128)S(1)} %get-tuple-element.69), channel_id=1, source_target_pairs={{0,496},{16,32},{32,16},{48,64},{64,48},{80,96},{96,80},{112,128},... | collective-permute-start | bytes 73736 | tf_op jit(solution)/shard_map/ppermute | solution.py:476
  60.2 5.1 %collective-permute-done.2 = f32[6,8,128]{2,1,0:T(8,128)S(1)} collective-permute-done((f32[6,8,128]{2,1,0:T(8,128)S(1)}, f32[6,8,128]{2,1,0:T(8,128)S(1)}, u32[]{:S(2)}, u32[]{:S(2)}) %collective-permute-start.2) | collective-permute-done | bytes 24608 | tf_op jit(solution)/shard_map/ppermute | solution.py:476
  66.1 9.6 %all-to-all-start.2 = ((f32[16,8,128]{2,1,0:T(8,128)}), f32[16,8,128]{2,1,0:T(8,128)S(1)}, u32[]{:S(2)}, u32[]{:S(2)}) async-start(f32[16,8,128]{2,1,0:T(8,128)} %get-tuple-element.48), calls=%async_computation.2 | async-start | bytes 131072 | tf_op jit(solution)/shard_map/all_to_all | solution.py:603
  75.7 2.7 %shard_map.183.near = f32[3,8,128]{2,1,0:T(8,128)S(1)} custom-call(s32[8]{0:T(128)S(1)} %copy-done.13, s32[8,8]{1,0:T(8,128)S(1)} %add_select_fusion.slots, f32[8,3,128,128]{3,2,1,0:T(8,128)S(1)} %get-tuple-element.40.target.partial, f32[8,3,128,128]{3,2,1,0:T(8,128)S(1)} %get-tuple-element.40.target.partial, f32[3,8,128]{2,1,0:T(8,128)S(1)} %bitcast.61, ...), custom_call_target="tpu_custom_call" | custom-call | flops 268435456 | bytes 1048576 | tf_op jit(solution)/shard_map/pallas_call | solution.py:55
  78.4 5.2 %all-to-all-done.2.received = f32[16,8,128]{2,1,0:T(8,128)S(1)} async-done(((f32[16,8,128]{2,1,0:T(8,128)}), f32[16,8,128]{2,1,0:T(8,128)S(1)}, u32[]{:S(2)}, u32[]{:S(2)}) %all-to-all-start.2) | async-done | bytes 65568 | tf_op jit(solution)/shard_map/all_to_all | solution.py:603
  83.6 1.4 %shard_map.184 = (f32[3,8,128]{2,1,0:T(8,128)}, f32[24,128]{1,0:T(8,128)S(1)}, f32[32,128]{1,0:T(8,128)S(1)}, f32[32,128]{1,0:T(8,128)S(1)}, f32[2,8,128]{2,1,0:T(8,128)S(1)}, /*index=5*/f32[2,8,128]{2,1,0:T(8,128)S(1)}) custom-call(f32[16,8,128]{2,1,0:T(8,128)S(1)} %all-to-all-done.2.received, f32[8,128]{1,0:T(8,128)S(1)} %get-tuple-element.49.tile, ...), custom_call_target="tpu_custom_call" | custom-call | bytes 1048576 | tf_op jit(solution)/shard_map/pallas_call | solution.py:55
  85.0 1.9 %collective-permute-start.4 = (f32[2,8,128]{2,1,0:T(8,128)S(1)}, f32[2,8,128]{2,1,0:T(8,128)S(1)}, u32[]{:S(2)}, u32[]{:S(2)}) collective-permute-start(f32[2,8,128]{2,1,0:T(8,128)S(1)} %get-tuple-element.71), channel_id=1, source_target_pairs={{0,16},{16,0},{32,48},{48,32},{64,80},{80,64},{96,112},{112,96},{1... | collective-permute-start | bytes 24584 | tf_op jit(solution)/shard_map/ppermute | solution.py:484
  87.0 3.6 %collective-permute-done.4.first = f32[2,8,128]{2,1,0:T(8,128)S(1)} collective-permute-done((f32[2,8,128]{2,1,0:T(8,128)S(1)}, f32[2,8,128]{2,1,0:T(8,128)S(1)}, u32[]{:S(2)}, u32[]{:S(2)}) %collective-permute-start.4) | collective-permute-done | bytes 8224 | tf_op jit(solution)/shard_map/ppermute | solution.py:484
  90.6 4.0 %collective-permute-start.5 = (f32[2,8,128]{2,1,0:T(8,128)S(1)}, f32[2,8,128]{2,1,0:T(8,128)S(1)}, u32[]{:S(2)}, u32[]{:S(2)}) collective-permute-start(f32[2,8,128]{2,1,0:T(8,128)S(1)} %pad_maximum_fusion), channel_id=1, source_target_pairs={{0,496},{16,32},{32,16},{48,64},{64,48},{80,96},{96,80},{112,128},... | collective-permute-start | bytes 24584 | tf_op jit(solution)/shard_map/ppermute | solution.py:489
  94.6 4.9 %collective-permute-done.5.second = f32[2,8,128]{2,1,0:T(8,128)S(1)} collective-permute-done((f32[2,8,128]{2,1,0:T(8,128)S(1)}, f32[2,8,128]{2,1,0:T(8,128)S(1)}, u32[]{:S(2)}, u32[]{:S(2)}) %collective-permute-start.5) | collective-permute-done | bytes 8224 | tf_op jit(solution)/shard_map/ppermute | solution.py:489
  99.5 1.9 %collective-permute-start.6 = (f32[8,128]{1,0:T(8,128)S(1)}, f32[8,128]{1,0:T(8,128)S(1)}, u32[]{:S(2)}, u32[]{:S(2)}) collective-permute-start(f32[8,128]{1,0:T(8,128)S(1)} %fusion.4), channel_id=1, source_target_pairs={{0,16},{16,0},{32,48},{48,32},{64,80},{80,64},{96,112},{112,96},{1... | collective-permute-start | bytes 12296 | tf_op jit(solution)/shard_map/ppermute | solution.py:490
  101.4 3.6 %collective-permute-done.6.third = f32[8,128]{1,0:T(8,128)S(1)} collective-permute-done((f32[8,128]{1,0:T(8,128)S(1)}, f32[8,128]{1,0:T(8,128)S(1)}, u32[]{:S(2)}, u32[]{:S(2)}) %collective-permute-start.6) | collective-permute-done | bytes 4128 | tf_op jit(solution)/shard_map/ppermute | solution.py:490
  106.5 2.9 %collective-permute-done.7.left = f32[8,128]{1,0:T(8,128)S(1)} collective-permute-done((f32[8,128]{1,0:T(8,128)S(1)}, f32[8,128]{1,0:T(8,128)S(1)}, u32[]{:S(2)}, u32[]{:S(2)}) %collective-permute-start.7) | collective-permute-done | bytes 4128 | tf_op jit(solution)/shard_map/ppermute | solution.py:466
  109.4 1.0 shard_map.186
  (63 shorter events, 2.7 us)
Async XLA Ops:
  0.6 25.8 %copy-start.14 = (s32[8,4,128]{2,1,0:T(4,128)S(1)}, s32[8,4,128]{2,1,0:T(4,128)}, u32[]{:S(2)}) copy-start(s32[8,4,128]{2,1,0:T(4,128)} %param.29) | copy-start | bytes 49156
  0.6 25.8 %copy-start.15 = (f32[8,4,128]{2,1,0:T(4,128)S(1)}, f32[8,4,128]{2,1,0:T(4,128)}, u32[]{:S(2)}) copy-start(f32[8,4,128]{2,1,0:T(4,128)} %param.30) | copy-start | bytes 49156
  5.4 21.2 %copy-start.1 = (f32[512,16]{1,0:T(8,128)S(1)}, f32[512,16]{1,0:T(8,128)}, u32[]{:S(2)}) copy-start(f32[512,16]{1,0:T(8,128)} %get-tuple-element.34.after.h) | copy-start | bytes 98308
  5.4 21.2 %copy-start.2 = (f32[8,3,128]{2,0,1:T(8,128)S(1)}, f32[8,3,128]{2,0,1:T(8,128)}, u32[]{:S(2)}) copy-start(f32[8,3,128]{2,0,1:T(8,128)} %param.17) | copy-start | bytes 36868
  5.5 21.2 %copy-start.4 = (f32[8,3,128]{2,0,1:T(8,128)S(1)}, f32[8,3,128]{2,0,1:T(8,128)}, u32[]{:S(2)}) copy-start(f32[8,3,128]{2,0,1:T(8,128)} %param.18) | copy-start | bytes 36868
  5.5 21.2 %copy-start.6 = (f32[8,128]{1,0:T(8,128)S(1)}, f32[8,128]{1,0:T(8,128)}, u32[]{:S(2)}) copy-start(f32[8,128]{1,0:T(8,128)} %pressure.5) | copy-start | bytes 12292
  5.5 21.2 %copy-start.7 = (f32[8,128]{1,0:T(8,128)S(1)}, f32[8,128]{1,0:T(8,128)}, u32[]{:S(2)}) copy-start(f32[8,128]{1,0:T(8,128)} %mobility.5) | copy-start | bytes 12292
  5.5 28.5 %copy-start.16 = (s32[8,8]{1,0:T(8,128)S(1)}, s32[8,8]{1,0:T(8,128)}, u32[]{:S(2)}) copy-start(s32[8,8]{1,0:T(8,128)} %param.19) | copy-start | bytes 772
  5.5 28.5 %copy-start.13 = (s32[8]{0:T(128)S(1)}, s32[8]{0:T(128)}, u32[]{:S(2)}) copy-start(s32[8]{0:T(128)} %counts.5) | copy-start | bytes 100
  5.5 35.9 %all-to-all-start = ((f32[512,1,128]{2,1,0:T(1,128)}), f32[512,1,128]{2,1,0:T(1,128)S(1)}, u32[]{:S(2)}, u32[]{:S(2)}) async-start(f32[512,1,128]{2,1,0:T(1,128)} %bitcast.69), calls=%async_computation | async-start | bytes 524288 | tf_op jit(solution)/shard_map/all_to_all | solution.py:545
  26.7 9.8 %collective-permute-start.1 = (f32[8,8,128]{2,1,0:T(8,128)S(1)}, f32[8,8,128]{2,1,0:T(8,128)S(1)}, u32[]{:S(2)}, u32[]{:S(2)}) collective-permute-start(f32[8,8,128]{2,1,0:T(8,128)S(1)} %shard_map.177), channel_id=1, source_target_pairs={{0,16},{16,0},{32,48},{48,32},{64,80},{80,64},{96,112},{112,96},{1... | collective-permute-start | bytes 98312 | tf_op jit(solution)/shard_map/ppermute | solution.py:475
  30.1 9.1 %collective-permute-start = (f32[8,8,128]{2,1,0:T(8,128)S(1)}, f32[8,8,128]{2,1,0:T(8,128)S(1)}, u32[]{:S(2)}, u32[]{:S(2)}) collective-permute-start(f32[8,8,128]{2,1,0:T(8,128)S(1)} %shard_map.177), channel_id=1, source_target_pairs={{0,496},{16,32},{32,16},{48,64},{64,48},{80,96},{96,80},{112,128},... | collective-permute-start | bytes 98312 | tf_op jit(solution)/shard_map/ppermute | solution.py:476
  39.2 2.2 %copy-start = (f32[8,16,3,128]{3,1,2,0:T(8,128)S(1)}, f32[8,16,3,128]{3,1,2,0:T(8,128)}, u32[]{:S(2)}) copy-start(f32[8,16,3,128]{3,1,2,0:T(8,128)} %param.21) | copy-start | bytes 589828
  39.3 2.2 %copy-start.3 = (f32[256,16]{1,0:T(8,128)S(1)}, f32[256,16]{1,0:T(8,128)}, u32[]{:S(2)}) copy-start(f32[256,16]{1,0:T(8,128)} %get-tuple-element.39.lifts) | copy-start | bytes 49156
  39.3 2.2 %copy-start.5 = (f32[8,3,128]{2,0,1:T(8,128)S(1)}, f32[8,3,128]{2,0,1:T(8,128)}, u32[]{:S(2)}) copy-start(f32[8,3,128]{2,0,1:T(8,128)} %param.24) | copy-start | bytes 36868
  43.6 21.7 %all-to-all-start.1 = ((f32[32,16,128]{2,1,0:T(8,128)}), f32[32,16,128]{2,1,0:T(8,128)S(1)}, u32[]{:S(2)}, u32[]{:S(2)}) async-start(f32[32,16,128]{2,1,0:T(8,128)} %get-tuple-element.44), calls=%async_computation.1 | async-start | bytes 524288 | tf_op jit(solution)/shard_map/all_to_all | solution.py:596
  52.8 7.4 %collective-permute-start.3 = (f32[6,8,128]{2,1,0:T(8,128)S(1)}, f32[6,8,128]{2,1,0:T(8,128)S(1)}, u32[]{:S(2)}, u32[]{:S(2)}) collective-permute-start(f32[6,8,128]{2,1,0:T(8,128)S(1)} %get-tuple-element.68), channel_id=1, source_target_pairs={{0,16},{16,0},{32,48},{48,32},{64,80},{80,64},{96,112},{112,96},{1... | collective-permute-start | bytes 73736 | tf_op jit(solution)/shard_map/ppermute | solution.py:475
  56.2 9.0 %collective-permute-start.2 = (f32[6,8,128]{2,1,0:T(8,128)S(1)}, f32[6,8,128]{2,1,0:T(8,128)S(1)}, u32[]{:S(2)}, u32[]{:S(2)}) collective-permute-start(f32[6,8,128]{2,1,0:T(8,128)S(1)} %get-tuple-element.69), channel_id=1, source_target_pairs={{0,496},{16,32},{32,16},{48,64},{64,48},{80,96},{96,80},{112,128},... | collective-permute-start | bytes 73736 | tf_op jit(solution)/shard_map/ppermute | solution.py:476
  66.1 17.5 %all-to-all-start.2 = ((f32[16,8,128]{2,1,0:T(8,128)}), f32[16,8,128]{2,1,0:T(8,128)S(1)}, u32[]{:S(2)}, u32[]{:S(2)}) async-start(f32[16,8,128]{2,1,0:T(8,128)} %get-tuple-element.48), calls=%async_computation.2 | async-start | bytes 131072 | tf_op jit(solution)/shard_map/all_to_all | solution.py:603
  85.0 5.5 %collective-permute-start.4 = (f32[2,8,128]{2,1,0:T(8,128)S(1)}, f32[2,8,128]{2,1,0:T(8,128)S(1)}, u32[]{:S(2)}, u32[]{:S(2)}) collective-permute-start(f32[2,8,128]{2,1,0:T(8,128)S(1)} %get-tuple-element.71), channel_id=1, source_target_pairs={{0,16},{16,0},{32,48},{48,32},{64,80},{80,64},{96,112},{112,96},{1... | collective-permute-start | bytes 24584 | tf_op jit(solution)/shard_map/ppermute | solution.py:484
  90.6 8.9 %collective-permute-start.5 = (f32[2,8,128]{2,1,0:T(8,128)S(1)}, f32[2,8,128]{2,1,0:T(8,128)S(1)}, u32[]{:S(2)}, u32[]{:S(2)}) collective-permute-start(f32[2,8,128]{2,1,0:T(8,128)S(1)} %pad_maximum_fusion), channel_id=1, source_target_pairs={{0,496},{16,32},{32,16},{48,64},{64,48},{80,96},{96,80},{112,128},... | collective-permute-start | bytes 24584 | tf_op jit(solution)/shard_map/ppermute | solution.py:489
  99.5 5.5 %collective-permute-start.6 = (f32[8,128]{1,0:T(8,128)S(1)}, f32[8,128]{1,0:T(8,128)S(1)}, u32[]{:S(2)}, u32[]{:S(2)}) collective-permute-start(f32[8,128]{1,0:T(8,128)S(1)} %fusion.4), channel_id=1, source_target_pairs={{0,16},{16,0},{32,48},{48,32},{64,80},{80,64},{96,112},{112,96},{1... | collective-permute-start | bytes 12296 | tf_op jit(solution)/shard_map/ppermute | solution.py:490
  105.1 1.3 %collective-permute-start.8 = (f32[8,128]{1,0:T(8,128)S(1)}, f32[8,128]{1,0:T(8,128)S(1)}, u32[]{:S(2)}, u32[]{:S(2)}) collective-permute-start(f32[8,128]{1,0:T(8,128)S(1)} %get-tuple-element.60), channel_id=1, source_target_pairs={{0,15},{1,0},{2,1},{3,2},{4,3},{5,4},{6,5},{7,6},{8,7},{9,8},{10,9... | collective-permute-start | bytes 12296 | tf_op jit(solution)/shard_map/ppermute | solution.py:466
  105.1 4.3 %collective-permute-start.7 = (f32[8,128]{1,0:T(8,128)S(1)}, f32[8,128]{1,0:T(8,128)S(1)}, u32[]{:S(2)}, u32[]{:S(2)}) collective-permute-start(f32[8,128]{1,0:T(8,128)S(1)} %get-tuple-element.60), channel_id=1, source_target_pairs={{0,1},{1,2},{2,3},{3,4},{4,5},{5,6},{6,7},{7,8},{8,9},{9,10},{10,1... | collective-permute-start | bytes 12296 | tf_op jit(solution)/shard_map/ppermute | solution.py:466
  (5 other events, 10.8 us)
